TPU v7x, 128 devices: a whole 4x4x4 slice. The times are simulated.
128 devices in a mesh: passage: 8 (over x, core), span: 16 (over z, y).
Axes of the slice: x: 4, y: 4, z: 4, core: 2. Of those that a mesh axis runs over, the one named last changes fastest.
Arguments:
- snapshots: bfloat16 [5, 256, 384, 1024], P(None, 'passage', 'span'), may hold values from -23 to 23
- sketch: bfloat16 [1024, 144], replicated, may hold values from -0.1875 to 0.1875
- blade_row: int32 [256], P('passage'), may hold values from 0 to 1
- row_speed: float32 [2], replicated, may hold values from 0.5 to 1.5
- stencil_reach: int32 [384], P('span'), may hold values from 1 to 2, as said below
Outputs:
- basis: float32 [15, 256, 384, 144], P(None, 'passage', 'span')
- coefficients: float32 [1024, 144], P(('passage', 'span'))
Inputs may be any that keep to these rules, and one draw needn't show every extreme that they name: `stencil_reach`: both offsets occur.
All inputs are finite; a program needn't handle non-finite values.
Results may differ from a plain program's by a relative error of at most 0.0037.
The roundings to bfloat16 on the way count: a program that leaves them out, or rounds other values in their place, can miss the bound.
Values may be sent and summed in bfloat16 or wider, within the bound.
No kernel may reach another device: no remote copies, remote signals or barrier semaphores. Data moves between devices by JAX's collectives and lax.ppermute only.
A program may use at most 192 MiB of HBM per device.

v0:
```python
import math

import jax
import jax.numpy as jnp
from jax import lax
from jax.sharding import PartitionSpec as P


def with_halo(x, sides, width, wrap):
    for axis, dim in sides:
        devices, length = (lax.axis_size(axis), x.shape[dim])
        up = [(i, (i + 1) % devices) for i in range(devices if wrap else devices - 1)]
        down = [(j, i) for i, j in up]
        last = lax.slice_in_dim(x, length - width, length, axis=dim)
        initial = lax.slice_in_dim(x, 0, width, axis=dim)
        before = lax.ppermute(last, axis, up)
        after = lax.ppermute(initial, axis, down)
        x = jnp.concatenate([before, x, after], axis=dim)
    return x


def frame_of(blade_row, row_speed, radial_pos, radial_total):
    radius = 0.6 + 0.4 * (radial_pos + 0.5) / radial_total
    labels = jnp.arange(row_speed.shape[0], dtype=jnp.int32)
    column_speed = jnp.sum(
        jnp.where(blade_row[:, None] == labels[None, :], row_speed[None, :], 0.0), axis=1
    )
    return column_speed[:, None] * radius[None, :]


def transform(snapshots, frame_shift):
    density = snapshots[0].astype(jnp.float32)
    axial_vel = snapshots[1].astype(jnp.float32)
    swirl_vel = snapshots[2].astype(jnp.float32) + frame_shift[:, :, None]
    radial_vel = snapshots[3].astype(jnp.float32)
    kinetic = axial_vel * axial_vel + swirl_vel * swirl_vel + radial_vel * radial_vel
    total_press = (
        snapshots[4].astype(jnp.float32) + 0.05 * (1.0 + 0.2 * jnp.tanh(density)) * kinetic
    )
    return jnp.stack([density, axial_vel, swirl_vel, radial_vel, total_press]).astype(jnp.bfloat16)


def inverse_t(gram_total):
    factor = jnp.linalg.cholesky(gram_total)
    unit_matrix = jnp.eye(gram_total.shape[0], dtype=gram_total.dtype)
    lower_inv = lax.linalg.triangular_solve(factor, unit_matrix, left_side=True, lower=True)
    return lower_inv.T


def turning_of(circum, stencil_reach):
    wide = circum.astype(jnp.float32)
    nearer = 0.5 * (wide[:, 3:-1] - wide[:, 1:-3])
    farther = 0.25 * (wide[:, 4:] - wide[:, :-4])
    return jnp.where((stencil_reach == 2)[None, None, :, None], farther, nearer)


def spanwise_of(radial_pad):
    wide = radial_pad.astype(jnp.float32)
    return 0.5 * (wide[:, :, 2:] - wide[:, :, :-2])


def gram_of(sketched):
    return lax.dot_general(
        sketched, sketched, (((0,), (0,)), ((), ())), preferred_element_type=jnp.float32
    )


def shards(snapshots, sketch, blade_row, row_speed, stencil_reach):
    variables, theta_cells, radial_cells, columns = snapshots.shape
    sketch_width = sketch.shape[1]
    passages = lax.axis_size("passage")
    layers = lax.axis_size("span")
    radial_total = radial_cells * layers
    row_total = 3 * variables * theta_cells * passages * radial_total
    radial_pos = (
        lax.axis_index("span") * radial_cells + jnp.arange(radial_cells, dtype=jnp.int32)
    ).astype(jnp.float32)
    frame_shift = frame_of(blade_row, row_speed, radial_pos, radial_total)
    fields = transform(snapshots, frame_shift)
    local_rows = variables * theta_cells * radial_cells
    field_rows = fields.reshape(local_rows, columns)
    field_sketch = jnp.dot(field_rows, sketch, preferred_element_type=jnp.float32)
    first_sketch = field_sketch.astype(jnp.bfloat16)
    full = lax.Precision.HIGHEST
    circum = with_halo(fields, (("passage", 1),), 2, True)
    radial_pad = with_halo(fields, (("span", 2),), 1, False)
    derived = jnp.concatenate([turning_of(circum, stencil_reach), spanwise_of(radial_pad)], axis=0)
    derived_rows = derived.reshape(2 * local_rows, columns)
    later_sketch = jnp.dot(derived_rows, sketch.astype(jnp.float32), precision=full).astype(
        jnp.bfloat16
    )
    later_wide = later_sketch.astype(jnp.float32)
    sketched = jnp.concatenate([first_sketch, later_sketch], axis=0)
    own_gram = gram_of(first_sketch) + gram_of(later_sketch)
    owned_rows = columns // (passages * layers)
    result = lax.dot_general(
        field_rows, first_sketch, (((0,), (0,)), ((), ())), preferred_element_type=jnp.float32
    )
    full_proj, gram_total = lax.psum(
        (
            result
            + lax.dot_general(derived_rows, later_wide, (((0,), (0,)), ((), ())), precision=full),
            own_gram,
        ),
        ("passage", "span"),
    )
    owned_part = lax.dynamic_slice_in_dim(
        full_proj, lax.axis_index(("passage", "span")) * owned_rows, owned_rows, 0
    )
    inv_factor = inverse_t(gram_total)
    row_scale = math.sqrt(row_total)
    product = jnp.dot(sketched.astype(jnp.float32), inv_factor, precision=full)
    basis = (product * row_scale).reshape(3 * variables, theta_cells, radial_cells, sketch_width)
    coefficients = jnp.dot(owned_part, inv_factor, precision=full) / row_scale
    return (basis, coefficients)


def solution(mesh):
    return jax.shard_map(
        shards,
        mesh=mesh,
        in_specs=(P(None, "passage", "span", None), P(), P("passage"), P(), P("span")),
        out_specs=(P(None, "passage", "span", None), P(("passage", "span"), None)),
        check_vma=False,
    )
```

profile of v0, /device:TPU:1, one launch (start us, length us, event | category | flops | bytes accessed | tf_op | source)
XLA Modules:
  0.0 381.9 jit_solution(10969197178039620780)
XLA Ops:
  7.3 1.7 convert_dynamic-update-slice_fusion.2
  9.0 1.8 convert_dynamic-update-slice_fusion.1
  11.9 2.3 fusion.16
  14.2 1.2 fusion.41
  15.4 2.6 collective-permute-start
  18.0 1.3 fusion.42
  19.3 1.3 collective-permute-start.3
  20.8 4.7 %collective-permute-start.2 = (bf16[5,32,1,1024]{3,1,2,0:T(8,128)(2,1)S(1)}, bf16[5,32,1,1024]{3,1,2,0:T(8,128)(2,1)}, u32[]{:S(2)}, u32[]{:S(2)}) collective-permute-start(bf16[5,32,1,1024]{3,1,2,0:T(8,128)(2,1)S(1)} %copy.36), channel_id=1, source_target_pairs={{0,1},{1,2},{2,3},{3,4},{4,5},{5,6},{6,7},{7,8},{8,9},{9,10},{10,1... | collective-permute-start | bytes 983048 | tf_op jit(solution)/shard_map/ppermute | solution.py:16
  25.5 2.7 convolution_convert_fusion
  28.2 2.2 fusion.45
  30.5 1.1 fusion.44
  32.2 1.5 copy.38
  33.6 7.4 %maximum_convert_fusion = f32[5,32,26,1024]{3,2,1,0:T(8,128)S(1)} fusion(bf16[5,32,1,1024]{3,2,1,0:T(2,128)(2,1)S(1)} %copy.39, bf16[5,32,24,1024]{3,2,1,0:T(8,128)(2,1)} %copy-done.1, bf16[5,32,1,1024]{3,2,1,0:T(2,128)(2,1)S(1)} %copy.38), kind=kLoop, calls=%fused_computation.13 | loop fusion | flops 25559040 | bytes 25559040 | tf_op jit(solution)/shard_map/convert_element_type | solution.py:58
  41.1 6.5 %fusion = f32[5,32,24,1024]{3,2,1,0:T(8,128)} fusion(f32[5,32,26,1024]{3,2,1,0:T(8,128)S(1)} %maximum_convert_fusion), kind=kLoop, calls=%fused_computation.2 | loop fusion | flops 7864320 | bytes 47185920 | tf_op jit(solution)/shard_map/mul | solution.py:59
  47.7 9.2 %maximum_convert_fusion.1 = f32[5,36,24,1024]{3,2,1,0:T(8,128)} fusion(bf16[5,2,24,1024]{3,2,1,0:T(8,128)(2,1)} %collective-permute-done.1, bf16[5,32,24,1024]{3,2,1,0:T(8,128)(2,1)S(1)} %bitcast.47, bf16[5,2,24,1024]{3,2,1,0:T(8,128)(2,1)} %collective-permute-done), kind=kLoop, calls=%fused_computation.14 | loop fusion | flops 13271040 | bytes 26542080 | tf_op jit(solution)/shard_map/convert_element_type | solution.py:51
  56.9 27.9 %fusion.2 = f32[5,32,24,1024]{3,2,1,0:T(8,128)} fusion(f32[5,36,24,1024]{3,2,1,0:T(8,128)} %maximum_convert_fusion.1, pred[24]{0:T(512)(128)(4,1)S(1)} %broadcast_compare_fusion), kind=kLoop, calls=%fused_computation.5 | loop fusion | flops 19660800 | bytes 78643224 | tf_op jit(solution)/shard_map/jit(_where)/select_n | solution.py:54
  84.8 17.7 %pad_maximum_fusion = f32[10,32,24,1024]{3,2,1,0:T(8,128)} fusion(f32[5,32,24,1024]{3,2,1,0:T(8,128)S(1)} %bitcast.43, f32[5,32,24,1024]{3,2,1,0:T(8,128)} %fusion.2), kind=kLoop, calls=%fused_computation | loop fusion | flops 7864320 | bytes 62914560 | tf_op jit(solution)/shard_map/concatenate | solution.py:87
  102.5 21.7 %fusion.43 = bf16[7680,144]{0,1:T(8,128)(2,1)S(1)} fusion(f32[7680,1024]{1,0:T(8,128)} %bitcast.40, bf16[1024,144]{0,1:T(8,128)(2,1)S(1)} %copy-done), kind=kOutput, calls=%fused_computation.84 | convolution fusion | flops 13589544960 | bytes 33964032 | tf_op jit(solution)/shard_map/dot_general | solution.py:89
  124.3 29.4 %fusion.20 = f32[1024,144]{1,0:T(8,128)} fusion(f32[1024,144]{1,0:T(8,128)S(1)} %fusion.45, f32[7680,1024]{1,0:T(8,128)} %bitcast.41, bf16[7680,144]{0,1:T(8,128)(2,1)S(1)} %fusion.43), kind=kOutput, calls=%fused_computation.35 | convolution fusion | flops 13589692416 | bytes 34848768 | tf_op jit(solution)/shard_map/dot_general | solution.py:102
  153.6 2.3 fusion.23
  156.0 152.4 %all-reduce.6.cloned.1.call-done = (f32[144,144]{0,1:T(8,128)}, f32[1024,144]{1,0:T(8,128)}) async-done(((f32[144,144]{0,1:T(8,128)}, f32[1024,144]{1,0:T(8,128)}), (f32[144,144]{0,1:T(8,128)}, f32[1024,144]{1,0:T(8,128)})) %all-reduce.6.cloned.1.call-update) | async-done | bytes 672784 | tf_op jit(solution)/shard_map/psum | solution.py:99
  308.4 1.0 copy.42
  309.4 0.9 fusion.26
  310.3 11.7 %cholesky.51 = f32[128,128]{1,0:T(8,128)S(1)} custom-call(f32[128,128]{1,0:T(8,128)S(1)} %cholesky.124), custom_call_target="Cholesky" | custom-call | tf_op jit(solution)/shard_map/jit(cholesky)/cholesky | solution.py:44
  322.1 0.6 compare_reduce_fusion.1
  322.7 9.8 %custom-call.14 = f32[1,128,128]{1,2,0:T(8,128)S(1)} custom-call(f32[1,128,128]{2,1,0:T(8,128)S(1)} %get-tuple-element.31), custom_call_target="InvertDiagBlocksLowerTriangular" | custom-call | tf_op jit(solution)/shard_map/jit(cholesky)/cholesky | solution.py:44
  332.9 1.5 cholesky.110
  334.4 0.6 compare_reduce_fusion
  336.5 19.9 %custom-call.15 = f32[2,128,128]{1,2,0:T(8,128)S(1)} custom-call(f32[2,128,128]{2,1,0:T(8,128)S(1)} %pad_maximum_fusion.2), custom_call_target="InvertDiagBlocksLowerTriangular" | custom-call | tf_op jit(solution)/shard_map/triangular_solve | solution.py:46
  357.2 7.0 %convolution_multiply_fusion = f32[11520,144]{0,1:T(8,128)} fusion(bf16[7680,144]{0,1:T(8,128)(2,1)S(1)} %fusion.43, bf16[3840,144]{0,1:T(8,128)(2,1)} %copy-done.3, f32[16,144]{0,1:T(8,128)S(1)} %fusion.33, f32[128,144]{0,1:T(8,128)S(1)} %fusion.27), kind=kOutput, calls=%fused_computation.8 | convolution fusion | flops 2874859776 | bytes 10036224 | tf_op jit(solution)/shard_map/dot_general | solution.py:112
  364.3 9.3 %copy.44 = f32[11520,144]{1,0:T(8,128)} copy(f32[11520,144]{0,1:T(8,128)} %convolution_multiply_fusion) | data formatting | bytes 13271040 | tf_op jit(solution)/shard_map/mul | solution.py:113
  373.6 1.5 convolution_multiply_fusion.1
  (60 shorter events, 3.3 us)
Async XLA Ops:
  7.2 18.3 %copy-start = (bf16[1024,144]{0,1:T(8,128)(2,1)S(1)}, bf16[1024,144]{0,1:T(8,128)(2,1)}, u32[]{:S(2)}) copy-start(bf16[1024,144]{0,1:T(8,128)(2,1)} %param.6) | copy-start | bytes 884740
  7.2 3.6 copy-start.4
  7.2 3.6 copy-start.5
  7.2 301.2 %all-reduce.6.cloned.1.call-start = ((), (), s32[]{:S(2)}) async-start(), calls=%async_computation | async-start | bytes 2392064 | tf_op jit(solution)/shard_map/psum | solution.py:99
  7.3 4.2 %copy-start.2 = (bf16[5,32,24,1024]{3,2,1,0:T(8,128)(2,1)S(1)}, bf16[5,32,24,1024]{3,2,1,0:T(8,128)(2,1)}, u32[]{:S(2)}) copy-start(bf16[5,32,24,1024]{3,2,1,0:T(8,128)(2,1)} %param.5) | copy-start | bytes 23592964
  14.2 14.0 %copy-start.1 = (bf16[5,32,24,1024]{3,2,1,0:T(8,128)(2,1)}, bf16[5,32,24,1024]{3,2,1,0:T(8,128)(2,1)S(1)}, u32[]{:S(2)}) copy-start(bf16[5,32,24,1024]{3,2,1,0:T(8,128)(2,1)S(1)} %fusion.16) | copy-start | bytes 23592964
  15.4 32.2 %collective-permute-start = (bf16[5,2,24,1024]{3,2,1,0:T(8,128)(2,1)}, bf16[5,2,24,1024]{3,2,1,0:T(8,128)(2,1)}, u32[]{:S(2)}, u32[]{:S(2)}) collective-permute-start(bf16[5,2,24,1024]{3,2,1,0:T(8,128)(2,1)} %get-tuple-element.26), channel_id=1, source_target_pairs={{0,16},{16,32},{32,48},{48,64},{64,80},{80,96},{96,112},{112,0},{1... | collective-permute-start | bytes 1474568 | tf_op jit(solution)/shard_map/ppermute | solution.py:16
  18.0 29.6 %collective-permute-start.1 = (bf16[5,2,24,1024]{3,2,1,0:T(8,128)(2,1)}, bf16[5,2,24,1024]{3,2,1,0:T(8,128)(2,1)}, u32[]{:S(2)}, u32[]{:S(2)}) collective-permute-start(bf16[5,2,24,1024]{3,2,1,0:T(8,128)(2,1)} %get-tuple-element.27), channel_id=1, source_target_pairs={{16,0},{32,16},{48,32},{64,48},{80,64},{96,80},{112,96},{0,112},{1... | collective-permute-start | bytes 1474568 | tf_op jit(solution)/shard_map/ppermute | solution.py:17
  19.3 12.3 %collective-permute-start.3 = (bf16[5,32,1,1024]{3,1,2,0:T(8,128)(2,1)S(1)}, bf16[5,32,1,1024]{3,1,2,0:T(8,128)(2,1)S(1)}, u32[]{:S(2)}, u32[]{:S(2)}) collective-permute-start(bf16[5,32,1,1024]{3,1,2,0:T(8,128)(2,1)S(1)} %copy.37), channel_id=1, source_target_pairs={{1,0},{2,1},{3,2},{4,3},{5,4},{6,5},{7,6},{8,7},{9,8},{10,9},{11,1... | collective-permute-start | bytes 983048 | tf_op jit(solution)/shard_map/ppermute | solution.py:17
  20.8 11.4 %collective-permute-start.2 = (bf16[5,32,1,1024]{3,1,2,0:T(8,128)(2,1)S(1)}, bf16[5,32,1,1024]{3,1,2,0:T(8,128)(2,1)}, u32[]{:S(2)}, u32[]{:S(2)}) collective-permute-start(bf16[5,32,1,1024]{3,1,2,0:T(8,128)(2,1)S(1)} %copy.36), channel_id=1, source_target_pairs={{0,1},{1,2},{2,3},{3,4},{4,5},{5,6},{6,7},{7,8},{8,9},{9,10},{10,1... | collective-permute-start | bytes 983048 | tf_op jit(solution)/shard_map/ppermute | solution.py:16
  28.2 3.4 copy-start.3
  28.2 2.2 copy-start.6
  33.6 14.0 %slice-start.4 = ((s8[7864320]{0:T(1024)(128)(4,1)}), s8[4194304]{0:T(1024)(128)(4,1)S(1)}, s32[]{:S(2)}) async-start(s8[7864320]{0:T(1024)(128)(4,1)} %bitcast.46), calls=%async_computation.5 | async-start | bytes 8388608
  41.1 6.5 %slice-start.5 = ((s8[7864320]{0:T(1024)(128)(4,1)}), s8[3670016]{0:T(1024)(128)(4,1)S(1)}, s32[]{:S(2)}) async-start(s8[7864320]{0:T(1024)(128)(4,1)} %bitcast.46), calls=%async_computation.6 | async-start | bytes 7340032
  47.6 37.1 %slice-start = ((s8[15728640]{0:T(1024)(128)(4,1)}), s8[4194304]{0:T(1024)(128)(4,1)S(1)}, s32[]{:S(2)}) async-start(s8[15728640]{0:T(1024)(128)(4,1)} %bitcast.42), calls=%async_computation.1 | async-start | bytes 8388608
  47.6 37.1 %slice-start.1 = ((s8[15728640]{0:T(1024)(128)(4,1)}), s8[4194304]{0:T(1024)(128)(4,1)S(1)}, s32[]{:S(2)}) async-start(s8[15728640]{0:T(1024)(128)(4,1)} %bitcast.42), calls=%async_computation.2 | async-start | bytes 8388608
  56.8 27.9 %slice-start.2 = ((s8[15728640]{0:T(1024)(128)(4,1)}), s8[4194304]{0:T(1024)(128)(4,1)S(1)}, s32[]{:S(2)}) async-start(s8[15728640]{0:T(1024)(128)(4,1)} %bitcast.42), calls=%async_computation.3 | async-start | bytes 8388608
  56.8 27.9 %slice-start.3 = ((s8[15728640]{0:T(1024)(128)(4,1)}), s8[3145728]{0:T(1024)(128)(4,1)S(1)}, s32[]{:S(2)}) async-start(s8[15728640]{0:T(1024)(128)(4,1)} %bitcast.42), calls=%async_computation.4 | async-start | bytes 6291456
Sparse Core Ops, SparseCore 0:
  156.1 152.2 all-reduce.5
where the time goes:
time: 383 us; the launch traced here: 382 us
  waiting for transfers between devices  152 us (40%)
  other arithmetic  121 us (32%)
  matrix products  69.1 us (18%)
  between operations  15.8 us (4%)
  local copies, waits for them, and re-layouts  15.5 us (4%)
  starting transfers between devices  8.67 us (2%)
    psum x1, waiting for transfers between devices, shards(): lax.psum((result + lax.dot_general(derived_rows, later_wide, (((0,), (0,)...  152 us
    dot_general x1, matrix products, shards(): lax.dot_general(derived_rows, later_wide, (((0,), (0,)), ((), ())), preci...  29.4 us
    select_n x1, other arithmetic, turning_of(): return jnp.where((stencil_reach == 2)[None, None, :, None], farther, nearer)  27.9 us
    another operation x7, other arithmetic, inverse_t(): factor = jnp.linalg.cholesky(gram_total)  24.3 us
    dot_general x1, matrix products, shards(): jnp.dot(derived_rows, sketch.astype(jnp.float32), precision=full)  21.7 us
    another operation x6, other arithmetic, inverse_t(): lax.linalg.triangular_solve(factor, unit_matrix, left_side=True, lower=True)  20.1 us
    concatenate x1, other arithmetic, shards(): jnp.concatenate([turning_of(circum, stencil_reach), spanwise_of(radial_pa...  17.7 us
    mul x1, local copies, waits for them, and re-layouts, shards(): product * row_scale  9.35 us
  transfers between devices with their start and end apart: 5, of which 1 were waited for; matrix products, arithmetic and copies ran while one was open for 6% of the time, Pallas kernels for 0%

commit v1 on v0

v1 whole, which is shorter than its diff:
```python
import functools
import math

import jax
import jax.numpy as jnp
from jax import lax
from jax.experimental import pallas as pl
from jax.experimental.pallas import tpu as pltpu
from jax.sharding import PartitionSpec as P

F32 = jnp.float32
BF16 = jnp.bfloat16
MIB = 1024 * 1024


def params(mib, **kw):
    return pltpu.CompilerParams(vmem_limit_bytes=mib * MIB, **kw)


def fields_kernel(radial_total, lines, blade_ref, speed_ref, snap_ref, sketch_ref,
                  field_ref, y_ref, first_t_ref, last_t_ref, first_r_ref, last_r_ref):
    step = pl.program_id(0)
    steps = pl.num_programs(0)
    variables, rows, columns = snap_ref.shape
    group = 2 * lines
    cells = rows // lines
    row_id = lax.broadcasted_iota(jnp.int32, (group, 128), 0)
    line_id = jnp.where(row_id >= lines, row_id - lines, row_id)
    radial_pos = (lax.axis_index("span") * lines + line_id).astype(F32)
    radius = 0.6 + 0.4 * (radial_pos + 0.5) / radial_total

    def column_speed(cell):
        label = blade_ref[step * cells + cell]
        total = jnp.float32(0.0)
        for row in range(speed_ref.shape[0]):
            total = jnp.where(label == row, speed_ref[row], total)
        return total

    for pair in range(rows // group):
        speed = jnp.where(row_id < lines, column_speed(2 * pair), column_speed(2 * pair + 1))
        shift = speed * radius
        at = pl.ds(pair * group, group)
        for tile in range(columns // 128):
            lanes = pl.ds(tile * 128, 128)
            density = snap_ref[0, at, lanes].astype(F32)
            axial = snap_ref[1, at, lanes].astype(F32)
            swirl = snap_ref[2, at, lanes].astype(F32) + shift
            radial = snap_ref[3, at, lanes].astype(F32)
            kinetic = axial * axial + swirl * swirl + radial * radial
            press = snap_ref[4, at, lanes].astype(F32) + 0.05 * (1.0 + 0.2 * jnp.tanh(density)) * kinetic
            field_ref[0, at, lanes] = snap_ref[0, at, lanes]
            field_ref[1, at, lanes] = snap_ref[1, at, lanes]
            field_ref[2, at, lanes] = swirl.astype(BF16)
            field_ref[3, at, lanes] = snap_ref[3, at, lanes]
            field_ref[4, at, lanes] = press.astype(BF16)
    for v in range(variables):
        y_ref[v] = lax.dot_general(field_ref[v], sketch_ref[...], (((1,), (1,)), ((), ())),
                                   preferred_element_type=F32)
        for cell in range(cells):
            for side in range(2):
                row = cell * lines + side
                first_r_ref[side, v, cell:cell + 1] = y_ref[v, row:row + 1]
                row = row + lines - 2
                last_r_ref[side, v, cell:cell + 1] = y_ref[v, row:row + 1]

    edge = first_t_ref.shape[1]

    @pl.when(step == 0)
    def _():
        first_t_ref[...] = y_ref[:, :edge, :]

    @pl.when(step == steps - 1)
    def _():
        last_t_ref[...] = y_ref[:, rows - edge:, :]


def fields_and_sketch(snapshots, sketch_t, blade_row, row_speed, lines, radial_total):
    variables, rows, columns = snapshots.shape
    width = sketch_t.shape[0]
    steps = 4
    block = rows // steps
    cells = rows // lines
    edge = 4 * lines
    return pl.pallas_call(
        functools.partial(fields_kernel, radial_total, lines),
        grid=(steps,),
        in_specs=[
            pl.BlockSpec(memory_space=pltpu.SMEM),
            pl.BlockSpec(memory_space=pltpu.SMEM),
            pl.BlockSpec((variables, block, columns), lambda i: (0, i, 0)),
            pl.BlockSpec((width, columns), lambda i: (0, 0)),
        ],
        out_specs=[
            pl.BlockSpec((variables, block, columns), lambda i: (0, i, 0)),
            pl.BlockSpec((variables, block, width), lambda i: (0, i, 0)),
            pl.BlockSpec((variables, edge, width), lambda i: (0, 0, 0)),
            pl.BlockSpec((variables, edge, width), lambda i: (0, 0, 0)),
            pl.BlockSpec((2, variables, cells // steps, width), lambda i: (0, 0, i, 0)),
            pl.BlockSpec((2, variables, cells // steps, width), lambda i: (0, 0, i, 0)),
        ],
        out_shape=[
            jax.ShapeDtypeStruct((variables, rows, columns), BF16),
            jax.ShapeDtypeStruct((variables, rows, width), F32),
            jax.ShapeDtypeStruct((variables, edge, width), F32),
            jax.ShapeDtypeStruct((variables, edge, width), F32),
            jax.ShapeDtypeStruct((2, variables, cells, width), F32),
            jax.ShapeDtypeStruct((2, variables, cells, width), F32),
        ],
        compiler_params=params(40),
        name="fields_sketch",
    )(blade_row, row_speed, snapshots, sketch_t)


def stencil_kernel(lines, reach_ref, y_ref, before_t_ref, after_t_ref, before_r_ref, after_r_ref,
                   z_ref, w_ref, gram_ref, acc_ref):
    v = pl.program_id(0)
    rows, width = y_ref.shape[1:]
    cells = rows // lines
    wide = reach_ref[...] == 2
    scale = jnp.where(wide, 0.25, 0.5)
    row_id = lax.broadcasted_iota(jnp.int32, (lines, width), 0)
    span = lax.axis_index("span")
    has_before = jnp.where(span > 0, 0.5, 0.0).astype(F32)
    has_after = jnp.where(span < lax.axis_size("span") - 1, 0.5, 0.0).astype(F32)

    def y_at(t):
        if t < 0:
            return before_t_ref[0, (t + 4) * lines:(t + 5) * lines, :]
        if t >= cells:
            return after_t_ref[0, (t - cells) * lines:(t - cells + 1) * lines, :]
        return y_ref[0, t * lines:(t + 1) * lines, :]

    def turn(get, t):
        return scale * jnp.where(wide, get(t + 2) - get(t - 2), get(t + 1) - get(t - 1))

    def rounded(x):
        return x.astype(BF16).astype(F32)

    z1 = {}

    def z1_at(t):
        if t not in z1:
            z1[t] = rounded(turn(y_at, t))
        return z1[t]

    def down(x, end):
        return jnp.where(row_id == 0, end, pltpu.roll(x, 1, 0))

    def up(x, end):
        return jnp.where(row_id == lines - 1, end, pltpu.roll(x, lines - 1, 0))

    for pair in range(cells // 2):
        kept = []
        for t in (2 * pair, 2 * pair + 1):
            y = y_at(t)
            w1 = -turn(z1_at, t)
            one = slice(t, t + 1)
            before2, before1 = before_r_ref[0, 0, one, :], before_r_ref[1, 0, one, :]
            after1, after2 = after_r_ref[0, 0, one, :], after_r_ref[1, 0, one, :]
            z2 = rounded(0.5 * (up(y, after1) - down(y, before1)))
            z2_before = rounded(has_before * (y[0:1] - before2))
            z2_after = rounded(has_after * (after2 - y[lines - 1:lines]))
            w2 = 0.5 * (down(z2, z2_before) - up(z2, z2_after))
            kept.append((y, z1_at(t), z2, rounded(y) + w1 + w2))
        at = pl.ds(2 * pair * lines, 2 * lines)
        a, b = kept
        for family in range(3):
            z_ref[family, 0, at, :] = jnp.concatenate([a[family], b[family]], axis=0).astype(BF16)
        w_ref[0, at, :] = jnp.concatenate([a[3], b[3]], axis=0).astype(BF16)

    gram = jnp.zeros((width, width), F32)
    for family in range(3):
        z = z_ref[family, 0]
        gram = gram + lax.dot_general(z, z, (((0,), (0,)), ((), ())), preferred_element_type=F32)

    @pl.when(v == 0)
    def _():
        acc_ref[...] = gram

    @pl.when(v > 0)
    def _():
        acc_ref[...] += gram

    @pl.when(v == pl.num_programs(0) - 1)
    def _():
        gram_ref[:width, :] = acc_ref[:, :128]
        gram_ref[width:, :] = jnp.zeros((gram_ref.shape[0] - width, 128), F32)
        gram_ref[width:, :width - 128] = acc_ref[128:, 128:]


def stencils(y, before_t, after_t, before_r, after_r, reach, lines):
    variables, rows, width = y.shape
    cells = rows // lines
    edge = 4 * lines
    packed = width + (width - 128)
    return pl.pallas_call(
        functools.partial(stencil_kernel, lines),
        grid=(variables,),
        in_specs=[
            pl.BlockSpec((lines, width), lambda v: (0, 0)),
            pl.BlockSpec((1, rows, width), lambda v: (v, 0, 0)),
            pl.BlockSpec((1, edge, width), lambda v: (v, 0, 0)),
            pl.BlockSpec((1, edge, width), lambda v: (v, 0, 0)),
            pl.BlockSpec((2, 1, cells, width), lambda v: (0, v, 0, 0)),
            pl.BlockSpec((2, 1, cells, width), lambda v: (0, v, 0, 0)),
        ],
        out_specs=[
            pl.BlockSpec((3, 1, rows, width), lambda v: (0, v, 0, 0)),
            pl.BlockSpec((1, rows, width), lambda v: (v, 0, 0)),
            pl.BlockSpec((packed, 128), lambda v: (0, 0)),
        ],
        out_shape=[
            jax.ShapeDtypeStruct((3, variables, rows, width), BF16),
            jax.ShapeDtypeStruct((variables, rows, width), BF16),
            jax.ShapeDtypeStruct((packed, 128), F32),
        ],
        scratch_shapes=[pltpu.VMEM((width, width), F32)],
        compiler_params=params(40),
        name="stencils",
    )(reach, y, before_t, after_t, before_r, after_r)


def project_kernel(field_ref, w_ref, out_ref, acc_ref):
    v = pl.program_id(0)
    part = lax.dot_general(w_ref[0], field_ref[0], (((0,), (0,)), ((), ())), preferred_element_type=F32)

    @pl.when(v == 0)
    def _():
        acc_ref[...] = part

    @pl.when(v > 0)
    def _():
        acc_ref[...] += part

    @pl.when(v == pl.num_programs(0) - 1)
    def _():
        out_ref[...] = acc_ref[...].T.astype(out_ref.dtype)


def project(fields, w):
    variables, rows, columns = fields.shape
    width = w.shape[2]
    return pl.pallas_call(
        project_kernel,
        grid=(variables,),
        in_specs=[
            pl.BlockSpec((1, rows, columns), lambda v: (v, 0, 0)),
            pl.BlockSpec((1, rows, width), lambda v: (v, 0, 0)),
        ],
        out_specs=pl.BlockSpec((columns, width), lambda v: (0, 0)),
        out_shape=jax.ShapeDtypeStruct((columns, width), F32),
        scratch_shapes=[pltpu.VMEM((width, columns), F32)],
        compiler_params=params(40),
        cost_estimate=pl.CostEstimate(flops=2 * variables * rows * columns * 256,
                                      bytes_accessed=variables * rows * columns * 2, transcendentals=0),
        name="project",
    )(fields, w)


def split3(x):
    high = x.astype(BF16)
    rest = x - high.astype(F32)
    mid = rest.astype(BF16)
    return high, mid, (rest - mid.astype(F32)).astype(BF16)


def inverse_factor_kernel(width, gram_ref, out_ref, a_ref):
    size = 16
    packed = gram_ref[...]
    a_ref[...] = jnp.zeros_like(a_ref)
    a_ref[:, :128] = packed[:width]
    a_ref[:128, 128:width] = packed[128:width].T
    a_ref[128:, 128:width] = packed[width:, :width - 128]
    a_ref[:, 256:] = jnp.where(
        lax.broadcasted_iota(jnp.int32, (width, 256), 0) == lax.broadcasted_iota(jnp.int32, (width, 256), 1),
        1.0, 0.0)
    row = lax.broadcasted_iota(jnp.int32, (size, 128), 0)
    lane = lax.broadcasted_iota(jnp.int32, (size, 256), 1)
    for start in range(0, width, size):
        panels = [a_ref[start:start + size, tile * 128:(tile + 1) * 128] for tile in range(4)]
        tile, offset = start // 128, start % 128
        cols = [jnp.broadcast_to(panels[tile][:, offset + j:offset + j + 1], (size, 128)) for j in range(size)]
        for j in range(size):
            pivot = jnp.broadcast_to(cols[j][j:j + 1, :], (size, 128))
            inv = lax.rsqrt(pivot)
            inv = inv * (1.5 - 0.5 * pivot * inv * inv)
            low = cols[j] * inv
            for i in range(j + 1, size):
                cols[i] = cols[i] - low * jnp.broadcast_to(low[i:i + 1, :], (size, 128))
            below = jnp.where(row > j, low, 0.0)
            for p in range(4):
                lead = jnp.broadcast_to(panels[p][j:j + 1, :], (size, 128)) * inv
                panels[p] = jnp.where(row == j, lead, panels[p] - below * lead)
        out_ref[start:start + size, :] = jnp.concatenate([panels[2], panels[3]], axis=1)[:, :width]
        if start + size < width:
            whole = jnp.concatenate(panels, axis=1)
            left = jnp.where(lane >= start + size, whole[:, :256], 0.0)
            lh, lm, ll = split3(left)
            rh, rm, rl = split3(whole)
            lhs = jnp.concatenate([lh, lh, lm, lm, lh, ll], axis=0)
            rhs = jnp.concatenate([rh, rm, rh, rm, rl, rh], axis=0)
            update = lax.dot_general(lhs, rhs, (((0,), (0,)), ((), ())), preferred_element_type=F32)
            a_ref[start + size:, :] -= update[start + size:width, :]


def inverse_factor(gram, width):
    return pl.pallas_call(
        functools.partial(inverse_factor_kernel, width),
        in_specs=[pl.BlockSpec(memory_space=pltpu.VMEM)],
        out_specs=pl.BlockSpec(memory_space=pltpu.VMEM),
        out_shape=jax.ShapeDtypeStruct((width, width), F32),
        scratch_shapes=[pltpu.VMEM((width, 512), F32)],
        compiler_params=params(32),
        name="inverse_factor",
    )(gram)


def basis_kernel(scale, z_ref, inv_ref, out_ref):
    inv = inv_ref[...] * scale
    high = inv.astype(BF16)
    low = (inv - high.astype(F32)).astype(BF16)
    nt = (((1,), (1,)), ((), ()))
    z = z_ref[...]
    out_ref[...] = (lax.dot_general(z, low, nt, preferred_element_type=F32)
                    + lax.dot_general(z, high, nt, preferred_element_type=F32))


def basis_of(z, inv, scale):
    rows, width = z.shape
    block = rows // 10
    return pl.pallas_call(
        functools.partial(basis_kernel, scale),
        grid=(rows // block,),
        in_specs=[
            pl.BlockSpec((block, width), lambda i: (i, 0)),
            pl.BlockSpec((width, width), lambda i: (0, 0)),
        ],
        out_specs=pl.BlockSpec((block, width), lambda i: (i, 0)),
        out_shape=jax.ShapeDtypeStruct((rows, width), F32),
        compiler_params=params(32),
        cost_estimate=pl.CostEstimate(flops=4 * rows * 256 * 256, bytes_accessed=rows * 256 * 6, transcendentals=0),
        name="basis",
    )(z, inv)


def coefficients_kernel(scale, parts_ref, inv_ref, out_ref):
    owned = jnp.sum(parts_ref[...].astype(F32), axis=0)
    out_ref[...] = lax.dot_general(owned, inv_ref[...], (((1,), (1,)), ((), ())),
                                   precision=lax.Precision.HIGHEST, preferred_element_type=F32) * scale


def coefficients_of(parts, inv, scale):
    _, rows, width = parts.shape
    return pl.pallas_call(
        functools.partial(coefficients_kernel, scale),
        in_specs=[pl.BlockSpec(memory_space=pltpu.VMEM)] * 2,
        out_specs=pl.BlockSpec(memory_space=pltpu.VMEM),
        out_shape=jax.ShapeDtypeStruct((rows, width), F32),
        compiler_params=params(32),
        name="coefficients",
    )(parts, inv)


def reduce_all(x):
    passages, layers = lax.axis_size("passage"), lax.axis_size("span")

    def exchange(x, axis, length, moves):
        parts = [lax.ppermute(x, axis, [(i, move(i)) for i in range(length)]) for move in moves]
        for part in parts:
            x = x + part
        return x

    x = exchange(x, "passage", passages, [lambda i: i ^ 1])
    x = exchange(x, "passage", passages, [lambda i, k=k: (i + 2 * k) % passages for k in (2, 1, 3)])
    x = exchange(x, "span", layers, [lambda i, k=k: i // 4 * 4 + (i + k) % 4 for k in (2, 1, 3)])
    x = exchange(x, "span", layers, [lambda i, k=k: (i + 4 * k) % layers for k in (2, 1, 3)])
    return x


def shards(snapshots, sketch, blade_row, row_speed, stencil_reach):
    variables, cells, lines, columns = snapshots.shape
    width = sketch.shape[1]
    passages, layers = lax.axis_size("passage"), lax.axis_size("span")
    row_total = 3 * variables * cells * passages * lines * layers
    fields, y, first_t, last_t, first_r, last_r = fields_and_sketch(
        snapshots.reshape(variables, cells * lines, columns), sketch.T, blade_row, row_speed,
        lines, lines * layers)
    ring_up = [(i, (i + 1) % passages) for i in range(passages)]
    ring_down = [(j, i) for i, j in ring_up]
    line_up = [(i, i + 1) for i in range(layers - 1)]
    line_down = [(j, i) for i, j in line_up]
    before_t = lax.ppermute(last_t, "passage", ring_up)
    after_t = lax.ppermute(first_t, "passage", ring_down)
    before_r = lax.ppermute(last_r, "span", line_up)
    after_r = lax.ppermute(first_r, "span", line_down)
    reach = jnp.broadcast_to(stencil_reach[:, None], (lines, width))
    z, w, gram = stencils(y, before_t, after_t, before_r, after_r, reach, lines)
    projected = project(fields, w)
    gram = reduce_all(gram)
    owned = columns // (passages * layers)
    parts = lax.all_to_all(projected.reshape(passages * layers, owned, width), ("passage", "span"), 0, 0, tiled=True)
    inv = inverse_factor(gram, width)
    basis = basis_of(z.reshape(-1, width), inv, math.sqrt(row_total))
    coefficients = coefficients_of(parts, inv, 1.0 / math.sqrt(row_total))
    return basis.reshape(3 * variables, cells, lines, width), coefficients


def solution(mesh):
    return jax.shard_map(
        shards,
        mesh=mesh,
        in_specs=(P(None, "passage", "span", None), P(), P("passage"), P(), P("span")),
        out_specs=(P(None, "passage", "span", None), P(("passage", "span"), None)),
        check_vma=False,
    )
```

time: 383 us -> 99.2 us (0.26)
  waiting for transfers between devices: 152 us -> 19.5 us
  other arithmetic: 121 us -> 0.08 us
  matrix products: 69.1 us -> 0 us
  Pallas kernels: 0 us -> 32 us
  starting transfers between devices: 8.67 us -> 34.8 us
  between operations: 15.8 us -> 0.78 us
  local copies, waits for them, and re-layouts: 15.5 us -> 11.6 us
    psum x1 -> x0, waiting for transfers between devices: 152 us -> none  [shards(): lax.psum((result + lax.dot_general(derived_rows, later_wide, (((0,), (0,)...]
    dot_general x8 -> x0, matrix products: 68 us -> none  [the longest x1 29.4 us: shards(): lax.dot_general(derived_rows, later_wide, (((0,), (0,)), ((), ())), preci...]
    another operation x14 -> x0, other arithmetic: 46.7 us -> none  [the longest x7 24.3 us: inverse_t(): factor = jnp.linalg.cholesky(gram_total)]
    pallas_call x0 -> x6, Pallas kernels: none -> 32 us  [the longest x1 7.94 us: basis_of(): pl.pallas_call(functools.partial(basis_kernel, scale), grid=(rows // bloc...]
    select_n x1 -> x0, other arithmetic: 27.9 us -> none  [turning_of(): return jnp.where((stencil_reach == 2)[None, None, :, None], farther, nearer)]
    concatenate x1 -> x0, other arithmetic: 17.7 us -> none  [shards(): jnp.concatenate([turning_of(circum, stencil_reach), spanwise_of(radial_pa...]
    convert_element_type x2 -> x0, other arithmetic: 16.6 us -> none  [the longest x1 9.19 us: turning_of(): wide = circum.astype(jnp.float32)]
    ppermute x4 -> x14, starting transfers between devices: 8.63 us -> 25.2 us  [the longest x10 18 us: exchange(): lax.ppermute(x, axis, [(i, move(i)) for i in range(length)])]
  transfers between devices with their start and end apart: 5 -> 15, of which waited for: 1 -> 8; matrix products, arithmetic and copies ran while one was open for 6% -> 0% of each run, Pallas kernels for 0% -> 17%
where the time goes in v1:
time: 99.2 us; the launch traced here: 98.8 us
  starting transfers between devices  34.8 us (35%)
  Pallas kernels  32 us (32%)
  waiting for transfers between devices  19.5 us (20%)
  local copies, waits for them, and re-layouts  11.6 us (12%)
    ppermute x10, starting transfers between devices, exchange(): lax.ppermute(x, axis, [(i, move(i)) for i in range(length)])  18 us
    unnamed x16, local copies, waits for them, and re-layouts  11.5 us
    all_to_all x1, starting transfers between devices, shards(): lax.all_to_all(projected.reshape(passages * layers, owned, width), ('pass...  9.66 us
    ppermute x10, waiting for transfers between devices, exchange(): lax.ppermute(x, axis, [(i, move(i)) for i in range(length)])  8.4 us
    pallas_call x1, Pallas kernels, basis_of(): pl.pallas_call(functools.partial(basis_kernel, scale), grid=(rows // bloc...  7.94 us
    pallas_call x1, Pallas kernels, stencils(): pl.pallas_call(functools.partial(stencil_kernel, lines), grid=(variables,...  7.53 us
    pallas_call x1, Pallas kernels, fields_and_sketch(): pl.pallas_call(functools.partial(fields_kernel, radial_total, lines), gri...  7.13 us
    pallas_call x1, Pallas kernels, inverse_factor(): pl.pallas_call(functools.partial(inverse_factor_kernel, width), in_specs=...  4.68 us
  transfers between devices with their start and end apart: 15, of which 8 were waited for; matrix products, arithmetic and copies ran while one was open for 0% of the time, Pallas kernels for 17%

profile of v1, /device:TPU:1, one launch (start us, length us, event | category | flops | bytes accessed | tf_op | source)
XLA Modules:
  0.0 98.8 jit_solution(17369989970967965371)
XLA Ops:
  0.7 1.0 copy-done.4
  1.6 0.7 copy-done.5
  2.3 0.7 copy-done.6
  2.9 7.1 %fields_sketch.1 = (bf16[5,768,1024]{2,1,0:T(8,128)(2,1)S(1)}, f32[5,768,144]{2,1,0:T(8,128)S(1)}, f32[5,96,144]{2,1,0:T(8,128)S(1)}, f32[5,96,144]{2,1,0:T(8,12...) custom-call(s32[32]{0:T(128)S(1)} %copy-done.5, f32[2]{0:T(128)S(1)} %copy-done.6, ...), custom_call_target="tpu_custom_call" | custom-call | tf_op jit(solution)/shard_map/fields_sketch/pallas_call | solution.py:84
  10.1 1.9 %copy-done.2 = f32[5,768,144]{2,1,0:T(8,128)} copy-done((f32[5,768,144]{2,1,0:T(8,128)}, f32[5,768,144]{2,1,0:T(8,128)S(1)}, u32[]{:S(2)}) %copy-start.2) | copy-done | bytes 2211864
  12.0 2.6 %collective-permute-start = (f32[5,96,144]{2,1,0:T(8,128)S(1)}, f32[5,96,144]{2,1,0:T(8,128)S(1)}, u32[]{:S(2)}, u32[]{:S(2)}) collective-permute-start(f32[5,96,144]{2,1,0:T(8,128)S(1)} %get-tuple-element.12), channel_id=1, source_target_pairs={{0,16},{16,32},{32,48},{48,64},{64,80},{80,96},{96,112},{112,0},{1... | collective-permute-start | bytes 829448 | tf_op jit(solution)/shard_map/ppermute | solution.py:392
  14.6 3.2 %collective-permute-start.2 = (f32[2,5,32,144]{3,2,1,0:T(8,128)S(1)}, f32[2,5,32,144]{3,2,1,0:T(8,128)S(1)}, u32[]{:S(2)}, u32[]{:S(2)}) collective-permute-start(f32[2,5,32,144]{3,2,1,0:T(8,128)S(1)} %get-tuple-element.14), channel_id=1, source_target_pairs={{0,1},{1,2},{2,3},{3,4},{4,5},{5,6},{6,7},{7,8},{8,9},{9,10},{10,1... | collective-permute-start | bytes 552968 | tf_op jit(solution)/shard_map/ppermute | solution.py:394
  17.8 1.3 %collective-permute-start.3 = (f32[2,5,32,144]{3,2,1,0:T(8,128)S(1)}, f32[2,5,32,144]{3,2,1,0:T(8,128)S(1)}, u32[]{:S(2)}, u32[]{:S(2)}) collective-permute-start(f32[2,5,32,144]{3,2,1,0:T(8,128)S(1)} %get-tuple-element.15), channel_id=1, source_target_pairs={{1,0},{2,1},{3,2},{4,3},{5,4},{6,5},{7,6},{8,7},{9,8},{10,9},{11,1... | collective-permute-start | bytes 552968 | tf_op jit(solution)/shard_map/ppermute | solution.py:395
  19.1 3.8 %collective-permute-done.2.before_r_ref = f32[2,5,32,144]{3,2,1,0:T(8,128)S(1)} collective-permute-done((f32[2,5,32,144]{3,2,1,0:T(8,128)S(1)}, f32[2,5,32,144]{3,2,1,0:T(8,128)S(1)}, u32[]{:S(2)}, u32[]{:S(2)}) %collective-permute-start.2) | collective-permute-done | bytes 184352 | tf_op jit(solution)/shard_map/ppermute | solution.py:394
  22.9 3.8 %collective-permute-done.3.after_r_ref = f32[2,5,32,144]{3,2,1,0:T(8,128)S(1)} collective-permute-done((f32[2,5,32,144]{3,2,1,0:T(8,128)S(1)}, f32[2,5,32,144]{3,2,1,0:T(8,128)S(1)}, u32[]{:S(2)}, u32[]{:S(2)}) %collective-permute-start.3) | collective-permute-done | bytes 184352 | tf_op jit(solution)/shard_map/ppermute | solution.py:395
  26.8 2.1 %copy-done.3 = f32[5,768,144]{2,1,0:T(8,128)S(1)} copy-done((f32[5,768,144]{2,1,0:T(8,128)S(1)}, f32[5,768,144]{2,1,0:T(8,128)}, u32[]{:S(2)}) %copy-start.3) | copy-done | bytes 2211864
  29.0 7.5 %stencils.1 = (bf16[3,5,768,144]{3,2,1,0:T(8,128)(2,1)S(1)}, bf16[5,768,144]{2,1,0:T(8,128)(2,1)S(1)}, f32[160,128]{1,0:T(8,128)S(1)}) custom-call(s32[24,144]{1,0:T(8,128)S(1)} %broadcast_in_dim.2.reach_ref, f32[5,768,144]{2,1,0:T(8,128)S(1)} %copy-done.3, f32[5,96,144]{2,1,0:T(8,128)S(1)} %collective-permute-done.before_t_ref, ...), custom_call_target="tpu_custom_call" | custom-call | tf_op jit(solution)/shard_map/stencils/pallas_call | solution.py:196
  36.5 2.6 %copy-done = bf16[3,5,768,144]{3,2,1,0:T(8,128)(2,1)} copy-done((bf16[3,5,768,144]{3,2,1,0:T(8,128)(2,1)}, bf16[3,5,768,144]{3,2,1,0:T(8,128)(2,1)S(1)}, u32[]{:S(2)}) %copy-start) | copy-done | bytes 3317784
  39.1 3.1 %collective-permute-start.4 = (f32[160,128]{1,0:T(8,128)S(1)}, f32[160,128]{1,0:T(8,128)S(1)}, u32[]{:S(2)}, u32[]{:S(2)}) collective-permute-start(f32[160,128]{1,0:T(8,128)S(1)} %get-tuple-element.17), channel_id=1, source_target_pairs={{0,16},{16,0},{32,48},{48,32},{64,80},{80,64},{96,112},{112,96},{1... | collective-permute-start | bytes 245768 | tf_op jit(solution)/shard_map/ppermute | solution.py:368
  42.1 0.9 collective-permute-done.4
  43.1 1.5 %collective-permute-start.7 = (f32[160,128]{1,0:T(8,128)S(1)}, f32[160,128]{1,0:T(8,128)S(1)}, u32[]{:S(2)}, u32[]{:S(2)}) collective-permute-start(f32[160,128]{1,0:T(8,128)S(1)} %add.30), channel_id=1, source_target_pairs={{0,96},{16,112},{32,0},{48,16},{64,32},{80,48},{96,64},{112,80},{1... | collective-permute-start | bytes 245768 | tf_op jit(solution)/shard_map/ppermute | solution.py:368
  44.6 2.4 %collective-permute-start.5 = (f32[160,128]{1,0:T(8,128)S(1)}, f32[160,128]{1,0:T(8,128)S(1)}, u32[]{:S(2)}, u32[]{:S(2)}) collective-permute-start(f32[160,128]{1,0:T(8,128)S(1)} %add.30), channel_id=1, source_target_pairs={{0,64},{16,80},{32,96},{48,112},{64,0},{80,16},{96,32},{112,48},{1... | collective-permute-start | bytes 245768 | tf_op jit(solution)/shard_map/ppermute | solution.py:368
  47.1 3.0 %collective-permute-done.6 = f32[160,128]{1,0:T(8,128)S(1)} collective-permute-done((f32[160,128]{1,0:T(8,128)S(1)}, f32[160,128]{1,0:T(8,128)S(1)}, u32[]{:S(2)}, u32[]{:S(2)}) %collective-permute-start.6) | collective-permute-done | bytes 81952 | tf_op jit(solution)/shard_map/ppermute | solution.py:368
  50.1 0.3 collective-permute-done.5
  50.4 4.9 %collective-permute-start.10 = (f32[160,128]{1,0:T(8,128)S(1)}, f32[160,128]{1,0:T(8,128)S(1)}, u32[]{:S(2)}, u32[]{:S(2)}) collective-permute-start(f32[160,128]{1,0:T(8,128)S(1)} %add_add_fusion.2), channel_id=1, source_target_pairs={{0,3},{1,0},{2,1},{3,2},{4,7},{5,4},{6,5},{7,6},{8,11},{9,8},{10,9... | collective-permute-start | bytes 245768 | tf_op jit(solution)/shard_map/ppermute | solution.py:368
  55.3 1.3 %collective-permute-start.8 = (f32[160,128]{1,0:T(8,128)S(1)}, f32[160,128]{1,0:T(8,128)S(1)}, u32[]{:S(2)}, u32[]{:S(2)}) collective-permute-start(f32[160,128]{1,0:T(8,128)S(1)} %add_add_fusion.2), channel_id=1, source_target_pairs={{0,2},{1,3},{2,0},{3,1},{4,6},{5,7},{6,4},{7,5},{8,10},{9,11},{10,... | collective-permute-start | bytes 245768 | tf_op jit(solution)/shard_map/ppermute | solution.py:368
  56.8 3.9 %collective-permute-done.9 = f32[160,128]{1,0:T(8,128)S(1)} collective-permute-done((f32[160,128]{1,0:T(8,128)S(1)}, f32[160,128]{1,0:T(8,128)S(1)}, u32[]{:S(2)}, u32[]{:S(2)}) %collective-permute-start.9) | collective-permute-done | bytes 81952 | tf_op jit(solution)/shard_map/ppermute | solution.py:368
  60.8 0.4 collective-permute-start.13
  61.1 1.4 %collective-permute-start.12 = (f32[160,128]{1,0:T(8,128)S(1)}, f32[160,128]{1,0:T(8,128)S(1)}, u32[]{:S(2)}, u32[]{:S(2)}) collective-permute-start(f32[160,128]{1,0:T(8,128)S(1)} %add_add_fusion.1), channel_id=1, source_target_pairs={{0,4},{1,5},{2,6},{3,7},{4,8},{5,9},{6,10},{7,11},{8,12},{9,13},{1... | collective-permute-start | bytes 245768 | tf_op jit(solution)/shard_map/ppermute | solution.py:368
  62.6 3.0 %collective-permute-start.11 = (f32[160,128]{1,0:T(8,128)S(1)}, f32[160,128]{1,0:T(8,128)S(1)}, u32[]{:S(2)}, u32[]{:S(2)}) collective-permute-start(f32[160,128]{1,0:T(8,128)S(1)} %add_add_fusion.1), channel_id=1, source_target_pairs={{0,8},{1,9},{2,10},{3,11},{4,12},{5,13},{6,14},{7,15},{8,0},{9,1},... | collective-permute-start | bytes 245768 | tf_op jit(solution)/shard_map/ppermute | solution.py:368
  65.6 3.8 %project.1 = f32[1024,144]{1,0:T(8,128)} custom-call(bf16[5,768,1024]{2,1,0:T(8,128)(2,1)S(1)} %get-tuple-element.18.field_ref, bf16[5,768,144]{2,1,0:T(8,128)(2,1)S(1)} %get-tuple-element.19.w_ref), custom_call_target="tpu_custom_call" | custom-call | flops 2013265920 | bytes 7864320 | tf_op jit(solution)/shard_map/project/pallas_call | solution.py:243
  69.4 9.7 %all-to-all-start = ((f32[128,8,144]{2,1,0:T(8,128)}), f32[128,8,144]{2,1,0:T(8,128)S(1)}, u32[]{:S(2)}, u32[]{:S(2)}) async-start(f32[128,8,144]{2,1,0:T(8,128)} %bitcast.4), calls=%async_computation | async-start | bytes 2097152 | tf_op jit(solution)/shard_map/all_to_all | solution.py:401
  79.1 4.7 %inverse_factor.1.inv_ref = f32[144,144]{1,0:T(8,128)S(1)} custom-call(f32[160,128]{1,0:T(8,128)S(1)} %add_add_fusion.gram_ref), custom_call_target="tpu_custom_call" | custom-call | tf_op jit(solution)/shard_map/inverse_factor/pallas_call | solution.py:307
  83.8 2.7 %copy-done.1 = bf16[3,5,768,144]{3,2,1,0:T(8,128)(2,1)S(1)} copy-done((bf16[3,5,768,144]{3,2,1,0:T(8,128)(2,1)S(1)}, bf16[3,5,768,144]{3,2,1,0:T(8,128)(2,1)}, u32[]{:S(2)}) %copy-start.1) | copy-done | bytes 3317784
  86.5 7.9 %basis.1 = f32[11520,144]{1,0:T(8,128)} custom-call(bf16[11520,144]{1,0:T(8,128)(2,1)S(1)} %bitcast.5, f32[144,144]{1,0:T(8,128)S(1)} %inverse_factor.1.inv_ref), custom_call_target="tpu_custom_call" | custom-call | flops 3019898880 | bytes 17694720 | tf_op jit(solution)/shard_map/basis/pallas_call | solution.py:331
  94.4 3.5 %all-to-all-done.parts_ref = f32[128,8,144]{2,1,0:T(8,128)S(1)} async-done(((f32[128,8,144]{2,1,0:T(8,128)}), f32[128,8,144]{2,1,0:T(8,128)S(1)}, u32[]{:S(2)}, u32[]{:S(2)}) %all-to-all-start) | async-done | bytes 589856 | tf_op jit(solution)/shard_map/all_to_all | solution.py:401
  97.9 1.0 coefficients.1
  (25 shorter events, 0.4 us)
Async XLA Ops:
  0.6 26.1 %copy-start.7 = (s32[24]{0:T(128)S(1)}, s32[24]{0:T(128)}, u32[]{:S(2)}) copy-start(s32[24]{0:T(128)} %param.9) | copy-start | bytes 292
  0.6 1.0 copy-start.4
  1.6 0.7 copy-start.5
  2.3 0.7 copy-start.6
  10.1 1.9 %copy-start.2 = (f32[5,768,144]{2,1,0:T(8,128)}, f32[5,768,144]{2,1,0:T(8,128)S(1)}, u32[]{:S(2)}) copy-start(f32[5,768,144]{2,1,0:T(8,128)S(1)} %get-tuple-element.11.y_ref) | copy-start | bytes 6635524
  12.0 14.8 %collective-permute-start = (f32[5,96,144]{2,1,0:T(8,128)S(1)}, f32[5,96,144]{2,1,0:T(8,128)S(1)}, u32[]{:S(2)}, u32[]{:S(2)}) collective-permute-start(f32[5,96,144]{2,1,0:T(8,128)S(1)} %get-tuple-element.12), channel_id=1, source_target_pairs={{0,16},{16,32},{32,48},{48,64},{64,80},{80,96},{96,112},{112,0},{1... | collective-permute-start | bytes 829448 | tf_op jit(solution)/shard_map/ppermute | solution.py:392
  14.6 12.2 %collective-permute-start.1 = (f32[5,96,144]{2,1,0:T(8,128)S(1)}, f32[5,96,144]{2,1,0:T(8,128)S(1)}, u32[]{:S(2)}, u32[]{:S(2)}) collective-permute-start(f32[5,96,144]{2,1,0:T(8,128)S(1)} %get-tuple-element.13), channel_id=1, source_target_pairs={{16,0},{32,16},{48,32},{64,48},{80,64},{96,80},{112,96},{0,112},{1... | collective-permute-start | bytes 829448 | tf_op jit(solution)/shard_map/ppermute | solution.py:393
  14.6 8.3 %collective-permute-start.2 = (f32[2,5,32,144]{3,2,1,0:T(8,128)S(1)}, f32[2,5,32,144]{3,2,1,0:T(8,128)S(1)}, u32[]{:S(2)}, u32[]{:S(2)}) collective-permute-start(f32[2,5,32,144]{3,2,1,0:T(8,128)S(1)} %get-tuple-element.14), channel_id=1, source_target_pairs={{0,1},{1,2},{2,3},{3,4},{4,5},{5,6},{6,7},{7,8},{8,9},{9,10},{10,1... | collective-permute-start | bytes 552968 | tf_op jit(solution)/shard_map/ppermute | solution.py:394
  17.8 9.0 %collective-permute-start.3 = (f32[2,5,32,144]{3,2,1,0:T(8,128)S(1)}, f32[2,5,32,144]{3,2,1,0:T(8,128)S(1)}, u32[]{:S(2)}, u32[]{:S(2)}) collective-permute-start(f32[2,5,32,144]{3,2,1,0:T(8,128)S(1)} %get-tuple-element.15), channel_id=1, source_target_pairs={{1,0},{2,1},{3,2},{4,3},{5,4},{6,5},{7,6},{8,7},{9,8},{10,9},{11,1... | collective-permute-start | bytes 552968 | tf_op jit(solution)/shard_map/ppermute | solution.py:395
  26.8 2.1 %copy-start.3 = (f32[5,768,144]{2,1,0:T(8,128)S(1)}, f32[5,768,144]{2,1,0:T(8,128)}, u32[]{:S(2)}) copy-start(f32[5,768,144]{2,1,0:T(8,128)} %copy-done.2) | copy-start | bytes 6635524
  36.5 2.6 %copy-start = (bf16[3,5,768,144]{3,2,1,0:T(8,128)(2,1)}, bf16[3,5,768,144]{3,2,1,0:T(8,128)(2,1)S(1)}, u32[]{:S(2)}) copy-start(bf16[3,5,768,144]{3,2,1,0:T(8,128)(2,1)S(1)} %get-tuple-element.16) | copy-start | bytes 9953284
  39.1 4.0 %collective-permute-start.4 = (f32[160,128]{1,0:T(8,128)S(1)}, f32[160,128]{1,0:T(8,128)S(1)}, u32[]{:S(2)}, u32[]{:S(2)}) collective-permute-start(f32[160,128]{1,0:T(8,128)S(1)} %get-tuple-element.17), channel_id=1, source_target_pairs={{0,16},{16,0},{32,48},{48,32},{64,80},{80,64},{96,112},{112,96},{1... | collective-permute-start | bytes 245768 | tf_op jit(solution)/shard_map/ppermute | solution.py:368
  43.1 4.0 %collective-permute-start.7 = (f32[160,128]{1,0:T(8,128)S(1)}, f32[160,128]{1,0:T(8,128)S(1)}, u32[]{:S(2)}, u32[]{:S(2)}) collective-permute-start(f32[160,128]{1,0:T(8,128)S(1)} %add.30), channel_id=1, source_target_pairs={{0,96},{16,112},{32,0},{48,16},{64,32},{80,48},{96,64},{112,80},{1... | collective-permute-start | bytes 245768 | tf_op jit(solution)/shard_map/ppermute | solution.py:368
  44.6 5.5 %collective-permute-start.6 = (f32[160,128]{1,0:T(8,128)S(1)}, f32[160,128]{1,0:T(8,128)S(1)}, u32[]{:S(2)}, u32[]{:S(2)}) collective-permute-start(f32[160,128]{1,0:T(8,128)S(1)} %add.30), channel_id=1, source_target_pairs={{0,32},{16,48},{32,64},{48,80},{64,96},{80,112},{96,0},{112,16},{1... | collective-permute-start | bytes 245768 | tf_op jit(solution)/shard_map/ppermute | solution.py:368
  44.6 5.8 %collective-permute-start.5 = (f32[160,128]{1,0:T(8,128)S(1)}, f32[160,128]{1,0:T(8,128)S(1)}, u32[]{:S(2)}, u32[]{:S(2)}) collective-permute-start(f32[160,128]{1,0:T(8,128)S(1)} %add.30), channel_id=1, source_target_pairs={{0,64},{16,80},{32,96},{48,112},{64,0},{80,16},{96,32},{112,48},{1... | collective-permute-start | bytes 245768 | tf_op jit(solution)/shard_map/ppermute | solution.py:368
  50.4 6.4 %collective-permute-start.10 = (f32[160,128]{1,0:T(8,128)S(1)}, f32[160,128]{1,0:T(8,128)S(1)}, u32[]{:S(2)}, u32[]{:S(2)}) collective-permute-start(f32[160,128]{1,0:T(8,128)S(1)} %add_add_fusion.2), channel_id=1, source_target_pairs={{0,3},{1,0},{2,1},{3,2},{4,7},{5,4},{6,5},{7,6},{8,11},{9,8},{10,9... | collective-permute-start | bytes 245768 | tf_op jit(solution)/shard_map/ppermute | solution.py:368
  55.3 5.4 %collective-permute-start.9 = (f32[160,128]{1,0:T(8,128)S(1)}, f32[160,128]{1,0:T(8,128)S(1)}, u32[]{:S(2)}, u32[]{:S(2)}) collective-permute-start(f32[160,128]{1,0:T(8,128)S(1)} %add_add_fusion.2), channel_id=1, source_target_pairs={{0,1},{1,2},{2,3},{3,0},{4,5},{5,6},{6,7},{7,4},{8,9},{9,10},{10,1... | collective-permute-start | bytes 245768 | tf_op jit(solution)/shard_map/ppermute | solution.py:368
  55.3 5.4 %collective-permute-start.8 = (f32[160,128]{1,0:T(8,128)S(1)}, f32[160,128]{1,0:T(8,128)S(1)}, u32[]{:S(2)}, u32[]{:S(2)}) collective-permute-start(f32[160,128]{1,0:T(8,128)S(1)} %add_add_fusion.2), channel_id=1, source_target_pairs={{0,2},{1,3},{2,0},{3,1},{4,6},{5,7},{6,4},{7,5},{8,10},{9,11},{10,... | collective-permute-start | bytes 245768 | tf_op jit(solution)/shard_map/ppermute | solution.py:368
  60.8 18.3 %collective-permute-start.13 = (f32[160,128]{1,0:T(8,128)S(1)}, f32[160,128]{1,0:T(8,128)S(1)}, u32[]{:S(2)}, u32[]{:S(2)}) collective-permute-start(f32[160,128]{1,0:T(8,128)S(1)} %add_add_fusion.1), channel_id=1, source_target_pairs={{0,12},{1,13},{2,14},{3,15},{4,0},{5,1},{6,2},{7,3},{8,4},{9,5},{1... | collective-permute-start | bytes 245768 | tf_op jit(solution)/shard_map/ppermute | solution.py:368
  61.1 17.9 %collective-permute-start.12 = (f32[160,128]{1,0:T(8,128)S(1)}, f32[160,128]{1,0:T(8,128)S(1)}, u32[]{:S(2)}, u32[]{:S(2)}) collective-permute-start(f32[160,128]{1,0:T(8,128)S(1)} %add_add_fusion.1), channel_id=1, source_target_pairs={{0,4},{1,5},{2,6},{3,7},{4,8},{5,9},{6,10},{7,11},{8,12},{9,13},{1... | collective-permute-start | bytes 245768 | tf_op jit(solution)/shard_map/ppermute | solution.py:368
  62.6 16.5 %collective-permute-start.11 = (f32[160,128]{1,0:T(8,128)S(1)}, f32[160,128]{1,0:T(8,128)S(1)}, u32[]{:S(2)}, u32[]{:S(2)}) collective-permute-start(f32[160,128]{1,0:T(8,128)S(1)} %add_add_fusion.1), channel_id=1, source_target_pairs={{0,8},{1,9},{2,10},{3,11},{4,12},{5,13},{6,14},{7,15},{8,0},{9,1},... | collective-permute-start | bytes 245768 | tf_op jit(solution)/shard_map/ppermute | solution.py:368
  69.4 28.5 %all-to-all-start = ((f32[128,8,144]{2,1,0:T(8,128)}), f32[128,8,144]{2,1,0:T(8,128)S(1)}, u32[]{:S(2)}, u32[]{:S(2)}) async-start(f32[128,8,144]{2,1,0:T(8,128)} %bitcast.4), calls=%async_computation | async-start | bytes 2097152 | tf_op jit(solution)/shard_map/all_to_all | solution.py:401
  83.8 2.7 %copy-start.1 = (bf16[3,5,768,144]{3,2,1,0:T(8,128)(2,1)S(1)}, bf16[3,5,768,144]{3,2,1,0:T(8,128)(2,1)}, u32[]{:S(2)}) copy-start(bf16[3,5,768,144]{3,2,1,0:T(8,128)(2,1)} %copy-done) | copy-start | bytes 9953284

commit v2 on v1

v2 whole, which is shorter than its diff:
```python
import functools
import math

import jax
import jax.numpy as jnp
from jax import lax
from jax.experimental import pallas as pl
from jax.experimental.pallas import tpu as pltpu
from jax.sharding import PartitionSpec as P

F32 = jnp.float32
BF16 = jnp.bfloat16
MIB = 1024 * 1024
K1_MIB = 24
K1_CHUNKS = 8
K4_BLOCKS = 10
K2_MIB = 24
K3_MIB = 24
K4_MIB = 24


def in_hbm(x):
    return pltpu.with_memory_space_constraint(x, pltpu.HBM)


def params(mib, **kw):
    return pltpu.CompilerParams(vmem_limit_bytes=mib * MIB, **kw)


def packed_rows(rows, groups):
    return rows + rows // groups


def pack(dst_ref, v, value, groups):
    rows, width = value.shape
    part = rows // groups
    rest = value[:, 128:]
    tail = [rest[g * part:(g + 1) * part] for g in range(groups)]
    spare = 128 - groups * (width - 128)
    if spare:
        tail.append(jnp.zeros((part, spare), value.dtype))
    dst_ref[v, :rows] = value[:, :128].astype(BF16)
    dst_ref[v, rows:] = jnp.concatenate(tail, axis=1).astype(BF16)


def unpack(dst_ref, src_ref, v, groups):
    rows, width = dst_ref.shape
    part = rows // groups
    extra = width - 128
    dst_ref[:, :128] = src_ref[v, :rows].astype(F32)
    rest = src_ref[v, rows:].astype(F32)
    for g in range(groups):
        dst_ref[g * part:(g + 1) * part, 128:] = rest[:, g * extra:(g + 1) * extra]


T_GROUPS = 6
R_GROUPS = 4
VMEM_SPEC = pl.BlockSpec(memory_space=pltpu.VMEM)
HBM_SPEC = pl.BlockSpec(memory_space=pltpu.HBM)


def fields_kernel(radial_total, lines, blade_hbm, speed_hbm, sketch_hbm, snap_hbm,
                  field_ref, y_ref, first_t_ref, last_t_ref, first_r_ref, last_r_ref,
                  blade_ref, speed_ref, sketch_ref, turned_ref, low_r_ref, high_r_ref, small_sems, sems):
    variables, rows, columns = field_ref.shape
    chunks = sems.shape[0]
    part = rows // chunks
    group = 2 * lines
    cells = part // lines
    spare = rows // lines
    small = [pltpu.make_async_copy(blade_hbm, blade_ref, small_sems.at[0]),
             pltpu.make_async_copy(speed_hbm, speed_ref, small_sems.at[1]),
             pltpu.make_async_copy(sketch_hbm, sketch_ref, small_sems.at[2])]
    for copy in small:
        copy.start()

    def copy_of(c):
        at = pl.ds(pl.multiple_of(c * part, part), part)
        return pltpu.make_async_copy(snap_hbm.at[:, at], field_ref.at[:, at], sems.at[c])

    for c in range(chunks):
        copy_of(c).start()
    row_id = lax.broadcasted_iota(jnp.int32, (group, 128), 0)
    line_id = jnp.where(row_id >= lines, row_id - lines, row_id)
    radial_pos = (lax.axis_index("span") * lines + line_id).astype(F32)
    radius = 0.6 + 0.4 * (radial_pos + 0.5) / radial_total
    for copy in small:
        copy.wait()
    turned_ref[...] = sketch_ref[...].T

    def column_speed(cell):
        label = blade_ref[cell]
        total = jnp.float32(0.0)
        for row in range(speed_ref.shape[0]):
            total = jnp.where(label == row, speed_ref[row], total)
        return total

    def one_chunk(c, carry):
        copy_of(c).wait()
        base = pl.multiple_of(c * part, part)
        def one_pair(pair, carry):
            cell = c * cells + 2 * pair
            speed = jnp.where(row_id < lines, column_speed(cell), column_speed(cell + 1))
            shift = speed * radius
            at = pl.ds(pl.multiple_of(base + pair * group, group), group)
            for tile in range(columns // 128):
                lanes = pl.ds(tile * 128, 128)
                density = field_ref[0, at, lanes].astype(F32)
                axial = field_ref[1, at, lanes].astype(F32)
                swirl = field_ref[2, at, lanes].astype(F32) + shift
                radial = field_ref[3, at, lanes].astype(F32)
                kinetic = axial * axial + swirl * swirl + radial * radial
                press = (field_ref[4, at, lanes].astype(F32)
                         + 0.05 * (1.0 + 0.2 * jnp.tanh(density)) * kinetic)
                field_ref[2, at, lanes] = swirl.astype(BF16)
                field_ref[4, at, lanes] = press.astype(BF16)
            return carry

        lax.fori_loop(0, part // group, one_pair, 0)
        block = pl.ds(base, part)
        y = jnp.dot(field_ref[:, block].reshape(variables * part, columns), turned_ref[...],
                    preferred_element_type=F32)
        for v in range(variables):
            y_ref[v, block] = y[v * part:(v + 1) * part]
            for cell in range(cells):
                for side in range(2):
                    to = pl.ds(side * spare + c * cells + cell, 1)
                    row = v * part + cell * lines + side
                    low_r_ref[v, to] = y[row:row + 1]
                    row = row + lines - 2
                    high_r_ref[v, to] = y[row:row + 1]
        return carry

    lax.fori_loop(0, chunks, one_chunk, 0)
    for v in range(variables):
        pack(first_t_ref, v, y_ref[v, :4 * lines], T_GROUPS)
        pack(last_t_ref, v, y_ref[v, rows - 4 * lines:], T_GROUPS)
        pack(first_r_ref, v, low_r_ref[v], R_GROUPS)
        pack(last_r_ref, v, high_r_ref[v], R_GROUPS)


def fields_and_sketch(snapshots, sketch_t, blade_row, row_speed, lines, radial_total):
    variables, rows, columns = snapshots.shape
    width = sketch_t.shape[0]
    chunks = K1_CHUNKS
    cells = rows // lines
    edge_t = jax.ShapeDtypeStruct((variables, packed_rows(4 * lines, T_GROUPS), 128), BF16)
    edge_r = jax.ShapeDtypeStruct((variables, packed_rows(2 * cells, R_GROUPS), 128), BF16)
    return pl.pallas_call(
        functools.partial(fields_kernel, radial_total, lines),
        in_specs=[HBM_SPEC] * 4,
        out_specs=[VMEM_SPEC] * 6,
        out_shape=[
            jax.ShapeDtypeStruct((variables, rows, columns), BF16),
            jax.ShapeDtypeStruct((variables, rows, width), F32),
            edge_t, edge_t, edge_r, edge_r,
        ],
        scratch_shapes=[
            pltpu.SMEM(blade_row.shape, blade_row.dtype),
            pltpu.SMEM(row_speed.shape, row_speed.dtype),
            pltpu.VMEM(sketch_t.shape, sketch_t.dtype),
            pltpu.VMEM(sketch_t.shape[::-1], sketch_t.dtype),
            pltpu.VMEM((variables, 2 * cells, width), F32),
            pltpu.VMEM((variables, 2 * cells, width), F32),
            pltpu.SemaphoreType.DMA((3,)),
            pltpu.SemaphoreType.DMA((chunks,)),
        ],
        compiler_params=params(K1_MIB),
        name="fields_sketch",
    )(in_hbm(blade_row), in_hbm(row_speed), in_hbm(sketch_t), in_hbm(snapshots))


def stencil_kernel(lines, reach_ref, y_ref, before_t_in, after_t_in, before_r_in, after_r_in,
                   z_out, w_ref, gram_ref, acc_ref, before_t_ref, after_t_ref, before_r_ref, after_r_ref,
                   z_ref, sems):
    variables, rows, width = y_ref.shape
    cells = rows // lines
    wide = reach_ref[...] == 2
    scale = jnp.where(wide, 0.25, 0.5)
    row_id = lax.broadcasted_iota(jnp.int32, (lines, width), 0)
    span = lax.axis_index("span")
    has_before = jnp.where(span > 0, 0.5, 0.0).astype(F32)
    has_after = jnp.where(span < lax.axis_size("span") - 1, 0.5, 0.0).astype(F32)

    def rounded(x):
        return x.astype(BF16).astype(F32)

    def down(x, end):
        return jnp.where(row_id == 0, end, pltpu.roll(x, 1, 0))

    def up(x, end):
        return jnp.where(row_id == lines - 1, end, pltpu.roll(x, lines - 1, 0))

    def copy_of(v):
        return pltpu.make_async_copy(z_ref.at[:, v], z_out.at[:, v], sems.at[v])

    acc_ref[...] = jnp.zeros_like(acc_ref)

    def one_variable(v, carry):
        unpack(before_t_ref, before_t_in, v, T_GROUPS)
        unpack(after_t_ref, after_t_in, v, T_GROUPS)
        unpack(before_r_ref, before_r_in, v, R_GROUPS)
        unpack(after_r_ref, after_r_in, v, R_GROUPS)

        def y_at(t):
            if t < 0:
                return before_t_ref[(t + 4) * lines:(t + 5) * lines, :]
            if t >= cells:
                return after_t_ref[(t - cells) * lines:(t - cells + 1) * lines, :]
            return y_ref[v, t * lines:(t + 1) * lines, :]

        def turn(get, t):
            return scale * jnp.where(wide, get(t + 2) - get(t - 2), get(t + 1) - get(t - 1))

        z1 = {}

        def z1_at(t):
            if t not in z1:
                z1[t] = rounded(turn(y_at, t))
            return z1[t]

        for pair in range(cells // 2):
            kept = []
            for t in (2 * pair, 2 * pair + 1):
                y = y_at(t)
                w1 = -turn(z1_at, t)
                one, two = slice(t, t + 1), slice(cells + t, cells + t + 1)
                before2, before1 = before_r_ref[one, :], before_r_ref[two, :]
                after1, after2 = after_r_ref[one, :], after_r_ref[two, :]
                z2 = rounded(0.5 * (up(y, after1) - down(y, before1)))
                z2_before = rounded(has_before * (y[0:1] - before2))
                z2_after = rounded(has_after * (after2 - y[lines - 1:lines]))
                w2 = 0.5 * (down(z2, z2_before) - up(z2, z2_after))
                kept.append((y, z1_at(t), z2, rounded(y) + w1 + w2))
            at = pl.ds(2 * pair * lines, 2 * lines)
            a, b = kept
            for family in range(3):
                z_ref[family, v, at, :] = jnp.concatenate([a[family], b[family]], axis=0).astype(BF16)
            w_ref[v, at, :] = jnp.concatenate([a[3], b[3]], axis=0).astype(BF16)
        for family in range(3):
            z = z_ref[family, v]
            acc_ref[...] += lax.dot_general(z, z, (((0,), (0,)), ((), ())), preferred_element_type=F32)
        copy_of(v).start()
        return carry

    lax.fori_loop(0, variables, one_variable, 0)
    gram_ref[:width, :] = acc_ref[:, :128]
    gram_ref[width:, :] = jnp.zeros((gram_ref.shape[0] - width, 128), F32)
    gram_ref[width:, :width - 128] = acc_ref[128:, 128:]
    for v in range(variables):
        copy_of(v).wait()


def stencils(y, before_t, after_t, before_r, after_r, reach, lines):
    variables, rows, width = y.shape
    cells = rows // lines
    return pl.pallas_call(
        functools.partial(stencil_kernel, lines),
        in_specs=[VMEM_SPEC] * 6,
        out_specs=[HBM_SPEC, VMEM_SPEC, VMEM_SPEC],
        out_shape=[
            pltpu.HBM((3, variables, rows, width), BF16),
            jax.ShapeDtypeStruct((variables, rows, width), BF16),
            jax.ShapeDtypeStruct((width + (width - 128), 128), F32),
        ],
        scratch_shapes=[
            pltpu.VMEM((width, width), F32),
            pltpu.VMEM((4 * lines, width), F32),
            pltpu.VMEM((4 * lines, width), F32),
            pltpu.VMEM((2 * cells, width), F32),
            pltpu.VMEM((2 * cells, width), F32),
            pltpu.VMEM((3, variables, rows, width), BF16),
            pltpu.SemaphoreType.DMA((variables,)),
        ],
        compiler_params=params(K2_MIB),
        name="stencils",
    )(reach, y, before_t, after_t, before_r, after_r)


def project_kernel(field_ref, w_ref, out_ref, acc_ref):
    for v in range(field_ref.shape[0]):
        part = lax.dot_general(w_ref[v], field_ref[v], (((0,), (0,)), ((), ())), preferred_element_type=F32)
        acc_ref[...] = part if v == 0 else acc_ref[...] + part
    out_ref[...] = acc_ref[...].T.astype(BF16)


def project(fields, w):
    variables, rows, columns = fields.shape
    width = w.shape[2]
    return pl.pallas_call(
        project_kernel,
        in_specs=[VMEM_SPEC] * 2,
        out_specs=VMEM_SPEC,
        out_shape=jax.ShapeDtypeStruct((columns, width), BF16),
        scratch_shapes=[pltpu.VMEM((width, columns), F32)],
        compiler_params=params(K3_MIB),
        cost_estimate=pl.CostEstimate(flops=2 * variables * rows * columns * 256,
                                      bytes_accessed=variables * rows * columns * 2, transcendentals=0),
        name="project",
    )(fields, w)


def split3(x):
    high = x.astype(BF16)
    rest = x - high.astype(F32)
    mid = rest.astype(BF16)
    return high, mid, (rest - mid.astype(F32)).astype(BF16)


def inverse_factor_of(width, gram_ref, out_ref, a_ref):
    size = 16
    packed = gram_ref[...]
    a_ref[...] = jnp.zeros_like(a_ref)
    a_ref[:, :128] = packed[:width]
    a_ref[:128, 128:width] = packed[128:width].T
    a_ref[128:, 128:width] = packed[width:, :width - 128]
    a_ref[:, 256:] = jnp.where(
        lax.broadcasted_iota(jnp.int32, (width, 256), 0) == lax.broadcasted_iota(jnp.int32, (width, 256), 1),
        1.0, 0.0)
    row = lax.broadcasted_iota(jnp.int32, (size, 128), 0)
    lane = lax.broadcasted_iota(jnp.int32, (size, 256), 1)
    for start in range(0, width, size):
        panels = [a_ref[start:start + size, tile * 128:(tile + 1) * 128] for tile in range(4)]
        tile, offset = start // 128, start % 128
        cols = [jnp.broadcast_to(panels[tile][:, offset + j:offset + j + 1], (size, 128)) for j in range(size)]
        for j in range(size):
            pivot = jnp.broadcast_to(cols[j][j:j + 1, :], (size, 128))
            inv = lax.rsqrt(pivot)
            inv = inv * (1.5 - 0.5 * pivot * inv * inv)
            low = cols[j] * inv
            for i in range(j + 1, size):
                cols[i] = cols[i] - low * jnp.broadcast_to(low[i:i + 1, :], (size, 128))
            below = jnp.where(row > j, low, 0.0)
            for p in range(4):
                lead = jnp.broadcast_to(panels[p][j:j + 1, :], (size, 128)) * inv
                panels[p] = jnp.where(row == j, lead, panels[p] - below * lead)
        out_ref[start:start + size, :] = jnp.concatenate([panels[2], panels[3]], axis=1)[:, :width]
        if start + size < width:
            whole = jnp.concatenate(panels, axis=1)
            left = jnp.where(lane >= start + size, whole[:, :256], 0.0)
            lh, lm, ll = split3(left)
            rh, rm, rl = split3(whole)
            lhs = jnp.concatenate([lh, lh, lm, lm, lh, ll], axis=0)
            rhs = jnp.concatenate([rh, rm, rh, rm, rl, rh], axis=0)
            update = lax.dot_general(lhs, rhs, (((0,), (0,)), ((), ())), preferred_element_type=F32)
            a_ref[start + size:, :] -= update[start + size:width, :]


def basis_kernel(scale, gram_ref, z_hbm, out_hbm, inv_ref, a_ref, high_ref, low_ref, z_ref, out_ref, z_sem, sems):
    width = z_ref.shape[1]
    blocks = sems.shape[0]
    rows = z_ref.shape[0] // blocks
    z_copy = pltpu.make_async_copy(z_hbm, z_ref, z_sem)
    z_copy.start()
    inverse_factor_of(width, gram_ref, inv_ref, a_ref)
    turned = inv_ref[...].T * scale
    high_ref[...] = turned.astype(BF16)
    low_ref[...] = (turned - high_ref[...].astype(F32)).astype(BF16)
    z_copy.wait()

    def copy_of(i):
        at = pl.ds(pl.multiple_of(i * rows, rows), rows)
        return pltpu.make_async_copy(out_ref.at[at], out_hbm.at[at], sems.at[i])

    def one_block(i, carry):
        at = pl.ds(pl.multiple_of(i * rows, rows), rows)
        z = z_ref[at]
        out_ref[at] = (jnp.dot(z, low_ref[...], preferred_element_type=F32)
                       + jnp.dot(z, high_ref[...], preferred_element_type=F32))
        copy_of(i).start()
        return carry

    lax.fori_loop(0, blocks, one_block, 0)
    for i in range(blocks):
        copy_of(i).wait()


def basis_of(z, gram, scale):
    rows, width = z.shape
    return pl.pallas_call(
        functools.partial(basis_kernel, scale),
        in_specs=[VMEM_SPEC, HBM_SPEC],
        out_specs=[HBM_SPEC, VMEM_SPEC],
        out_shape=[pltpu.HBM((rows, width), F32), jax.ShapeDtypeStruct((width, width), F32)],
        scratch_shapes=[pltpu.VMEM((width, 512), F32), pltpu.VMEM((width, width), BF16),
                        pltpu.VMEM((width, width), BF16), pltpu.VMEM((rows, width), BF16),
                        pltpu.VMEM((rows, width), F32), pltpu.SemaphoreType.DMA,
                        pltpu.SemaphoreType.DMA((K4_BLOCKS,))],
        compiler_params=params(K4_MIB),
        cost_estimate=pl.CostEstimate(flops=1000, bytes_accessed=1000, transcendentals=0),
        name="basis",
    )(gram, in_hbm(z))


def coefficients_kernel(scale, parts_ref, inv_ref, out_ref):
    owned = jnp.sum(parts_ref[...].astype(F32), axis=0)
    out_ref[...] = lax.dot_general(owned, inv_ref[...], (((1,), (1,)), ((), ())),
                                   precision=lax.Precision.HIGHEST, preferred_element_type=F32) * scale


def coefficients_of(parts, inv, scale):
    _, rows, width = parts.shape
    return pl.pallas_call(
        functools.partial(coefficients_kernel, scale),
        in_specs=[pl.BlockSpec(memory_space=pltpu.VMEM)] * 2,
        out_specs=pl.BlockSpec(memory_space=pltpu.VMEM),
        out_shape=jax.ShapeDtypeStruct((rows, width), F32),
        compiler_params=params(32),
        name="coefficients",
    )(parts, inv)


def reduce_all(x, meanwhile):
    passages, layers = lax.axis_size("passage"), lax.axis_size("span")

    def exchange(x, axis, length, moves, meanwhile=None):
        parts = [lax.ppermute(x, axis, [(i, move(i)) for i in range(length)]) for move in moves]
        if meanwhile is not None:
            parts, meanwhile = lax.optimization_barrier((parts, meanwhile))
        for part in parts:
            x = x + part
        return x, meanwhile

    x, _ = exchange(x, "passage", passages, [lambda i: i ^ 1])
    x, meanwhile = exchange(x, "passage", passages, [lambda i, k=k: (i + 2 * k) % passages for k in (1, 3, 2)],
                            meanwhile)
    x, _ = exchange(x, "span", layers, [lambda i, k=k: i // 4 * 4 + (i + k) % 4 for k in (1, 3, 2)])
    x, _ = exchange(x, "span", layers, [lambda i, k=k: (i + 4 * k) % layers for k in (1, 3, 2)])
    return x, meanwhile


def shards(snapshots, sketch, blade_row, row_speed, stencil_reach):
    variables, cells, lines, columns = snapshots.shape
    width = sketch.shape[1]
    passages, layers = lax.axis_size("passage"), lax.axis_size("span")
    row_total = 3 * variables * cells * passages * lines * layers
    fields, y, first_t, last_t, first_r, last_r = fields_and_sketch(
        snapshots.reshape(variables, cells * lines, columns), sketch.T, blade_row, row_speed,
        lines, lines * layers)
    ring_up = [(i, (i + 1) % passages) for i in range(passages)]
    ring_down = [(j, i) for i, j in ring_up]
    line_up = [(i, i + 1) for i in range(layers - 1)]
    line_down = [(j, i) for i, j in line_up]
    before_r = lax.ppermute(last_r, "span", line_up)
    after_r = lax.ppermute(first_r, "span", line_down)
    before_t = lax.ppermute(last_t, "passage", ring_up)
    after_t = lax.ppermute(first_t, "passage", ring_down)
    reach = jnp.broadcast_to(stencil_reach[:, None], (lines, width))
    z, w, gram = stencils(y, before_t, after_t, before_r, after_r, reach, lines)
    projected = project(fields, w)
    gram, projected = reduce_all(gram, projected)
    owned = columns // (passages * layers)
    parts = lax.all_to_all(projected.reshape(passages * layers, owned, width), ("passage", "span"), 0, 0, tiled=True)
    basis, inv = basis_of(z.reshape(-1, width), gram, math.sqrt(row_total))
    coefficients = coefficients_of(parts, inv, 1.0 / math.sqrt(row_total))
    return basis.reshape(3 * variables, cells, lines, width), coefficients


def solution(mesh):
    return jax.shard_map(
        shards,
        mesh=mesh,
        in_specs=(P(None, "passage", "span", None), P(), P("passage"), P(), P("span")),
        out_specs=(P(None, "passage", "span", None), P(("passage", "span"), None)),
        check_vma=False,
    )
```

time: 99.2 us -> 78.9 us (0.80)
  local copies, waits for them, and re-layouts: 11.6 us -> 0.07 us
  waiting for transfers between devices: 19.5 us -> 14.1 us
  starting transfers between devices: 34.8 us -> 32.8 us
  Pallas kernels: 32 us -> 30.9 us
    unnamed x16 -> x2, local copies, waits for them, and re-layouts: 11.5 us -> 0.01 us
    ppermute x1, waiting for transfers between devices: 3.81 us -> 0.35 us  [shards(): before_r = lax.ppermute(last_r, 'span', line_up)]
    ppermute x10, waiting for transfers between devices: 8.4 us -> 6.5 us  [exchange(): lax.ppermute(x, axis, [(i, move(i)) for i in range(length)])]
    ppermute x10, starting transfers between devices: 18 us -> 16.8 us  [exchange(): lax.ppermute(x, axis, [(i, move(i)) for i in range(length)])]
    pallas_call x5 -> x4, Pallas kernels: 31.1 us -> 29.9 us  [the longest x1 10.5 us: basis_of(): pl.pallas_call(functools.partial(basis_kernel, scale), in_specs=[VMEM_SPE...]
  transfers between devices with their start and end apart: 15 -> 15, of which waited for: 8 -> 8; matrix products, arithmetic and copies ran while one was open for 0% -> 0% of each run, Pallas kernels for 17% -> 16%
where the time goes in v2:
time: 78.9 us; the launch traced here: 78.7 us
  starting transfers between devices  32.8 us (42%)
  Pallas kernels  30.9 us (39%)
  waiting for transfers between devices  14.1 us (18%)
    ppermute x10, starting transfers between devices, exchange(): lax.ppermute(x, axis, [(i, move(i)) for i in range(length)])  16.8 us
    pallas_call x1, Pallas kernels, basis_of(): pl.pallas_call(functools.partial(basis_kernel, scale), in_specs=[VMEM_SPE...  10.5 us
    pallas_call x1, Pallas kernels, fields_and_sketch(): pl.pallas_call(functools.partial(fields_kernel, radial_total, lines), in_...  8.92 us
    all_to_all x1, starting transfers between devices, shards(): lax.all_to_all(projected.reshape(passages * layers, owned, width), ('pass...  8.89 us
    pallas_call x1, Pallas kernels, stencils(): pl.pallas_call(functools.partial(stencil_kernel, lines), in_specs=[VMEM_S...  8.19 us
    ppermute x10, waiting for transfers between devices, exchange(): lax.ppermute(x, axis, [(i, move(i)) for i in range(length)])  6.5 us
    ppermute x1, waiting for transfers between devices, shards(): after_r = lax.ppermute(first_r, 'span', line_down)  3.75 us
    all_to_all x1, waiting for transfers between devices, shards(): lax.all_to_all(projected.reshape(passages * layers, owned, width), ('pass...  3.52 us
  transfers between devices with their start and end apart: 15, of which 8 were waited for; matrix products, arithmetic and copies ran while one was open for 0% of the time, Pallas kernels for 16%

profile of v2, /device:TPU:1, one launch (start us, length us, event | category | flops | bytes accessed | tf_op | source)
XLA Modules:
  0.0 78.7 jit_solution(3389570535304936863)
XLA Ops:
  0.6 8.9 %fields_sketch.1 = (bf16[5,768,1024]{2,1,0:T(8,128)(2,1)S(1)}, f32[5,768,144]{2,1,0:T(8,128)S(1)}, bf16[5,112,128]{2,1,0:T(8,128)(2,1)S(1)}, bf16[5,112,128]{2,1...) custom-call(s32[32]{0:T(128)} %blade_hbm.1, f32[2]{0:T(128)} %speed_hbm.1, ...), custom_call_target="tpu_custom_call" | custom-call | tf_op jit(solution)/shard_map/fields_sketch/pallas_call | solution.py:149
  9.6 2.6 %collective-permute-start = (bf16[5,112,128]{2,1,0:T(8,128)(2,1)S(1)}, bf16[5,112,128]{2,1,0:T(8,128)(2,1)S(1)}, u32[]{:S(2)}, u32[]{:S(2)}) collective-permute-start(bf16[5,112,128]{2,1,0:T(8,128)(2,1)S(1)} %get-tuple-element.18), channel_id=1, source_target_pairs={{0,16},{16,32},{32,48},{48,64},{64,80},{80,96},{96,112},{112,0},{1... | collective-permute-start | bytes 430088 | tf_op jit(solution)/shard_map/ppermute | solution.py:446
  12.2 3.2 %collective-permute-start.2 = (bf16[5,80,128]{2,1,0:T(8,128)(2,1)S(1)}, bf16[5,80,128]{2,1,0:T(8,128)(2,1)S(1)}, u32[]{:S(2)}, u32[]{:S(2)}) collective-permute-start(bf16[5,80,128]{2,1,0:T(8,128)(2,1)S(1)} %get-tuple-element.20), channel_id=1, source_target_pairs={{0,1},{1,2},{2,3},{3,4},{4,5},{5,6},{6,7},{7,8},{8,9},{9,10},{10,1... | collective-permute-start | bytes 307208 | tf_op jit(solution)/shard_map/ppermute | solution.py:444
  15.4 1.3 %collective-permute-start.3 = (bf16[5,80,128]{2,1,0:T(8,128)(2,1)S(1)}, bf16[5,80,128]{2,1,0:T(8,128)(2,1)S(1)}, u32[]{:S(2)}, u32[]{:S(2)}) collective-permute-start(bf16[5,80,128]{2,1,0:T(8,128)(2,1)S(1)} %get-tuple-element.21), channel_id=1, source_target_pairs={{1,0},{2,1},{3,2},{4,3},{5,4},{6,5},{7,6},{8,7},{9,8},{10,9},{11,1... | collective-permute-start | bytes 307208 | tf_op jit(solution)/shard_map/ppermute | solution.py:445
  16.7 0.4 collective-permute-done.2.before_r_in
  17.0 3.7 %collective-permute-done.3.after_r_in = bf16[5,80,128]{2,1,0:T(8,128)(2,1)S(1)} collective-permute-done((bf16[5,80,128]{2,1,0:T(8,128)(2,1)S(1)}, bf16[5,80,128]{2,1,0:T(8,128)(2,1)S(1)}, u32[]{:S(2)}, u32[]{:S(2)}) %collective-permute-start.3) | collective-permute-done | bytes 102432 | tf_op jit(solution)/shard_map/ppermute | solution.py:445
  20.8 0.0 collective-permute-done.1.after_t_in
  20.8 0.1 broadcast_in_dim.2.reach_ref
  20.9 8.2 %stencils.1 = (bf16[3,5,768,144]{3,2,1,0:T(8,128)(2,1)}, bf16[5,768,144]{2,1,0:T(8,128)(2,1)S(1)}, f32[160,128]{1,0:T(8,128)S(1)}) custom-call(s32[24,144]{1,0:T(8,128)S(1)} %broadcast_in_dim.2.reach_ref, f32[5,768,144]{2,1,0:T(8,128)S(1)} %get-tuple-element.17.y_ref, bf16[5,112,128]{2,1,0:T(8,128)(2,1)S(1)} %collective-permute-done.before_t_in, ...), custom_call_target="tpu_custom_call" | custom-call | tf_op jit(solution)/shard_map/stencils/pallas_call | solution.py:257
  29.1 3.4 %collective-permute-start.4 = (f32[160,128]{1,0:T(8,128)S(1)}, f32[160,128]{1,0:T(8,128)S(1)}, u32[]{:S(2)}, u32[]{:S(2)}) collective-permute-start(f32[160,128]{1,0:T(8,128)S(1)} %get-tuple-element.22), channel_id=1, source_target_pairs={{0,16},{16,0},{32,48},{48,32},{64,80},{80,64},{96,112},{112,96},{1... | collective-permute-start | bytes 245768 | tf_op jit(solution)/shard_map/ppermute | solution.py:417
  32.4 0.9 %collective-permute-done.4 = f32[160,128]{1,0:T(8,128)S(1)} collective-permute-done((f32[160,128]{1,0:T(8,128)S(1)}, f32[160,128]{1,0:T(8,128)S(1)}, u32[]{:S(2)}, u32[]{:S(2)}) %collective-permute-start.4) | collective-permute-done | bytes 81952 | tf_op jit(solution)/shard_map/ppermute | solution.py:417
  33.4 1.6 %collective-permute-start.7 = (f32[160,128]{1,0:T(8,128)S(1)}, f32[160,128]{1,0:T(8,128)S(1)}, u32[]{:S(2)}, u32[]{:S(2)}) collective-permute-start(f32[160,128]{1,0:T(8,128)S(1)} %add.30), channel_id=1, source_target_pairs={{0,64},{16,80},{32,96},{48,112},{64,0},{80,16},{96,32},{112,48},{1... | collective-permute-start | bytes 245768 | tf_op jit(solution)/shard_map/ppermute | solution.py:417
  35.0 0.9 %collective-permute-start.6 = (f32[160,128]{1,0:T(8,128)S(1)}, f32[160,128]{1,0:T(8,128)S(1)}, u32[]{:S(2)}, u32[]{:S(2)}) collective-permute-start(f32[160,128]{1,0:T(8,128)S(1)} %add.30), channel_id=1, source_target_pairs={{0,96},{16,112},{32,0},{48,16},{64,32},{80,48},{96,64},{112,80},{1... | collective-permute-start | bytes 245768 | tf_op jit(solution)/shard_map/ppermute | solution.py:417
  35.8 0.6 collective-permute-start.5
  36.5 2.3 %project.1 = bf16[1024,144]{1,0:T(8,128)(2,1)} custom-call(bf16[5,768,1024]{2,1,0:T(8,128)(2,1)S(1)} %get-tuple-element.23.field_ref, bf16[5,768,144]{2,1,0:T(8,128)(2,1)S(1)} %get-tuple-element.24.w_ref), custom_call_target="tpu_custom_call" | custom-call | flops 2013265920 | bytes 7864320 | tf_op jit(solution)/shard_map/project/pallas_call | solution.py:290
  38.8 0.0 collective-permute-done.7
  38.8 0.7 collective-permute-done.6
  39.4 0.9 %collective-permute-done.5 = f32[160,128]{1,0:T(8,128)S(1)} collective-permute-done((f32[160,128]{1,0:T(8,128)S(1)}, f32[160,128]{1,0:T(8,128)S(1)}, u32[]{:S(2)}, u32[]{:S(2)}) %collective-permute-start.5) | collective-permute-done | bytes 81952 | tf_op jit(solution)/shard_map/ppermute | solution.py:417
  40.4 2.7 %collective-permute-start.10 = (f32[160,128]{1,0:T(8,128)S(1)}, f32[160,128]{1,0:T(8,128)S(1)}, u32[]{:S(2)}, u32[]{:S(2)}) collective-permute-start(f32[160,128]{1,0:T(8,128)S(1)} %add_add_fusion.2), channel_id=1, source_target_pairs={{0,2},{1,3},{2,0},{3,1},{4,6},{5,7},{6,4},{7,5},{8,10},{9,11},{10,... | collective-permute-start | bytes 245768 | tf_op jit(solution)/shard_map/ppermute | solution.py:417
  43.1 2.3 %collective-permute-start.9 = (f32[160,128]{1,0:T(8,128)S(1)}, f32[160,128]{1,0:T(8,128)S(1)}, u32[]{:S(2)}, u32[]{:S(2)}) collective-permute-start(f32[160,128]{1,0:T(8,128)S(1)} %add_add_fusion.2), channel_id=1, source_target_pairs={{0,3},{1,0},{2,1},{3,2},{4,7},{5,4},{6,5},{7,6},{8,11},{9,8},{10,9... | collective-permute-start | bytes 245768 | tf_op jit(solution)/shard_map/ppermute | solution.py:417
  45.4 0.5 collective-permute-start.8
  45.9 2.7 %collective-permute-done.9 = f32[160,128]{1,0:T(8,128)S(1)} collective-permute-done((f32[160,128]{1,0:T(8,128)S(1)}, f32[160,128]{1,0:T(8,128)S(1)}, u32[]{:S(2)}, u32[]{:S(2)}) %collective-permute-start.9) | collective-permute-done | bytes 81952 | tf_op jit(solution)/shard_map/ppermute | solution.py:417
  48.6 1.3 %collective-permute-done.8 = f32[160,128]{1,0:T(8,128)S(1)} collective-permute-done((f32[160,128]{1,0:T(8,128)S(1)}, f32[160,128]{1,0:T(8,128)S(1)}, u32[]{:S(2)}, u32[]{:S(2)}) %collective-permute-start.8) | collective-permute-done | bytes 81952 | tf_op jit(solution)/shard_map/ppermute | solution.py:417
  49.9 3.4 %collective-permute-start.13 = (f32[160,128]{1,0:T(8,128)S(1)}, f32[160,128]{1,0:T(8,128)S(1)}, u32[]{:S(2)}, u32[]{:S(2)}) collective-permute-start(f32[160,128]{1,0:T(8,128)S(1)} %add_add_fusion.1), channel_id=1, source_target_pairs={{0,8},{1,9},{2,10},{3,11},{4,12},{5,13},{6,14},{7,15},{8,0},{9,1},... | collective-permute-start | bytes 245768 | tf_op jit(solution)/shard_map/ppermute | solution.py:417
  53.3 0.7 collective-permute-start.12
  54.0 0.7 collective-permute-start.11
  54.8 8.9 %all-to-all-start = ((bf16[128,8,144]{2,1,0:T(8,128)(2,1)}), bf16[128,8,144]{2,1,0:T(8,128)(2,1)S(1)}, u32[]{:S(2)}, u32[]{:S(2)}) async-start(bf16[128,8,144]{2,1,0:T(8,128)(2,1)} %bitcast.4), calls=%async_computation | async-start | bytes 1048576 | tf_op jit(solution)/shard_map/all_to_all | solution.py:453
  63.7 0.0 collective-permute-done.13
  63.7 0.0 collective-permute-done.11
  63.7 10.5 %basis.1 = (f32[11520,144]{1,0:T(8,128)}, f32[144,144]{1,0:T(8,128)S(1)}) custom-call(f32[160,128]{1,0:T(8,128)S(1)} %add_add_fusion.gram_ref, bf16[11520,144]{1,0:T(8,128)(2,1)} %bitcast.6), custom_call_target="tpu_custom_call" | custom-call | flops 1000 | bytes 1000 | tf_op jit(solution)/shard_map/basis/pallas_call | solution.py:380
  74.2 3.5 %all-to-all-done.parts_ref = bf16[128,8,144]{2,1,0:T(8,128)(2,1)S(1)} async-done(((bf16[128,8,144]{2,1,0:T(8,128)(2,1)}), bf16[128,8,144]{2,1,0:T(8,128)(2,1)S(1)}, u32[]{:S(2)}, u32[]{:S(2)}) %all-to-all-start) | async-done | bytes 294944 | tf_op jit(solution)/shard_map/all_to_all | solution.py:453
  77.7 1.0 %coefficients.1 = f32[8,144]{1,0:T(8,128)} custom-call(bf16[128,8,144]{2,1,0:T(8,128)(2,1)S(1)} %all-to-all-done.parts_ref, f32[144,144]{1,0:T(8,128)S(1)} %get-tuple-element.31.inv_ref), custom_call_target="tpu_custom_call" | custom-call | tf_op jit(solution)/shard_map/coefficients/pallas_call | solution.py:403
  (10 shorter events, 0.1 us)
Async XLA Ops:
  0.6 20.2 %copy-start = (s32[24]{0:T(128)S(1)}, s32[24]{0:T(128)}, u32[]{:S(2)}) copy-start(s32[24]{0:T(128)} %param.9) | copy-start | bytes 292
  9.6 11.2 %collective-permute-start = (bf16[5,112,128]{2,1,0:T(8,128)(2,1)S(1)}, bf16[5,112,128]{2,1,0:T(8,128)(2,1)S(1)}, u32[]{:S(2)}, u32[]{:S(2)}) collective-permute-start(bf16[5,112,128]{2,1,0:T(8,128)(2,1)S(1)} %get-tuple-element.18), channel_id=1, source_target_pairs={{0,16},{16,32},{32,48},{48,64},{64,80},{80,96},{96,112},{112,0},{1... | collective-permute-start | bytes 430088 | tf_op jit(solution)/shard_map/ppermute | solution.py:446
  12.2 8.6 %collective-permute-start.1 = (bf16[5,112,128]{2,1,0:T(8,128)(2,1)S(1)}, bf16[5,112,128]{2,1,0:T(8,128)(2,1)S(1)}, u32[]{:S(2)}, u32[]{:S(2)}) collective-permute-start(bf16[5,112,128]{2,1,0:T(8,128)(2,1)S(1)} %get-tuple-element.19), channel_id=1, source_target_pairs={{16,0},{32,16},{48,32},{64,48},{80,64},{96,80},{112,96},{0,112},{1... | collective-permute-start | bytes 430088 | tf_op jit(solution)/shard_map/ppermute | solution.py:447
  12.2 4.8 %collective-permute-start.2 = (bf16[5,80,128]{2,1,0:T(8,128)(2,1)S(1)}, bf16[5,80,128]{2,1,0:T(8,128)(2,1)S(1)}, u32[]{:S(2)}, u32[]{:S(2)}) collective-permute-start(bf16[5,80,128]{2,1,0:T(8,128)(2,1)S(1)} %get-tuple-element.20), channel_id=1, source_target_pairs={{0,1},{1,2},{2,3},{3,4},{4,5},{5,6},{6,7},{7,8},{8,9},{9,10},{10,1... | collective-permute-start | bytes 307208 | tf_op jit(solution)/shard_map/ppermute | solution.py:444
  15.4 5.4 %collective-permute-start.3 = (bf16[5,80,128]{2,1,0:T(8,128)(2,1)S(1)}, bf16[5,80,128]{2,1,0:T(8,128)(2,1)S(1)}, u32[]{:S(2)}, u32[]{:S(2)}) collective-permute-start(bf16[5,80,128]{2,1,0:T(8,128)(2,1)S(1)} %get-tuple-element.21), channel_id=1, source_target_pairs={{1,0},{2,1},{3,2},{4,3},{5,4},{6,5},{7,6},{8,7},{9,8},{10,9},{11,1... | collective-permute-start | bytes 307208 | tf_op jit(solution)/shard_map/ppermute | solution.py:445
  29.1 4.3 %collective-permute-start.4 = (f32[160,128]{1,0:T(8,128)S(1)}, f32[160,128]{1,0:T(8,128)S(1)}, u32[]{:S(2)}, u32[]{:S(2)}) collective-permute-start(f32[160,128]{1,0:T(8,128)S(1)} %get-tuple-element.22), channel_id=1, source_target_pairs={{0,16},{16,0},{32,48},{48,32},{64,80},{80,64},{96,112},{112,96},{1... | collective-permute-start | bytes 245768 | tf_op jit(solution)/shard_map/ppermute | solution.py:417
  33.4 5.4 %collective-permute-start.7 = (f32[160,128]{1,0:T(8,128)S(1)}, f32[160,128]{1,0:T(8,128)S(1)}, u32[]{:S(2)}, u32[]{:S(2)}) collective-permute-start(f32[160,128]{1,0:T(8,128)S(1)} %add.30), channel_id=1, source_target_pairs={{0,64},{16,80},{32,96},{48,112},{64,0},{80,16},{96,32},{112,48},{1... | collective-permute-start | bytes 245768 | tf_op jit(solution)/shard_map/ppermute | solution.py:417
  35.0 4.5 %collective-permute-start.6 = (f32[160,128]{1,0:T(8,128)S(1)}, f32[160,128]{1,0:T(8,128)S(1)}, u32[]{:S(2)}, u32[]{:S(2)}) collective-permute-start(f32[160,128]{1,0:T(8,128)S(1)} %add.30), channel_id=1, source_target_pairs={{0,96},{16,112},{32,0},{48,16},{64,32},{80,48},{96,64},{112,80},{1... | collective-permute-start | bytes 245768 | tf_op jit(solution)/shard_map/ppermute | solution.py:417
  35.8 4.5 %collective-permute-start.5 = (f32[160,128]{1,0:T(8,128)S(1)}, f32[160,128]{1,0:T(8,128)S(1)}, u32[]{:S(2)}, u32[]{:S(2)}) collective-permute-start(f32[160,128]{1,0:T(8,128)S(1)} %add.30), channel_id=1, source_target_pairs={{0,32},{16,48},{32,64},{48,80},{64,96},{80,112},{96,0},{112,16},{1... | collective-permute-start | bytes 245768 | tf_op jit(solution)/shard_map/ppermute | solution.py:417
  40.4 5.5 %collective-permute-start.10 = (f32[160,128]{1,0:T(8,128)S(1)}, f32[160,128]{1,0:T(8,128)S(1)}, u32[]{:S(2)}, u32[]{:S(2)}) collective-permute-start(f32[160,128]{1,0:T(8,128)S(1)} %add_add_fusion.2), channel_id=1, source_target_pairs={{0,2},{1,3},{2,0},{3,1},{4,6},{5,7},{6,4},{7,5},{8,10},{9,11},{10,... | collective-permute-start | bytes 245768 | tf_op jit(solution)/shard_map/ppermute | solution.py:417
  43.1 5.5 %collective-permute-start.9 = (f32[160,128]{1,0:T(8,128)S(1)}, f32[160,128]{1,0:T(8,128)S(1)}, u32[]{:S(2)}, u32[]{:S(2)}) collective-permute-start(f32[160,128]{1,0:T(8,128)S(1)} %add_add_fusion.2), channel_id=1, source_target_pairs={{0,3},{1,0},{2,1},{3,2},{4,7},{5,4},{6,5},{7,6},{8,11},{9,8},{10,9... | collective-permute-start | bytes 245768 | tf_op jit(solution)/shard_map/ppermute | solution.py:417
  45.4 4.5 %collective-permute-start.8 = (f32[160,128]{1,0:T(8,128)S(1)}, f32[160,128]{1,0:T(8,128)S(1)}, u32[]{:S(2)}, u32[]{:S(2)}) collective-permute-start(f32[160,128]{1,0:T(8,128)S(1)} %add_add_fusion.2), channel_id=1, source_target_pairs={{0,1},{1,2},{2,3},{3,0},{4,5},{5,6},{6,7},{7,4},{8,9},{9,10},{10,1... | collective-permute-start | bytes 245768 | tf_op jit(solution)/shard_map/ppermute | solution.py:417
  49.9 13.8 %collective-permute-start.13 = (f32[160,128]{1,0:T(8,128)S(1)}, f32[160,128]{1,0:T(8,128)S(1)}, u32[]{:S(2)}, u32[]{:S(2)}) collective-permute-start(f32[160,128]{1,0:T(8,128)S(1)} %add_add_fusion.1), channel_id=1, source_target_pairs={{0,8},{1,9},{2,10},{3,11},{4,12},{5,13},{6,14},{7,15},{8,0},{9,1},... | collective-permute-start | bytes 245768 | tf_op jit(solution)/shard_map/ppermute | solution.py:417
  53.3 10.4 %collective-permute-start.12 = (f32[160,128]{1,0:T(8,128)S(1)}, f32[160,128]{1,0:T(8,128)S(1)}, u32[]{:S(2)}, u32[]{:S(2)}) collective-permute-start(f32[160,128]{1,0:T(8,128)S(1)} %add_add_fusion.1), channel_id=1, source_target_pairs={{0,12},{1,13},{2,14},{3,15},{4,0},{5,1},{6,2},{7,3},{8,4},{9,5},{1... | collective-permute-start | bytes 245768 | tf_op jit(solution)/shard_map/ppermute | solution.py:417
  54.0 9.7 %collective-permute-start.11 = (f32[160,128]{1,0:T(8,128)S(1)}, f32[160,128]{1,0:T(8,128)S(1)}, u32[]{:S(2)}, u32[]{:S(2)}) collective-permute-start(f32[160,128]{1,0:T(8,128)S(1)} %add_add_fusion.1), channel_id=1, source_target_pairs={{0,4},{1,5},{2,6},{3,7},{4,8},{5,9},{6,10},{7,11},{8,12},{9,13},{1... | collective-permute-start | bytes 245768 | tf_op jit(solution)/shard_map/ppermute | solution.py:417
  54.8 23.0 %all-to-all-start = ((bf16[128,8,144]{2,1,0:T(8,128)(2,1)}), bf16[128,8,144]{2,1,0:T(8,128)(2,1)S(1)}, u32[]{:S(2)}, u32[]{:S(2)}) async-start(bf16[128,8,144]{2,1,0:T(8,128)(2,1)} %bitcast.4), calls=%async_computation | async-start | bytes 1048576 | tf_op jit(solution)/shard_map/all_to_all | solution.py:453

commit v3 on v2

--- a/solution.py
+++ b/solution.py
@@ -13,7 +13,7 @@
 MIB = 1024 * 1024
 K1_MIB = 24
 K1_CHUNKS = 8
-K4_BLOCKS = 10
+K4_BLOCKS = 5
 K2_MIB = 24
 K3_MIB = 24
 K4_MIB = 24
@@ -170,31 +170,93 @@
     )(in_hbm(blade_row), in_hbm(row_speed), in_hbm(sketch_t), in_hbm(snapshots))
 
 
-def stencil_kernel(lines, reach_ref, y_ref, before_t_in, after_t_in, before_r_in, after_r_in,
-                   z_out, w_ref, gram_ref, acc_ref, before_t_ref, after_t_ref, before_r_ref, after_r_ref,
-                   z_ref, sems):
+def rounded(x):
+    return x.astype(BF16).astype(F32)
+
+
+def shift_down(x, end):
+    return jnp.where(lax.broadcasted_iota(jnp.int32, x.shape, 0) == 0, end, pltpu.roll(x, 1, 0))
+
+
+def shift_up(x, end):
+    last = x.shape[0] - 1
+    return jnp.where(lax.broadcasted_iota(jnp.int32, x.shape, 0) == last, end, pltpu.roll(x, last, 0))
+
+
+def turn(wide, scale, get, t):
+    return scale * jnp.where(wide, get(t + 2) - get(t - 2), get(t + 1) - get(t - 1))
+
+
+def inner_kernel(lines, reach_ref, y_ref, z_out, z_ref, gram_ref, sems):
     variables, rows, width = y_ref.shape
     cells = rows // lines
     wide = reach_ref[...] == 2
     scale = jnp.where(wide, 0.25, 0.5)
-    row_id = lax.broadcasted_iota(jnp.int32, (lines, width), 0)
+    inner = pl.ds(2 * lines, rows - 4 * lines)
+
+    def copies_of(v):
+        return [pltpu.make_async_copy(z_ref.at[0, v], z_out.at[0, v], sems.at[0, v]),
+                pltpu.make_async_copy(z_ref.at[1, v, inner], z_out.at[1, v, inner], sems.at[1, v])]
+
+    gram_ref[...] = jnp.zeros_like(gram_ref)
+
+    def one_variable(v, carry):
+        def y_at(t):
+            return y_ref[v, t * lines:(t + 1) * lines, :]
+
+        for pair in range(cells // 2):
+            at = pl.ds(2 * pair * lines, 2 * lines)
+            z_ref[0, v, at, :] = y_ref[v, at, :].astype(BF16)
+            if 0 < pair < cells // 2 - 1:
+                z1 = [turn(wide, scale, y_at, t) for t in (2 * pair, 2 * pair + 1)]
+                z_ref[1, v, at, :] = jnp.concatenate(z1, axis=0).astype(BF16)
+        for z in (z_ref[0, v], z_ref[1, v, inner]):
+            gram_ref[...] += lax.dot_general(z, z, (((0,), (0,)), ((), ())), preferred_element_type=F32)
+        for copy in copies_of(v):
+            copy.start()
+        return carry
+
+    lax.fori_loop(0, variables, one_variable, 0)
+    for v in range(variables):
+        for copy in copies_of(v):
+            copy.wait()
+
+
+def inner_stencils(y, reach, lines):
+    variables, rows, width = y.shape
+    return pl.pallas_call(
+        functools.partial(inner_kernel, lines),
+        in_specs=[VMEM_SPEC] * 2,
+        out_specs=[HBM_SPEC, VMEM_SPEC, VMEM_SPEC],
+        out_shape=[
+            pltpu.HBM((2, variables, rows, width), BF16),
+            jax.ShapeDtypeStruct((2, variables, rows, width), BF16),
+            jax.ShapeDtypeStruct((width, width), F32),
+        ],
+        scratch_shapes=[pltpu.SemaphoreType.DMA((2, variables))],
+        compiler_params=params(16),
+        cost_estimate=pl.CostEstimate(flops=4 * variables * rows * 256 * 256, bytes_accessed=variables * rows * 2048,
+                                      transcendentals=0),
+        name="inner_stencils",
+    )(reach, y)
+
+
+def outer_kernel(lines, reach_ref, y_ref, before_t_in, after_t_in, before_r_in, after_r_in, inner_gram_ref,
+                 rim_out, z_out, z_ref, edge_t_ref, edge_r_ref, gram_ref,
+                 acc_ref, before_t_ref, after_t_ref, before_r_ref, after_r_ref, rim_ref, sems):
+    variables, rows, width = y_ref.shape
+    cells = rows // lines
+    wide = reach_ref[...] == 2
+    scale = jnp.where(wide, 0.25, 0.5)
     span = lax.axis_index("span")
     has_before = jnp.where(span > 0, 0.5, 0.0).astype(F32)
     has_after = jnp.where(span < lax.axis_size("span") - 1, 0.5, 0.0).astype(F32)
 
-    def rounded(x):
-        return x.astype(BF16).astype(F32)
-
-    def down(x, end):
-        return jnp.where(row_id == 0, end, pltpu.roll(x, 1, 0))
-
-    def up(x, end):
-        return jnp.where(row_id == lines - 1, end, pltpu.roll(x, lines - 1, 0))
-
-    def copy_of(v):
-        return pltpu.make_async_copy(z_ref.at[:, v], z_out.at[:, v], sems.at[v])
-
-    acc_ref[...] = jnp.zeros_like(acc_ref)
+    def copies_of(v):
+        return [pltpu.make_async_copy(rim_ref.at[v], rim_out.at[v], sems.at[0, v]),
+                pltpu.make_async_copy(z_ref.at[v], z_out.at[v], sems.at[1, v])]
+
+    acc_ref[...] = inner_gram_ref[...]
 
     def one_variable(v, carry):
         unpack(before_t_ref, before_t_in, v, T_GROUPS)
@@ -209,38 +271,23 @@
                 return after_t_ref[(t - cells) * lines:(t - cells + 1) * lines, :]
             return y_ref[v, t * lines:(t + 1) * lines, :]
 
-        def turn(get, t):
-            return scale * jnp.where(wide, get(t + 2) - get(t - 2), get(t + 1) - get(t - 1))
-
-        z1 = {}
-
-        def z1_at(t):
-            if t not in z1:
-                z1[t] = rounded(turn(y_at, t))
-            return z1[t]
-
+        rim = [turn(wide, scale, y_at, t) for t in RIM_FIRST + tuple(cells + t for t in RIM_LAST)]
+        for k, slab in enumerate(rim):
+            edge_t_ref[v, k] = rounded(slab)
+        rim_ref[v] = jnp.concatenate(rim[2:6], axis=0).astype(BF16)
         for pair in range(cells // 2):
             kept = []
             for t in (2 * pair, 2 * pair + 1):
                 y = y_at(t)
-                w1 = -turn(z1_at, t)
                 one, two = slice(t, t + 1), slice(cells + t, cells + t + 1)
-                before2, before1 = before_r_ref[one, :], before_r_ref[two, :]
-                after1, after2 = after_r_ref[one, :], after_r_ref[two, :]
-                z2 = rounded(0.5 * (up(y, after1) - down(y, before1)))
-                z2_before = rounded(has_before * (y[0:1] - before2))
-                z2_after = rounded(has_after * (after2 - y[lines - 1:lines]))
-                w2 = 0.5 * (down(z2, z2_before) - up(z2, z2_after))
-                kept.append((y, z1_at(t), z2, rounded(y) + w1 + w2))
-            at = pl.ds(2 * pair * lines, 2 * lines)
-            a, b = kept
-            for family in range(3):
-                z_ref[family, v, at, :] = jnp.concatenate([a[family], b[family]], axis=0).astype(BF16)
-            w_ref[v, at, :] = jnp.concatenate([a[3], b[3]], axis=0).astype(BF16)
-        for family in range(3):
-            z = z_ref[family, v]
+                edge_r_ref[v, one, :] = rounded(has_before * (y[0:1] - before_r_ref[one, :]))
+                edge_r_ref[v, two, :] = rounded(has_after * (after_r_ref[two, :] - y[lines - 1:lines]))
+                kept.append(0.5 * (shift_up(y, after_r_ref[one, :]) - shift_down(y, before_r_ref[two, :])))
+            z_ref[v, pl.ds(2 * pair * lines, 2 * lines), :] = jnp.concatenate(kept, axis=0).astype(BF16)
+        for z in (rim_ref[v], z_ref[v]):
             acc_ref[...] += lax.dot_general(z, z, (((0,), (0,)), ((), ())), preferred_element_type=F32)
-        copy_of(v).start()
+        for copy in copies_of(v):
+            copy.start()
         return carry
 
     lax.fori_loop(0, variables, one_variable, 0)
@@ -248,19 +295,27 @@
     gram_ref[width:, :] = jnp.zeros((gram_ref.shape[0] - width, 128), F32)
     gram_ref[width:, :width - 128] = acc_ref[128:, 128:]
     for v in range(variables):
-        copy_of(v).wait()
-
-
-def stencils(y, before_t, after_t, before_r, after_r, reach, lines):
+        for copy in copies_of(v):
+            copy.wait()
+
+
+RIM_FIRST = (-2, -1, 0, 1)
+RIM_LAST = (-2, -1, 0, 1)
+
+
+def outer_stencils(y, before_t, after_t, before_r, after_r, inner_gram, reach, lines):
     variables, rows, width = y.shape
     cells = rows // lines
     return pl.pallas_call(
-        functools.partial(stencil_kernel, lines),
-        in_specs=[VMEM_SPEC] * 6,
-        out_specs=[HBM_SPEC, VMEM_SPEC, VMEM_SPEC],
+        functools.partial(outer_kernel, lines),
+        in_specs=[VMEM_SPEC] * 7,
+        out_specs=[HBM_SPEC] * 2 + [VMEM_SPEC] * 4,
         out_shape=[
-            pltpu.HBM((3, variables, rows, width), BF16),
+            pltpu.HBM((variables, 4 * lines, width), BF16),
+            pltpu.HBM((variables, rows, width), BF16),
             jax.ShapeDtypeStruct((variables, rows, width), BF16),
+            jax.ShapeDtypeStruct((variables, 8, lines, width), F32),
+            jax.ShapeDtypeStruct((variables, 2 * cells, width), F32),
             jax.ShapeDtypeStruct((width + (width - 128), 128), F32),
         ],
         scratch_shapes=[
@@ -269,12 +324,61 @@
             pltpu.VMEM((4 * lines, width), F32),
             pltpu.VMEM((2 * cells, width), F32),
             pltpu.VMEM((2 * cells, width), F32),
-            pltpu.VMEM((3, variables, rows, width), BF16),
-            pltpu.SemaphoreType.DMA((variables,)),
+            pltpu.VMEM((variables, 4 * lines, width), BF16),
+            pltpu.SemaphoreType.DMA((2, variables)),
         ],
         compiler_params=params(K2_MIB),
-        name="stencils",
-    )(reach, y, before_t, after_t, before_r, after_r)
+        name="outer_stencils",
+    )(reach, y, before_t, after_t, before_r, after_r, inner_gram)
+
+
+def transposed_kernel(lines, reach_ref, z_ref, z2_ref, edge_t_ref, edge_r_ref, w_ref):
+    _, variables, rows, width = z_ref.shape
+    cells = rows // lines
+    wide = reach_ref[...] == 2
+    scale = jnp.where(wide, 0.25, 0.5)
+
+    def one_variable(v, carry):
+        slabs = {}
+
+        def z1_at(t):
+            if t < 2:
+                return edge_t_ref[v, t + 2]
+            if t >= cells - 2:
+                return edge_t_ref[v, t - cells + 6]
+            if t not in slabs:
+                first = t - t % 2
+                both = z_ref[1, v, first * lines:(first + 2) * lines, :].astype(F32)
+                slabs[first], slabs[first + 1] = both[:lines], both[lines:]
+            return slabs[t]
+
+        for pair in range(cells // 2):
+            at = slice(2 * pair * lines, 2 * (pair + 1) * lines)
+            z0 = z_ref[0, v, at, :].astype(F32)
+            z2 = z2_ref[v, at, :].astype(F32)
+            out = []
+            for k in range(2):
+                t = 2 * pair + k
+                part = slice(k * lines, (k + 1) * lines)
+                w2 = (shift_down(z2[part], edge_r_ref[v, t:t + 1, :])
+                      - shift_up(z2[part], edge_r_ref[v, cells + t:cells + t + 1, :]))
+                out.append(z0[part] - turn(wide, scale, z1_at, t) + 0.5 * w2)
+            w_ref[v, at, :] = jnp.concatenate(out, axis=0).astype(BF16)
+        return carry
+
+    lax.fori_loop(0, variables, one_variable, 0)
+
+
+def transposed_stencils(z, z2, edge_t, edge_r, reach, lines):
+    _, variables, rows, width = z.shape
+    return pl.pallas_call(
+        functools.partial(transposed_kernel, lines),
+        in_specs=[VMEM_SPEC] * 5,
+        out_specs=VMEM_SPEC,
+        out_shape=jax.ShapeDtypeStruct((variables, rows, width), BF16),
+        compiler_params=params(16),
+        name="transposed_stencils",
+    )(reach, z, z2, edge_t, edge_r)
 
 
 def project_kernel(field_ref, w_ref, out_ref, acc_ref):
@@ -346,17 +450,33 @@
             a_ref[start + size:, :] -= update[start + size:width, :]
 
 
-def basis_kernel(scale, gram_ref, z_hbm, out_hbm, inv_ref, a_ref, high_ref, low_ref, z_ref, out_ref, z_sem, sems):
-    width = z_ref.shape[1]
+def basis_kernel(scale, gram_ref, inner_hbm, rim_hbm, last_hbm, out_hbm, inv_ref, a_ref, high_ref, low_ref,
+                 z_ref, out_ref, z_sems, sems):
+    width = z_ref.shape[2]
     blocks = sems.shape[0]
-    rows = z_ref.shape[0] // blocks
-    z_copy = pltpu.make_async_copy(z_hbm, z_ref, z_sem)
-    z_copy.start()
+    group = z_ref.shape[0] // blocks
+    rows = group * z_ref.shape[1]
+    variables, rim = rim_hbm.shape[:2]
+    cells = last_hbm.shape[1]
+    half = rim // 2
+    middle = pl.ds(half, cells - rim)
+    second = z_ref.at[pl.ds(variables, variables)]
+    pieces = [
+        (inner_hbm.at[0], z_ref.at[pl.ds(0, variables)]),
+        (inner_hbm.at[1, :, middle], second.at[:, middle]),
+        (rim_hbm.at[:, pl.ds(0, half)], second.at[:, pl.ds(0, half)]),
+        (rim_hbm.at[:, pl.ds(half, half)], second.at[:, pl.ds(cells - half, half)]),
+        (last_hbm, z_ref.at[pl.ds(2 * variables, variables)]),
+    ]
+    z_copies = [pltpu.make_async_copy(source, target, z_sems.at[k]) for k, (source, target) in enumerate(pieces)]
+    for copy in z_copies:
+        copy.start()
     inverse_factor_of(width, gram_ref, inv_ref, a_ref)
     turned = inv_ref[...].T * scale
     high_ref[...] = turned.astype(BF16)
     low_ref[...] = (turned - high_ref[...].astype(F32)).astype(BF16)
-    z_copy.wait()
+    for copy in z_copies:
+        copy.wait()
 
     def copy_of(i):
         at = pl.ds(pl.multiple_of(i * rows, rows), rows)
@@ -364,7 +484,7 @@
 
     def one_block(i, carry):
         at = pl.ds(pl.multiple_of(i * rows, rows), rows)
-        z = z_ref[at]
+        z = z_ref[pl.ds(i * group, group)].reshape(rows, width)
         out_ref[at] = (jnp.dot(z, low_ref[...], preferred_element_type=F32)
                        + jnp.dot(z, high_ref[...], preferred_element_type=F32))
         copy_of(i).start()
@@ -375,21 +495,22 @@
         copy_of(i).wait()
 
 
-def basis_of(z, gram, scale):
-    rows, width = z.shape
+def basis_of(inner, rim, last, gram, scale):
+    variables, cells, width = last.shape
+    rows = 3 * variables * cells
     return pl.pallas_call(
         functools.partial(basis_kernel, scale),
-        in_specs=[VMEM_SPEC, HBM_SPEC],
+        in_specs=[VMEM_SPEC] + [HBM_SPEC] * 3,
         out_specs=[HBM_SPEC, VMEM_SPEC],
         out_shape=[pltpu.HBM((rows, width), F32), jax.ShapeDtypeStruct((width, width), F32)],
         scratch_shapes=[pltpu.VMEM((width, 512), F32), pltpu.VMEM((width, width), BF16),
-                        pltpu.VMEM((width, width), BF16), pltpu.VMEM((rows, width), BF16),
-                        pltpu.VMEM((rows, width), F32), pltpu.SemaphoreType.DMA,
+                        pltpu.VMEM((width, width), BF16), pltpu.VMEM((3 * variables, cells, width), BF16),
+                        pltpu.VMEM((rows, width), F32), pltpu.SemaphoreType.DMA((5,)),
                         pltpu.SemaphoreType.DMA((K4_BLOCKS,))],
         compiler_params=params(K4_MIB),
         cost_estimate=pl.CostEstimate(flops=1000, bytes_accessed=1000, transcendentals=0),
         name="basis",
-    )(gram, in_hbm(z))
+    )(gram, in_hbm(inner), in_hbm(rim), in_hbm(last))
 
 
 def coefficients_kernel(scale, parts_ref, inv_ref, out_ref):
@@ -410,7 +531,7 @@
     )(parts, inv)
 
 
-def reduce_all(x, meanwhile):
+def reduce_all(x, start, finish):
     passages, layers = lax.axis_size("passage"), lax.axis_size("span")
 
     def exchange(x, axis, length, moves, meanwhile=None):
@@ -421,12 +542,14 @@
             x = x + part
         return x, meanwhile
 
+    w = start()
+    x, w = exchange(x, "passage", passages, [lambda i, k=k: (i + 2 * k) % passages for k in (1, 3, 2)], w)
+    projected = finish(w)
+    x, projected = exchange(x, "span", layers, [lambda i, k=k: i // 4 * 4 + (i + k) % 4 for k in (1, 3, 2)],
+                            projected)
+    x, _ = exchange(x, "span", layers, [lambda i, k=k: (i + 4 * k) % layers for k in (1, 3, 2)])
     x, _ = exchange(x, "passage", passages, [lambda i: i ^ 1])
-    x, meanwhile = exchange(x, "passage", passages, [lambda i, k=k: (i + 2 * k) % passages for k in (1, 3, 2)],
-                            meanwhile)
-    x, _ = exchange(x, "span", layers, [lambda i, k=k: i // 4 * 4 + (i + k) % 4 for k in (1, 3, 2)])
-    x, _ = exchange(x, "span", layers, [lambda i, k=k: (i + 4 * k) % layers for k in (1, 3, 2)])
-    return x, meanwhile
+    return x, projected
 
 
 def shards(snapshots, sketch, blade_row, row_speed, stencil_reach):
@@ -446,12 +569,14 @@
     before_t = lax.ppermute(last_t, "passage", ring_up)
     after_t = lax.ppermute(first_t, "passage", ring_down)
     reach = jnp.broadcast_to(stencil_reach[:, None], (lines, width))
-    z, w, gram = stencils(y, before_t, after_t, before_r, after_r, reach, lines)
-    projected = project(fields, w)
-    gram, projected = reduce_all(gram, projected)
+    inner, held, inner_gram = inner_stencils(y, reach, lines)
+    halos, inner_gram = lax.optimization_barrier(((before_t, after_t, before_r, after_r), inner_gram))
+    rim, last, z2, edge_t, edge_r, gram = outer_stencils(y, *halos, inner_gram, reach, lines)
+    gram, projected = reduce_all(
+        gram, lambda: transposed_stencils(held, z2, edge_t, edge_r, reach, lines), lambda w: project(fields, w))
     owned = columns // (passages * layers)
     parts = lax.all_to_all(projected.reshape(passages * layers, owned, width), ("passage", "span"), 0, 0, tiled=True)
-    basis, inv = basis_of(z.reshape(-1, width), gram, math.sqrt(row_total))
+    basis, inv = basis_of(inner, rim, last, gram, math.sqrt(row_total))
     coefficients = coefficients_of(parts, inv, 1.0 / math.sqrt(row_total))
     return basis.reshape(3 * variables, cells, lines, width), coefficients
 

time: 78.9 us -> 72.7 us (0.921)
  waiting for transfers between devices: 14.1 us -> 6.66 us
  Pallas kernels: 30.9 us -> 33 us
  starting transfers between devices: 32.8 us -> 31.9 us
    all_to_all x1, waiting for transfers between devices: 3.52 us -> 0.03 us  [shards(): lax.all_to_all(projected.reshape(passages * layers, owned, width), ('pass...]
    ppermute x1, waiting for transfers between devices: 3.75 us -> 1.01 us  [shards(): after_r = lax.ppermute(first_r, 'span', line_down)]
    pallas_call x1, Pallas kernels: 10.5 us -> 11.9 us  [basis_of(): pl.pallas_call(functools.partial(basis_kernel, scale), in_specs=[VMEM_SPE...]
    ppermute x10, waiting for transfers between devices: 6.5 us -> 5.6 us  [exchange(): lax.ppermute(x, axis, [(i, move(i)) for i in range(length)])]
    pallas_call x1 -> x3, Pallas kernels: 8.19 us -> 8.95 us  [the longest x1 3.84 us: outer_stencils(): pl.pallas_call(functools.partial(outer_kernel, lines), in_specs=[VMEM_SPE...]
  transfers between devices with their start and end apart: 15 -> 15, of which waited for: 8 -> 5; matrix products, arithmetic and copies ran while one was open for 0% -> 0% of each run, Pallas kernels for 16% -> 27%
where the time goes in v3:
time: 72.7 us; the launch traced here: 72.5 us
  Pallas kernels  33 us (45%)
  starting transfers between devices  31.9 us (44%)
  waiting for transfers between devices  6.66 us (9%)
  between operations  0.78 us (1%)
    ppermute x10, starting transfers between devices, exchange(): lax.ppermute(x, axis, [(i, move(i)) for i in range(length)])  16.4 us
    pallas_call x1, Pallas kernels, basis_of(): pl.pallas_call(functools.partial(basis_kernel, scale), in_specs=[VMEM_SPE...  11.9 us
    pallas_call x1, Pallas kernels, fields_and_sketch(): pl.pallas_call(functools.partial(fields_kernel, radial_total, lines), in_...  8.92 us
    all_to_all x1, starting transfers between devices, shards(): lax.all_to_all(projected.reshape(passages * layers, owned, width), ('pass...  8.45 us
    ppermute x10, waiting for transfers between devices, exchange(): lax.ppermute(x, axis, [(i, move(i)) for i in range(length)])  5.6 us
    pallas_call x1, Pallas kernels, outer_stencils(): pl.pallas_call(functools.partial(outer_kernel, lines), in_specs=[VMEM_SPE...  3.84 us
    ppermute x1, starting transfers between devices, shards(): before_r = lax.ppermute(last_r, 'span', line_up)  3.19 us
    pallas_call x1, Pallas kernels, inner_stencils(): pl.pallas_call(functools.partial(inner_kernel, lines), in_specs=[VMEM_SPE...  3 us
  transfers between devices with their start and end apart: 15, of which 5 were waited for; matrix products, arithmetic and copies ran while one was open for 0% of the time, Pallas kernels for 27%

profile of v3, /device:TPU:1, one launch (start us, length us, event | category | flops | bytes accessed | tf_op | source)
XLA Modules:
  0.0 72.5 jit_solution(10037741877507052198)
XLA Ops:
  0.6 8.9 %fields_sketch.1 = (bf16[5,768,1024]{2,1,0:T(8,128)(2,1)S(1)}, f32[5,768,144]{2,1,0:T(8,128)S(1)}, bf16[5,112,128]{2,1,0:T(8,128)(2,1)S(1)}, bf16[5,112,128]{2,1...) custom-call(s32[32]{0:T(128)} %blade_hbm.1, f32[2]{0:T(128)} %speed_hbm.1, ...), custom_call_target="tpu_custom_call" | custom-call | tf_op jit(solution)/shard_map/fields_sketch/pallas_call | solution.py:149
  9.6 2.6 %collective-permute-start = (bf16[5,112,128]{2,1,0:T(8,128)(2,1)S(1)}, bf16[5,112,128]{2,1,0:T(8,128)(2,1)S(1)}, u32[]{:S(2)}, u32[]{:S(2)}) collective-permute-start(bf16[5,112,128]{2,1,0:T(8,128)(2,1)S(1)} %get-tuple-element.33), channel_id=1, source_target_pairs={{0,16},{16,32},{32,48},{48,64},{64,80},{80,96},{96,112},{112,0},{1... | collective-permute-start | bytes 430088 | tf_op jit(solution)/shard_map/ppermute | solution.py:569
  12.2 0.0 collective-permute-start.1
  12.2 3.2 %collective-permute-start.2 = (bf16[5,80,128]{2,1,0:T(8,128)(2,1)S(1)}, bf16[5,80,128]{2,1,0:T(8,128)(2,1)S(1)}, u32[]{:S(2)}, u32[]{:S(2)}) collective-permute-start(bf16[5,80,128]{2,1,0:T(8,128)(2,1)S(1)} %get-tuple-element.35), channel_id=1, source_target_pairs={{0,1},{1,2},{2,3},{3,4},{4,5},{5,6},{6,7},{7,8},{8,9},{9,10},{10,1... | collective-permute-start | bytes 307208 | tf_op jit(solution)/shard_map/ppermute | solution.py:567
  15.4 1.3 %collective-permute-start.3 = (bf16[5,80,128]{2,1,0:T(8,128)(2,1)S(1)}, bf16[5,80,128]{2,1,0:T(8,128)(2,1)S(1)}, u32[]{:S(2)}, u32[]{:S(2)}) collective-permute-start(bf16[5,80,128]{2,1,0:T(8,128)(2,1)S(1)} %get-tuple-element.36), channel_id=1, source_target_pairs={{1,0},{2,1},{3,2},{4,3},{5,4},{6,5},{7,6},{8,7},{9,8},{10,9},{11,1... | collective-permute-start | bytes 307208 | tf_op jit(solution)/shard_map/ppermute | solution.py:568
  16.7 0.1 broadcast_in_dim.2.reach_ref
  16.8 3.0 %inner_stencils.1 = (bf16[2,5,768,144]{3,2,1,0:T(8,128)(2,1)}, bf16[2,5,768,144]{3,2,1,0:T(8,128)(2,1)S(1)}, f32[144,144]{1,0:T(8,128)S(1)}) custom-call(s32[24,144]{1,0:T(8,128)S(1)} %broadcast_in_dim.2.reach_ref, f32[5,768,144]{2,1,0:T(8,128)S(1)} %get-tuple-element.32.y_ref), custom_call_target="tpu_custom_call" | custom-call | flops 1006632960 | bytes 7864320 | tf_op jit(solution)/shard_map/inner_stencils/pallas_call | solution.py:227
  19.8 0.0 collective-permute-done.2.before_r_in
  19.8 1.0 %collective-permute-done.3.after_r_in = bf16[5,80,128]{2,1,0:T(8,128)(2,1)S(1)} collective-permute-done((bf16[5,80,128]{2,1,0:T(8,128)(2,1)S(1)}, bf16[5,80,128]{2,1,0:T(8,128)(2,1)S(1)}, u32[]{:S(2)}, u32[]{:S(2)}) %collective-permute-start.3) | collective-permute-done | bytes 102432 | tf_op jit(solution)/shard_map/ppermute | solution.py:568
  20.8 0.0 collective-permute-done.before_t_in
  20.8 0.0 collective-permute-done.1.after_t_in
  20.8 3.8 %outer_stencils.1 = (bf16[5,96,144]{2,1,0:T(8,128)(2,1)}, bf16[5,768,144]{2,1,0:T(8,128)(2,1)}, bf16[5,768,144]{2,1,0:T(8,128)(2,1)S(1)}, f32[5,8,24,144]{3,2,1,...) custom-call(s32[24,144]{1,0:T(8,128)S(1)} %broadcast_in_dim.2.reach_ref, ...), custom_call_target="tpu_custom_call" | custom-call | tf_op jit(solution)/shard_map/outer_stencils/pallas_call | solution.py:309
  24.6 2.5 %collective-permute-start.6 = (f32[160,128]{1,0:T(8,128)S(1)}, f32[160,128]{1,0:T(8,128)S(1)}, u32[]{:S(2)}, u32[]{:S(2)}) collective-permute-start(f32[160,128]{1,0:T(8,128)S(1)} %get-tuple-element.43), channel_id=1, source_target_pairs={{0,64},{16,80},{32,96},{48,112},{64,0},{80,16},{96,32},{112,48},{1... | collective-permute-start | bytes 245768 | tf_op jit(solution)/shard_map/ppermute | solution.py:538
  27.2 1.2 %collective-permute-start.5 = (f32[160,128]{1,0:T(8,128)S(1)}, f32[160,128]{1,0:T(8,128)S(1)}, u32[]{:S(2)}, u32[]{:S(2)}) collective-permute-start(f32[160,128]{1,0:T(8,128)S(1)} %get-tuple-element.43), channel_id=1, source_target_pairs={{0,96},{16,112},{32,0},{48,16},{64,32},{80,48},{96,64},{112,80},{1... | collective-permute-start | bytes 245768 | tf_op jit(solution)/shard_map/ppermute | solution.py:538
  28.3 0.3 collective-permute-start.4
  28.6 2.1 %transposed_stencils.1.w_ref = bf16[5,768,144]{2,1,0:T(8,128)(2,1)S(1)} custom-call(s32[24,144]{1,0:T(8,128)S(1)} %broadcast_in_dim.2.reach_ref, bf16[2,5,768,144]{3,2,1,0:T(8,128)(2,1)S(1)} %get-tuple-element.44.z_ref, bf16[5,768,144]{2,1,0:T(8,128)(2,1)S(1)} %get-tuple-element.45.z2_ref, f32[5,8,24,144]{3,2,1,0:T(8,128)S(1)} %get-tuple-element.46.edge_t_ref, ...), custom_call_target="tpu_custom_call" | custom-call | tf_op jit(solution)/shard_map/transposed_stencils/pallas_call | solution.py:374
  30.8 2.9 %collective-permute-done.4 = f32[160,128]{1,0:T(8,128)S(1)} collective-permute-done((f32[160,128]{1,0:T(8,128)S(1)}, f32[160,128]{1,0:T(8,128)S(1)}, u32[]{:S(2)}, u32[]{:S(2)}) %collective-permute-start.4) | collective-permute-done | bytes 81952 | tf_op jit(solution)/shard_map/ppermute | solution.py:538
  33.7 2.8 %collective-permute-start.9 = (f32[160,128]{1,0:T(8,128)S(1)}, f32[160,128]{1,0:T(8,128)S(1)}, u32[]{:S(2)}, u32[]{:S(2)}) collective-permute-start(f32[160,128]{1,0:T(8,128)S(1)} %add_add_fusion.2), channel_id=1, source_target_pairs={{0,2},{1,3},{2,0},{3,1},{4,6},{5,7},{6,4},{7,5},{8,10},{9,11},{10,... | collective-permute-start | bytes 245768 | tf_op jit(solution)/shard_map/ppermute | solution.py:538
  36.5 2.2 %collective-permute-start.8 = (f32[160,128]{1,0:T(8,128)S(1)}, f32[160,128]{1,0:T(8,128)S(1)}, u32[]{:S(2)}, u32[]{:S(2)}) collective-permute-start(f32[160,128]{1,0:T(8,128)S(1)} %add_add_fusion.2), channel_id=1, source_target_pairs={{0,3},{1,0},{2,1},{3,2},{4,7},{5,4},{6,5},{7,6},{8,11},{9,8},{10,9... | collective-permute-start | bytes 245768 | tf_op jit(solution)/shard_map/ppermute | solution.py:538
  38.7 0.5 collective-permute-start.7
  39.2 2.3 %project.1 = bf16[1024,144]{1,0:T(8,128)(2,1)} custom-call(bf16[5,768,1024]{2,1,0:T(8,128)(2,1)S(1)} %get-tuple-element.51.field_ref, bf16[5,768,144]{2,1,0:T(8,128)(2,1)S(1)} %transposed_stencils.1.w_ref), custom_call_target="tpu_custom_call" | custom-call | flops 2013265920 | bytes 7864320 | tf_op jit(solution)/shard_map/project/pallas_call | solution.py:394
  41.5 0.7 %collective-permute-done.8 = f32[160,128]{1,0:T(8,128)S(1)} collective-permute-done((f32[160,128]{1,0:T(8,128)S(1)}, f32[160,128]{1,0:T(8,128)S(1)}, u32[]{:S(2)}, u32[]{:S(2)}) %collective-permute-start.8) | collective-permute-done | bytes 81952 | tf_op jit(solution)/shard_map/ppermute | solution.py:538
  42.2 1.0 %collective-permute-done.7 = f32[160,128]{1,0:T(8,128)S(1)} collective-permute-done((f32[160,128]{1,0:T(8,128)S(1)}, f32[160,128]{1,0:T(8,128)S(1)}, u32[]{:S(2)}, u32[]{:S(2)}) %collective-permute-start.7) | collective-permute-done | bytes 81952 | tf_op jit(solution)/shard_map/ppermute | solution.py:538
  43.3 4.3 %collective-permute-start.12 = (f32[160,128]{1,0:T(8,128)S(1)}, f32[160,128]{1,0:T(8,128)S(1)}, u32[]{:S(2)}, u32[]{:S(2)}) collective-permute-start(f32[160,128]{1,0:T(8,128)S(1)} %add_add_fusion.1), channel_id=1, source_target_pairs={{0,8},{1,9},{2,10},{3,11},{4,12},{5,13},{6,14},{7,15},{8,0},{9,1},... | collective-permute-start | bytes 245768 | tf_op jit(solution)/shard_map/ppermute | solution.py:538
  47.5 0.6 collective-permute-start.11
  48.2 0.8 %collective-permute-start.10 = (f32[160,128]{1,0:T(8,128)S(1)}, f32[160,128]{1,0:T(8,128)S(1)}, u32[]{:S(2)}, u32[]{:S(2)}) collective-permute-start(f32[160,128]{1,0:T(8,128)S(1)} %add_add_fusion.1), channel_id=1, source_target_pairs={{0,4},{1,5},{2,6},{3,7},{4,8},{5,9},{6,10},{7,11},{8,12},{9,13},{1... | collective-permute-start | bytes 245768 | tf_op jit(solution)/shard_map/ppermute | solution.py:538
  49.0 8.4 %all-to-all-start = ((bf16[128,8,144]{2,1,0:T(8,128)(2,1)}), bf16[128,8,144]{2,1,0:T(8,128)(2,1)S(1)}, u32[]{:S(2)}, u32[]{:S(2)}) async-start(bf16[128,8,144]{2,1,0:T(8,128)(2,1)} %bitcast.3), calls=%async_computation | async-start | bytes 1048576 | tf_op jit(solution)/shard_map/all_to_all | solution.py:578
  57.5 1.1 %collective-permute-start.13 = (f32[160,128]{1,0:T(8,128)S(1)}, f32[160,128]{1,0:T(8,128)S(1)}, u32[]{:S(2)}, u32[]{:S(2)}) collective-permute-start(f32[160,128]{1,0:T(8,128)S(1)} %add_add_fusion), channel_id=1, source_target_pairs={{0,16},{16,0},{32,48},{48,32},{64,80},{80,64},{96,112},{112,96},{1... | collective-permute-start | bytes 245768 | tf_op jit(solution)/shard_map/ppermute | solution.py:538
  58.7 0.9 %collective-permute-done.13 = f32[160,128]{1,0:T(8,128)S(1)} collective-permute-done((f32[160,128]{1,0:T(8,128)S(1)}, f32[160,128]{1,0:T(8,128)S(1)}, u32[]{:S(2)}, u32[]{:S(2)}) %collective-permute-start.13) | collective-permute-done | bytes 81952 | tf_op jit(solution)/shard_map/ppermute | solution.py:538
  59.6 11.9 %basis.1 = (f32[11520,144]{1,0:T(8,128)}, f32[144,144]{1,0:T(8,128)S(1)}) custom-call(f32[160,128]{1,0:T(8,128)S(1)} %add.39.gram_ref, bf16[2,5,768,144]{3,2,1,0:T(8,128)(2,1)} %get-tuple-element.56.inner_hbm, bf16[5,96,144]{2,1,0:T(8,128)(2,1)} %get-tuple-element.57.rim_hbm, bf16[5,768,144]{2,1,0:T(8,128)(2,1)} %get-tuple-element.58.last_hbm), custom_call_target="tpu_custom_call" | custom-call | flops 1000 | bytes 1000 | tf_op jit(solution)/shard_map/basis/pallas_call | solution.py:501
  71.5 0.0 all-to-all-done.parts_ref
  71.5 1.0 %coefficients.1 = f32[8,144]{1,0:T(8,128)} custom-call(bf16[128,8,144]{2,1,0:T(8,128)(2,1)S(1)} %all-to-all-done.parts_ref, f32[144,144]{1,0:T(8,128)S(1)} %get-tuple-element.61.inv_ref), custom_call_target="tpu_custom_call" | custom-call | tf_op jit(solution)/shard_map/coefficients/pallas_call | solution.py:524
  (12 shorter events, 0.1 us)
Async XLA Ops:
  0.6 16.1 %copy-start = (s32[24]{0:T(128)S(1)}, s32[24]{0:T(128)}, u32[]{:S(2)}) copy-start(s32[24]{0:T(128)} %param.9) | copy-start | bytes 292
  9.6 11.2 %collective-permute-start = (bf16[5,112,128]{2,1,0:T(8,128)(2,1)S(1)}, bf16[5,112,128]{2,1,0:T(8,128)(2,1)S(1)}, u32[]{:S(2)}, u32[]{:S(2)}) collective-permute-start(bf16[5,112,128]{2,1,0:T(8,128)(2,1)S(1)} %get-tuple-element.33), channel_id=1, source_target_pairs={{0,16},{16,32},{32,48},{48,64},{64,80},{80,96},{96,112},{112,0},{1... | collective-permute-start | bytes 430088 | tf_op jit(solution)/shard_map/ppermute | solution.py:569
  12.2 8.6 %collective-permute-start.1 = (bf16[5,112,128]{2,1,0:T(8,128)(2,1)S(1)}, bf16[5,112,128]{2,1,0:T(8,128)(2,1)S(1)}, u32[]{:S(2)}, u32[]{:S(2)}) collective-permute-start(bf16[5,112,128]{2,1,0:T(8,128)(2,1)S(1)} %get-tuple-element.34), channel_id=1, source_target_pairs={{16,0},{32,16},{48,32},{64,48},{80,64},{96,80},{112,96},{0,112},{1... | collective-permute-start | bytes 430088 | tf_op jit(solution)/shard_map/ppermute | solution.py:570
  12.2 7.6 %collective-permute-start.2 = (bf16[5,80,128]{2,1,0:T(8,128)(2,1)S(1)}, bf16[5,80,128]{2,1,0:T(8,128)(2,1)S(1)}, u32[]{:S(2)}, u32[]{:S(2)}) collective-permute-start(bf16[5,80,128]{2,1,0:T(8,128)(2,1)S(1)} %get-tuple-element.35), channel_id=1, source_target_pairs={{0,1},{1,2},{2,3},{3,4},{4,5},{5,6},{6,7},{7,8},{8,9},{9,10},{10,1... | collective-permute-start | bytes 307208 | tf_op jit(solution)/shard_map/ppermute | solution.py:567
  15.4 5.4 %collective-permute-start.3 = (bf16[5,80,128]{2,1,0:T(8,128)(2,1)S(1)}, bf16[5,80,128]{2,1,0:T(8,128)(2,1)S(1)}, u32[]{:S(2)}, u32[]{:S(2)}) collective-permute-start(bf16[5,80,128]{2,1,0:T(8,128)(2,1)S(1)} %get-tuple-element.36), channel_id=1, source_target_pairs={{1,0},{2,1},{3,2},{4,3},{5,4},{6,5},{7,6},{8,7},{9,8},{10,9},{11,1... | collective-permute-start | bytes 307208 | tf_op jit(solution)/shard_map/ppermute | solution.py:568
  24.6 6.1 %collective-permute-start.6 = (f32[160,128]{1,0:T(8,128)S(1)}, f32[160,128]{1,0:T(8,128)S(1)}, u32[]{:S(2)}, u32[]{:S(2)}) collective-permute-start(f32[160,128]{1,0:T(8,128)S(1)} %get-tuple-element.43), channel_id=1, source_target_pairs={{0,64},{16,80},{32,96},{48,112},{64,0},{80,16},{96,32},{112,48},{1... | collective-permute-start | bytes 245768 | tf_op jit(solution)/shard_map/ppermute | solution.py:538
  27.2 3.6 %collective-permute-start.5 = (f32[160,128]{1,0:T(8,128)S(1)}, f32[160,128]{1,0:T(8,128)S(1)}, u32[]{:S(2)}, u32[]{:S(2)}) collective-permute-start(f32[160,128]{1,0:T(8,128)S(1)} %get-tuple-element.43), channel_id=1, source_target_pairs={{0,96},{16,112},{32,0},{48,16},{64,32},{80,48},{96,64},{112,80},{1... | collective-permute-start | bytes 245768 | tf_op jit(solution)/shard_map/ppermute | solution.py:538
  28.3 5.4 %collective-permute-start.4 = (f32[160,128]{1,0:T(8,128)S(1)}, f32[160,128]{1,0:T(8,128)S(1)}, u32[]{:S(2)}, u32[]{:S(2)}) collective-permute-start(f32[160,128]{1,0:T(8,128)S(1)} %get-tuple-element.43), channel_id=1, source_target_pairs={{0,32},{16,48},{32,64},{48,80},{64,96},{80,112},{96,0},{112,16},{1... | collective-permute-start | bytes 245768 | tf_op jit(solution)/shard_map/ppermute | solution.py:538
  33.7 7.8 %collective-permute-start.9 = (f32[160,128]{1,0:T(8,128)S(1)}, f32[160,128]{1,0:T(8,128)S(1)}, u32[]{:S(2)}, u32[]{:S(2)}) collective-permute-start(f32[160,128]{1,0:T(8,128)S(1)} %add_add_fusion.2), channel_id=1, source_target_pairs={{0,2},{1,3},{2,0},{3,1},{4,6},{5,7},{6,4},{7,5},{8,10},{9,11},{10,... | collective-permute-start | bytes 245768 | tf_op jit(solution)/shard_map/ppermute | solution.py:538
  36.5 5.7 %collective-permute-start.8 = (f32[160,128]{1,0:T(8,128)S(1)}, f32[160,128]{1,0:T(8,128)S(1)}, u32[]{:S(2)}, u32[]{:S(2)}) collective-permute-start(f32[160,128]{1,0:T(8,128)S(1)} %add_add_fusion.2), channel_id=1, source_target_pairs={{0,3},{1,0},{2,1},{3,2},{4,7},{5,4},{6,5},{7,6},{8,11},{9,8},{10,9... | collective-permute-start | bytes 245768 | tf_op jit(solution)/shard_map/ppermute | solution.py:538
  38.7 4.5 %collective-permute-start.7 = (f32[160,128]{1,0:T(8,128)S(1)}, f32[160,128]{1,0:T(8,128)S(1)}, u32[]{:S(2)}, u32[]{:S(2)}) collective-permute-start(f32[160,128]{1,0:T(8,128)S(1)} %add_add_fusion.2), channel_id=1, source_target_pairs={{0,1},{1,2},{2,3},{3,0},{4,5},{5,6},{6,7},{7,4},{8,9},{9,10},{10,1... | collective-permute-start | bytes 245768 | tf_op jit(solution)/shard_map/ppermute | solution.py:538
  43.3 14.2 %collective-permute-start.12 = (f32[160,128]{1,0:T(8,128)S(1)}, f32[160,128]{1,0:T(8,128)S(1)}, u32[]{:S(2)}, u32[]{:S(2)}) collective-permute-start(f32[160,128]{1,0:T(8,128)S(1)} %add_add_fusion.1), channel_id=1, source_target_pairs={{0,8},{1,9},{2,10},{3,11},{4,12},{5,13},{6,14},{7,15},{8,0},{9,1},... | collective-permute-start | bytes 245768 | tf_op jit(solution)/shard_map/ppermute | solution.py:538
  47.5 9.9 %collective-permute-start.11 = (f32[160,128]{1,0:T(8,128)S(1)}, f32[160,128]{1,0:T(8,128)S(1)}, u32[]{:S(2)}, u32[]{:S(2)}) collective-permute-start(f32[160,128]{1,0:T(8,128)S(1)} %add_add_fusion.1), channel_id=1, source_target_pairs={{0,12},{1,13},{2,14},{3,15},{4,0},{5,1},{6,2},{7,3},{8,4},{9,5},{1... | collective-permute-start | bytes 245768 | tf_op jit(solution)/shard_map/ppermute | solution.py:538
  48.2 9.3 %collective-permute-start.10 = (f32[160,128]{1,0:T(8,128)S(1)}, f32[160,128]{1,0:T(8,128)S(1)}, u32[]{:S(2)}, u32[]{:S(2)}) collective-permute-start(f32[160,128]{1,0:T(8,128)S(1)} %add_add_fusion.1), channel_id=1, source_target_pairs={{0,4},{1,5},{2,6},{3,7},{4,8},{5,9},{6,10},{7,11},{8,12},{9,13},{1... | collective-permute-start | bytes 245768 | tf_op jit(solution)/shard_map/ppermute | solution.py:538
  49.0 22.5 %all-to-all-start = ((bf16[128,8,144]{2,1,0:T(8,128)(2,1)}), bf16[128,8,144]{2,1,0:T(8,128)(2,1)S(1)}, u32[]{:S(2)}, u32[]{:S(2)}) async-start(bf16[128,8,144]{2,1,0:T(8,128)(2,1)} %bitcast.3), calls=%async_computation | async-start | bytes 1048576 | tf_op jit(solution)/shard_map/all_to_all | solution.py:578
  57.5 2.1 %collective-permute-start.13 = (f32[160,128]{1,0:T(8,128)S(1)}, f32[160,128]{1,0:T(8,128)S(1)}, u32[]{:S(2)}, u32[]{:S(2)}) collective-permute-start(f32[160,128]{1,0:T(8,128)S(1)} %add_add_fusion), channel_id=1, source_target_pairs={{0,16},{16,0},{32,48},{48,32},{64,80},{80,64},{96,112},{112,96},{1... | collective-permute-start | bytes 245768 | tf_op jit(solution)/shard_map/ppermute | solution.py:538

commit v4 on v3

--- a/solution.py
+++ b/solution.py
@@ -12,7 +12,7 @@
 BF16 = jnp.bfloat16
 MIB = 1024 * 1024
 K1_MIB = 24
-K1_CHUNKS = 8
+K1_CHUNKS = 4
 K4_BLOCKS = 5
 K2_MIB = 24
 K3_MIB = 24

time: 72.7 us -> 71.8 us (0.988)
  Pallas kernels: 33 us -> 32.1 us
    pallas_call x1, Pallas kernels: 8.92 us -> 7.99 us  [fields_and_sketch(): pl.pallas_call(functools.partial(fields_kernel, radial_total, lines), in_...]
where the time goes in v4:
time: 71.8 us; the launch traced here: 71.6 us
  Pallas kernels  32.1 us (45%)
  starting transfers between devices  31.9 us (44%)
  waiting for transfers between devices  6.66 us (9%)
  between operations  0.78 us (1%)
    ppermute x10, starting transfers between devices, exchange(): lax.ppermute(x, axis, [(i, move(i)) for i in range(length)])  16.4 us
    pallas_call x1, Pallas kernels, basis_of(): pl.pallas_call(functools.partial(basis_kernel, scale), in_specs=[VMEM_SPE...  11.9 us
    all_to_all x1, starting transfers between devices, shards(): lax.all_to_all(projected.reshape(passages * layers, owned, width), ('pass...  8.45 us
    pallas_call x1, Pallas kernels, fields_and_sketch(): pl.pallas_call(functools.partial(fields_kernel, radial_total, lines), in_...  7.99 us
    ppermute x10, waiting for transfers between devices, exchange(): lax.ppermute(x, axis, [(i, move(i)) for i in range(length)])  5.6 us
    pallas_call x1, Pallas kernels, outer_stencils(): pl.pallas_call(functools.partial(outer_kernel, lines), in_specs=[VMEM_SPE...  3.84 us
    ppermute x1, starting transfers between devices, shards(): before_r = lax.ppermute(last_r, 'span', line_up)  3.2 us
    pallas_call x1, Pallas kernels, inner_stencils(): pl.pallas_call(functools.partial(inner_kernel, lines), in_specs=[VMEM_SPE...  3 us
  transfers between devices with their start and end apart: 15, of which 5 were waited for; matrix products, arithmetic and copies ran while one was open for 0% of the time, Pallas kernels for 27%

profile of v4, /device:TPU:1, one launch (start us, length us, event | category | flops | bytes accessed | tf_op | source)
XLA Modules:
  0.0 71.6 jit_solution(14287545053261545596)
XLA Ops:
  0.6 8.0 %fields_sketch.1 = (bf16[5,768,1024]{2,1,0:T(8,128)(2,1)S(1)}, f32[5,768,144]{2,1,0:T(8,128)S(1)}, bf16[5,112,128]{2,1,0:T(8,128)(2,1)S(1)}, bf16[5,112,128]{2,1...) custom-call(s32[32]{0:T(128)} %blade_hbm.1, f32[2]{0:T(128)} %speed_hbm.1, ...), custom_call_target="tpu_custom_call" | custom-call | tf_op jit(solution)/shard_map/fields_sketch/pallas_call | solution.py:149
  8.6 2.6 %collective-permute-start = (bf16[5,112,128]{2,1,0:T(8,128)(2,1)S(1)}, bf16[5,112,128]{2,1,0:T(8,128)(2,1)S(1)}, u32[]{:S(2)}, u32[]{:S(2)}) collective-permute-start(bf16[5,112,128]{2,1,0:T(8,128)(2,1)S(1)} %get-tuple-element.33), channel_id=1, source_target_pairs={{0,16},{16,32},{32,48},{48,64},{64,80},{80,96},{96,112},{112,0},{1... | collective-permute-start | bytes 430088 | tf_op jit(solution)/shard_map/ppermute | solution.py:569
  11.3 3.2 %collective-permute-start.2 = (bf16[5,80,128]{2,1,0:T(8,128)(2,1)S(1)}, bf16[5,80,128]{2,1,0:T(8,128)(2,1)S(1)}, u32[]{:S(2)}, u32[]{:S(2)}) collective-permute-start(bf16[5,80,128]{2,1,0:T(8,128)(2,1)S(1)} %get-tuple-element.35), channel_id=1, source_target_pairs={{0,1},{1,2},{2,3},{3,4},{4,5},{5,6},{6,7},{7,8},{8,9},{9,10},{10,1... | collective-permute-start | bytes 307208 | tf_op jit(solution)/shard_map/ppermute | solution.py:567
  14.5 1.3 %collective-permute-start.3 = (bf16[5,80,128]{2,1,0:T(8,128)(2,1)S(1)}, bf16[5,80,128]{2,1,0:T(8,128)(2,1)S(1)}, u32[]{:S(2)}, u32[]{:S(2)}) collective-permute-start(bf16[5,80,128]{2,1,0:T(8,128)(2,1)S(1)} %get-tuple-element.36), channel_id=1, source_target_pairs={{1,0},{2,1},{3,2},{4,3},{5,4},{6,5},{7,6},{8,7},{9,8},{10,9},{11,1... | collective-permute-start | bytes 307208 | tf_op jit(solution)/shard_map/ppermute | solution.py:568
  15.8 0.1 broadcast_in_dim.2.reach_ref
  15.8 3.0 %inner_stencils.1 = (bf16[2,5,768,144]{3,2,1,0:T(8,128)(2,1)}, bf16[2,5,768,144]{3,2,1,0:T(8,128)(2,1)S(1)}, f32[144,144]{1,0:T(8,128)S(1)}) custom-call(s32[24,144]{1,0:T(8,128)S(1)} %broadcast_in_dim.2.reach_ref, f32[5,768,144]{2,1,0:T(8,128)S(1)} %get-tuple-element.32.y_ref), custom_call_target="tpu_custom_call" | custom-call | flops 1006632960 | bytes 7864320 | tf_op jit(solution)/shard_map/inner_stencils/pallas_call | solution.py:227
  18.8 0.0 collective-permute-done.2.before_r_in
  18.9 1.0 %collective-permute-done.3.after_r_in = bf16[5,80,128]{2,1,0:T(8,128)(2,1)S(1)} collective-permute-done((bf16[5,80,128]{2,1,0:T(8,128)(2,1)S(1)}, bf16[5,80,128]{2,1,0:T(8,128)(2,1)S(1)}, u32[]{:S(2)}, u32[]{:S(2)}) %collective-permute-start.3) | collective-permute-done | bytes 102432 | tf_op jit(solution)/shard_map/ppermute | solution.py:568
  19.9 0.0 collective-permute-done.before_t_in
  19.9 0.0 collective-permute-done.1.after_t_in
  19.9 3.8 %outer_stencils.1 = (bf16[5,96,144]{2,1,0:T(8,128)(2,1)}, bf16[5,768,144]{2,1,0:T(8,128)(2,1)}, bf16[5,768,144]{2,1,0:T(8,128)(2,1)S(1)}, f32[5,8,24,144]{3,2,1,...) custom-call(s32[24,144]{1,0:T(8,128)S(1)} %broadcast_in_dim.2.reach_ref, ...), custom_call_target="tpu_custom_call" | custom-call | tf_op jit(solution)/shard_map/outer_stencils/pallas_call | solution.py:309
  23.7 2.5 %collective-permute-start.6 = (f32[160,128]{1,0:T(8,128)S(1)}, f32[160,128]{1,0:T(8,128)S(1)}, u32[]{:S(2)}, u32[]{:S(2)}) collective-permute-start(f32[160,128]{1,0:T(8,128)S(1)} %get-tuple-element.43), channel_id=1, source_target_pairs={{0,64},{16,80},{32,96},{48,112},{64,0},{80,16},{96,32},{112,48},{1... | collective-permute-start | bytes 245768 | tf_op jit(solution)/shard_map/ppermute | solution.py:538
  26.3 1.1 %collective-permute-start.5 = (f32[160,128]{1,0:T(8,128)S(1)}, f32[160,128]{1,0:T(8,128)S(1)}, u32[]{:S(2)}, u32[]{:S(2)}) collective-permute-start(f32[160,128]{1,0:T(8,128)S(1)} %get-tuple-element.43), channel_id=1, source_target_pairs={{0,96},{16,112},{32,0},{48,16},{64,32},{80,48},{96,64},{112,80},{1... | collective-permute-start | bytes 245768 | tf_op jit(solution)/shard_map/ppermute | solution.py:538
  27.4 0.3 collective-permute-start.4
  27.7 2.1 %transposed_stencils.1.w_ref = bf16[5,768,144]{2,1,0:T(8,128)(2,1)S(1)} custom-call(s32[24,144]{1,0:T(8,128)S(1)} %broadcast_in_dim.2.reach_ref, bf16[2,5,768,144]{3,2,1,0:T(8,128)(2,1)S(1)} %get-tuple-element.44.z_ref, bf16[5,768,144]{2,1,0:T(8,128)(2,1)S(1)} %get-tuple-element.45.z2_ref, f32[5,8,24,144]{3,2,1,0:T(8,128)S(1)} %get-tuple-element.46.edge_t_ref, ...), custom_call_target="tpu_custom_call" | custom-call | tf_op jit(solution)/shard_map/transposed_stencils/pallas_call | solution.py:374
  29.9 0.0 collective-permute-done.5
  29.9 2.9 %collective-permute-done.4 = f32[160,128]{1,0:T(8,128)S(1)} collective-permute-done((f32[160,128]{1,0:T(8,128)S(1)}, f32[160,128]{1,0:T(8,128)S(1)}, u32[]{:S(2)}, u32[]{:S(2)}) %collective-permute-start.4) | collective-permute-done | bytes 81952 | tf_op jit(solution)/shard_map/ppermute | solution.py:538
  32.8 2.8 %collective-permute-start.9 = (f32[160,128]{1,0:T(8,128)S(1)}, f32[160,128]{1,0:T(8,128)S(1)}, u32[]{:S(2)}, u32[]{:S(2)}) collective-permute-start(f32[160,128]{1,0:T(8,128)S(1)} %add_add_fusion.2), channel_id=1, source_target_pairs={{0,2},{1,3},{2,0},{3,1},{4,6},{5,7},{6,4},{7,5},{8,10},{9,11},{10,... | collective-permute-start | bytes 245768 | tf_op jit(solution)/shard_map/ppermute | solution.py:538
  35.6 2.2 %collective-permute-start.8 = (f32[160,128]{1,0:T(8,128)S(1)}, f32[160,128]{1,0:T(8,128)S(1)}, u32[]{:S(2)}, u32[]{:S(2)}) collective-permute-start(f32[160,128]{1,0:T(8,128)S(1)} %add_add_fusion.2), channel_id=1, source_target_pairs={{0,3},{1,0},{2,1},{3,2},{4,7},{5,4},{6,5},{7,6},{8,11},{9,8},{10,9... | collective-permute-start | bytes 245768 | tf_op jit(solution)/shard_map/ppermute | solution.py:538
  37.8 0.5 collective-permute-start.7
  38.3 2.3 %project.1 = bf16[1024,144]{1,0:T(8,128)(2,1)} custom-call(bf16[5,768,1024]{2,1,0:T(8,128)(2,1)S(1)} %get-tuple-element.51.field_ref, bf16[5,768,144]{2,1,0:T(8,128)(2,1)S(1)} %transposed_stencils.1.w_ref), custom_call_target="tpu_custom_call" | custom-call | flops 2013265920 | bytes 7864320 | tf_op jit(solution)/shard_map/project/pallas_call | solution.py:394
  40.6 0.7 %collective-permute-done.8 = f32[160,128]{1,0:T(8,128)S(1)} collective-permute-done((f32[160,128]{1,0:T(8,128)S(1)}, f32[160,128]{1,0:T(8,128)S(1)}, u32[]{:S(2)}, u32[]{:S(2)}) %collective-permute-start.8) | collective-permute-done | bytes 81952 | tf_op jit(solution)/shard_map/ppermute | solution.py:538
  41.3 1.0 %collective-permute-done.7 = f32[160,128]{1,0:T(8,128)S(1)} collective-permute-done((f32[160,128]{1,0:T(8,128)S(1)}, f32[160,128]{1,0:T(8,128)S(1)}, u32[]{:S(2)}, u32[]{:S(2)}) %collective-permute-start.7) | collective-permute-done | bytes 81952 | tf_op jit(solution)/shard_map/ppermute | solution.py:538
  42.3 4.3 %collective-permute-start.12 = (f32[160,128]{1,0:T(8,128)S(1)}, f32[160,128]{1,0:T(8,128)S(1)}, u32[]{:S(2)}, u32[]{:S(2)}) collective-permute-start(f32[160,128]{1,0:T(8,128)S(1)} %add_add_fusion.1), channel_id=1, source_target_pairs={{0,8},{1,9},{2,10},{3,11},{4,12},{5,13},{6,14},{7,15},{8,0},{9,1},... | collective-permute-start | bytes 245768 | tf_op jit(solution)/shard_map/ppermute | solution.py:538
  46.6 0.6 collective-permute-start.11
  47.2 0.8 %collective-permute-start.10 = (f32[160,128]{1,0:T(8,128)S(1)}, f32[160,128]{1,0:T(8,128)S(1)}, u32[]{:S(2)}, u32[]{:S(2)}) collective-permute-start(f32[160,128]{1,0:T(8,128)S(1)} %add_add_fusion.1), channel_id=1, source_target_pairs={{0,4},{1,5},{2,6},{3,7},{4,8},{5,9},{6,10},{7,11},{8,12},{9,13},{1... | collective-permute-start | bytes 245768 | tf_op jit(solution)/shard_map/ppermute | solution.py:538
  48.1 8.5 %all-to-all-start = ((bf16[128,8,144]{2,1,0:T(8,128)(2,1)}), bf16[128,8,144]{2,1,0:T(8,128)(2,1)S(1)}, u32[]{:S(2)}, u32[]{:S(2)}) async-start(bf16[128,8,144]{2,1,0:T(8,128)(2,1)} %bitcast.3), calls=%async_computation | async-start | bytes 1048576 | tf_op jit(solution)/shard_map/all_to_all | solution.py:578
  56.6 1.1 %collective-permute-start.13 = (f32[160,128]{1,0:T(8,128)S(1)}, f32[160,128]{1,0:T(8,128)S(1)}, u32[]{:S(2)}, u32[]{:S(2)}) collective-permute-start(f32[160,128]{1,0:T(8,128)S(1)} %add_add_fusion), channel_id=1, source_target_pairs={{0,16},{16,0},{32,48},{48,32},{64,80},{80,64},{96,112},{112,96},{1... | collective-permute-start | bytes 245768 | tf_op jit(solution)/shard_map/ppermute | solution.py:538
  57.7 0.9 %collective-permute-done.13 = f32[160,128]{1,0:T(8,128)S(1)} collective-permute-done((f32[160,128]{1,0:T(8,128)S(1)}, f32[160,128]{1,0:T(8,128)S(1)}, u32[]{:S(2)}, u32[]{:S(2)}) %collective-permute-start.13) | collective-permute-done | bytes 81952 | tf_op jit(solution)/shard_map/ppermute | solution.py:538
  58.7 11.9 %basis.1 = (f32[11520,144]{1,0:T(8,128)}, f32[144,144]{1,0:T(8,128)S(1)}) custom-call(f32[160,128]{1,0:T(8,128)S(1)} %add.39.gram_ref, bf16[2,5,768,144]{3,2,1,0:T(8,128)(2,1)} %get-tuple-element.56.inner_hbm, bf16[5,96,144]{2,1,0:T(8,128)(2,1)} %get-tuple-element.57.rim_hbm, bf16[5,768,144]{2,1,0:T(8,128)(2,1)} %get-tuple-element.58.last_hbm), custom_call_target="tpu_custom_call" | custom-call | flops 1000 | bytes 1000 | tf_op jit(solution)/shard_map/basis/pallas_call | solution.py:501
  70.6 0.0 all-to-all-done.parts_ref
  70.6 1.0 %coefficients.1 = f32[8,144]{1,0:T(8,128)} custom-call(bf16[128,8,144]{2,1,0:T(8,128)(2,1)S(1)} %all-to-all-done.parts_ref, f32[144,144]{1,0:T(8,128)S(1)} %get-tuple-element.61.inv_ref), custom_call_target="tpu_custom_call" | custom-call | tf_op jit(solution)/shard_map/coefficients/pallas_call | solution.py:524
  (12 shorter events, 0.1 us)
Async XLA Ops:
  0.6 15.1 %copy-start = (s32[24]{0:T(128)S(1)}, s32[24]{0:T(128)}, u32[]{:S(2)}) copy-start(s32[24]{0:T(128)} %param.9) | copy-start | bytes 292
  8.6 11.2 %collective-permute-start = (bf16[5,112,128]{2,1,0:T(8,128)(2,1)S(1)}, bf16[5,112,128]{2,1,0:T(8,128)(2,1)S(1)}, u32[]{:S(2)}, u32[]{:S(2)}) collective-permute-start(bf16[5,112,128]{2,1,0:T(8,128)(2,1)S(1)} %get-tuple-element.33), channel_id=1, source_target_pairs={{0,16},{16,32},{32,48},{48,64},{64,80},{80,96},{96,112},{112,0},{1... | collective-permute-start | bytes 430088 | tf_op jit(solution)/shard_map/ppermute | solution.py:569
  11.3 8.6 %collective-permute-start.1 = (bf16[5,112,128]{2,1,0:T(8,128)(2,1)S(1)}, bf16[5,112,128]{2,1,0:T(8,128)(2,1)S(1)}, u32[]{:S(2)}, u32[]{:S(2)}) collective-permute-start(bf16[5,112,128]{2,1,0:T(8,128)(2,1)S(1)} %get-tuple-element.34), channel_id=1, source_target_pairs={{16,0},{32,16},{48,32},{64,48},{80,64},{96,80},{112,96},{0,112},{1... | collective-permute-start | bytes 430088 | tf_op jit(solution)/shard_map/ppermute | solution.py:570
  11.3 7.6 %collective-permute-start.2 = (bf16[5,80,128]{2,1,0:T(8,128)(2,1)S(1)}, bf16[5,80,128]{2,1,0:T(8,128)(2,1)S(1)}, u32[]{:S(2)}, u32[]{:S(2)}) collective-permute-start(bf16[5,80,128]{2,1,0:T(8,128)(2,1)S(1)} %get-tuple-element.35), channel_id=1, source_target_pairs={{0,1},{1,2},{2,3},{3,4},{4,5},{5,6},{6,7},{7,8},{8,9},{9,10},{10,1... | collective-permute-start | bytes 307208 | tf_op jit(solution)/shard_map/ppermute | solution.py:567
  14.5 5.4 %collective-permute-start.3 = (bf16[5,80,128]{2,1,0:T(8,128)(2,1)S(1)}, bf16[5,80,128]{2,1,0:T(8,128)(2,1)S(1)}, u32[]{:S(2)}, u32[]{:S(2)}) collective-permute-start(bf16[5,80,128]{2,1,0:T(8,128)(2,1)S(1)} %get-tuple-element.36), channel_id=1, source_target_pairs={{1,0},{2,1},{3,2},{4,3},{5,4},{6,5},{7,6},{8,7},{9,8},{10,9},{11,1... | collective-permute-start | bytes 307208 | tf_op jit(solution)/shard_map/ppermute | solution.py:568
  23.7 6.1 %collective-permute-start.6 = (f32[160,128]{1,0:T(8,128)S(1)}, f32[160,128]{1,0:T(8,128)S(1)}, u32[]{:S(2)}, u32[]{:S(2)}) collective-permute-start(f32[160,128]{1,0:T(8,128)S(1)} %get-tuple-element.43), channel_id=1, source_target_pairs={{0,64},{16,80},{32,96},{48,112},{64,0},{80,16},{96,32},{112,48},{1... | collective-permute-start | bytes 245768 | tf_op jit(solution)/shard_map/ppermute | solution.py:538
  26.3 3.6 %collective-permute-start.5 = (f32[160,128]{1,0:T(8,128)S(1)}, f32[160,128]{1,0:T(8,128)S(1)}, u32[]{:S(2)}, u32[]{:S(2)}) collective-permute-start(f32[160,128]{1,0:T(8,128)S(1)} %get-tuple-element.43), channel_id=1, source_target_pairs={{0,96},{16,112},{32,0},{48,16},{64,32},{80,48},{96,64},{112,80},{1... | collective-permute-start | bytes 245768 | tf_op jit(solution)/shard_map/ppermute | solution.py:538
  27.4 5.4 %collective-permute-start.4 = (f32[160,128]{1,0:T(8,128)S(1)}, f32[160,128]{1,0:T(8,128)S(1)}, u32[]{:S(2)}, u32[]{:S(2)}) collective-permute-start(f32[160,128]{1,0:T(8,128)S(1)} %get-tuple-element.43), channel_id=1, source_target_pairs={{0,32},{16,48},{32,64},{48,80},{64,96},{80,112},{96,0},{112,16},{1... | collective-permute-start | bytes 245768 | tf_op jit(solution)/shard_map/ppermute | solution.py:538
  32.8 7.8 %collective-permute-start.9 = (f32[160,128]{1,0:T(8,128)S(1)}, f32[160,128]{1,0:T(8,128)S(1)}, u32[]{:S(2)}, u32[]{:S(2)}) collective-permute-start(f32[160,128]{1,0:T(8,128)S(1)} %add_add_fusion.2), channel_id=1, source_target_pairs={{0,2},{1,3},{2,0},{3,1},{4,6},{5,7},{6,4},{7,5},{8,10},{9,11},{10,... | collective-permute-start | bytes 245768 | tf_op jit(solution)/shard_map/ppermute | solution.py:538
  35.6 5.7 %collective-permute-start.8 = (f32[160,128]{1,0:T(8,128)S(1)}, f32[160,128]{1,0:T(8,128)S(1)}, u32[]{:S(2)}, u32[]{:S(2)}) collective-permute-start(f32[160,128]{1,0:T(8,128)S(1)} %add_add_fusion.2), channel_id=1, source_target_pairs={{0,3},{1,0},{2,1},{3,2},{4,7},{5,4},{6,5},{7,6},{8,11},{9,8},{10,9... | collective-permute-start | bytes 245768 | tf_op jit(solution)/shard_map/ppermute | solution.py:538
  37.8 4.5 %collective-permute-start.7 = (f32[160,128]{1,0:T(8,128)S(1)}, f32[160,128]{1,0:T(8,128)S(1)}, u32[]{:S(2)}, u32[]{:S(2)}) collective-permute-start(f32[160,128]{1,0:T(8,128)S(1)} %add_add_fusion.2), channel_id=1, source_target_pairs={{0,1},{1,2},{2,3},{3,0},{4,5},{5,6},{6,7},{7,4},{8,9},{9,10},{10,1... | collective-permute-start | bytes 245768 | tf_op jit(solution)/shard_map/ppermute | solution.py:538
  42.3 14.2 %collective-permute-start.12 = (f32[160,128]{1,0:T(8,128)S(1)}, f32[160,128]{1,0:T(8,128)S(1)}, u32[]{:S(2)}, u32[]{:S(2)}) collective-permute-start(f32[160,128]{1,0:T(8,128)S(1)} %add_add_fusion.1), channel_id=1, source_target_pairs={{0,8},{1,9},{2,10},{3,11},{4,12},{5,13},{6,14},{7,15},{8,0},{9,1},... | collective-permute-start | bytes 245768 | tf_op jit(solution)/shard_map/ppermute | solution.py:538
  46.6 9.9 %collective-permute-start.11 = (f32[160,128]{1,0:T(8,128)S(1)}, f32[160,128]{1,0:T(8,128)S(1)}, u32[]{:S(2)}, u32[]{:S(2)}) collective-permute-start(f32[160,128]{1,0:T(8,128)S(1)} %add_add_fusion.1), channel_id=1, source_target_pairs={{0,12},{1,13},{2,14},{3,15},{4,0},{5,1},{6,2},{7,3},{8,4},{9,5},{1... | collective-permute-start | bytes 245768 | tf_op jit(solution)/shard_map/ppermute | solution.py:538
  47.2 9.3 %collective-permute-start.10 = (f32[160,128]{1,0:T(8,128)S(1)}, f32[160,128]{1,0:T(8,128)S(1)}, u32[]{:S(2)}, u32[]{:S(2)}) collective-permute-start(f32[160,128]{1,0:T(8,128)S(1)} %add_add_fusion.1), channel_id=1, source_target_pairs={{0,4},{1,5},{2,6},{3,7},{4,8},{5,9},{6,10},{7,11},{8,12},{9,13},{1... | collective-permute-start | bytes 245768 | tf_op jit(solution)/shard_map/ppermute | solution.py:538
  48.1 22.5 %all-to-all-start = ((bf16[128,8,144]{2,1,0:T(8,128)(2,1)}), bf16[128,8,144]{2,1,0:T(8,128)(2,1)S(1)}, u32[]{:S(2)}, u32[]{:S(2)}) async-start(bf16[128,8,144]{2,1,0:T(8,128)(2,1)} %bitcast.3), calls=%async_computation | async-start | bytes 1048576 | tf_op jit(solution)/shard_map/all_to_all | solution.py:578
  56.6 2.1 %collective-permute-start.13 = (f32[160,128]{1,0:T(8,128)S(1)}, f32[160,128]{1,0:T(8,128)S(1)}, u32[]{:S(2)}, u32[]{:S(2)}) collective-permute-start(f32[160,128]{1,0:T(8,128)S(1)} %add_add_fusion), channel_id=1, source_target_pairs={{0,16},{16,0},{32,48},{48,32},{64,80},{80,64},{96,112},{112,96},{1... | collective-permute-start | bytes 245768 | tf_op jit(solution)/shard_map/ppermute | solution.py:538

commit v5 on v4

--- a/solution.py
+++ b/solution.py
@@ -210,10 +210,10 @@
             if 0 < pair < cells // 2 - 1:
                 z1 = [turn(wide, scale, y_at, t) for t in (2 * pair, 2 * pair + 1)]
                 z_ref[1, v, at, :] = jnp.concatenate(z1, axis=0).astype(BF16)
+        for copy in copies_of(v):
+            copy.start()
         for z in (z_ref[0, v], z_ref[1, v, inner]):
             gram_ref[...] += lax.dot_general(z, z, (((0,), (0,)), ((), ())), preferred_element_type=F32)
-        for copy in copies_of(v):
-            copy.start()
         return carry
 
     lax.fori_loop(0, variables, one_variable, 0)
@@ -284,10 +284,10 @@
                 edge_r_ref[v, two, :] = rounded(has_after * (after_r_ref[two, :] - y[lines - 1:lines]))
                 kept.append(0.5 * (shift_up(y, after_r_ref[one, :]) - shift_down(y, before_r_ref[two, :])))
             z_ref[v, pl.ds(2 * pair * lines, 2 * lines), :] = jnp.concatenate(kept, axis=0).astype(BF16)
+        for copy in copies_of(v):
+            copy.start()
         for z in (rim_ref[v], z_ref[v]):
             acc_ref[...] += lax.dot_general(z, z, (((0,), (0,)), ((), ())), preferred_element_type=F32)
-        for copy in copies_of(v):
-            copy.start()
         return carry
 
     lax.fori_loop(0, variables, one_variable, 0)

time: 71.8 us -> 71.8 us (level)
  no operation moved by 1% of the time
where the time goes in v5:
time: 71.8 us; the launch traced here: 71.6 us
  Pallas kernels  32.1 us (45%)
  starting transfers between devices  31.9 us (44%)
  waiting for transfers between devices  6.66 us (9%)
  between operations  0.78 us (1%)
    ppermute x10, starting transfers between devices, exchange(): lax.ppermute(x, axis, [(i, move(i)) for i in range(length)])  16.4 us
    pallas_call x1, Pallas kernels, basis_of(): pl.pallas_call(functools.partial(basis_kernel, scale), in_specs=[VMEM_SPE...  11.9 us
    all_to_all x1, starting transfers between devices, shards(): lax.all_to_all(projected.reshape(passages * layers, owned, width), ('pass...  8.45 us
    pallas_call x1, Pallas kernels, fields_and_sketch(): pl.pallas_call(functools.partial(fields_kernel, radial_total, lines), in_...  7.99 us
    ppermute x10, waiting for transfers between devices, exchange(): lax.ppermute(x, axis, [(i, move(i)) for i in range(length)])  5.6 us
    pallas_call x1, Pallas kernels, outer_stencils(): pl.pallas_call(functools.partial(outer_kernel, lines), in_specs=[VMEM_SPE...  3.84 us
    ppermute x1, starting transfers between devices, shards(): before_r = lax.ppermute(last_r, 'span', line_up)  3.2 us
    pallas_call x1, Pallas kernels, inner_stencils(): pl.pallas_call(functools.partial(inner_kernel, lines), in_specs=[VMEM_SPE...  3 us
  transfers between devices with their start and end apart: 15, of which 5 were waited for; matrix products, arithmetic and copies ran while one was open for 0% of the time, Pallas kernels for 27%

profile of v5, /device:TPU:1, one launch (start us, length us, event | category | flops | bytes accessed | tf_op | source)
XLA Modules:
  0.0 71.6 jit_solution(14287545053261545596)
XLA Ops:
  0.6 8.0 %fields_sketch.1 = (bf16[5,768,1024]{2,1,0:T(8,128)(2,1)S(1)}, f32[5,768,144]{2,1,0:T(8,128)S(1)}, bf16[5,112,128]{2,1,0:T(8,128)(2,1)S(1)}, bf16[5,112,128]{2,1...) custom-call(s32[32]{0:T(128)} %blade_hbm.1, f32[2]{0:T(128)} %speed_hbm.1, ...), custom_call_target="tpu_custom_call" | custom-call | tf_op jit(solution)/shard_map/fields_sketch/pallas_call | solution.py:149
  8.6 2.6 %collective-permute-start = (bf16[5,112,128]{2,1,0:T(8,128)(2,1)S(1)}, bf16[5,112,128]{2,1,0:T(8,128)(2,1)S(1)}, u32[]{:S(2)}, u32[]{:S(2)}) collective-permute-start(bf16[5,112,128]{2,1,0:T(8,128)(2,1)S(1)} %get-tuple-element.33), channel_id=1, source_target_pairs={{0,16},{16,32},{32,48},{48,64},{64,80},{80,96},{96,112},{112,0},{1... | collective-permute-start | bytes 430088 | tf_op jit(solution)/shard_map/ppermute | solution.py:569
  11.3 3.2 %collective-permute-start.2 = (bf16[5,80,128]{2,1,0:T(8,128)(2,1)S(1)}, bf16[5,80,128]{2,1,0:T(8,128)(2,1)S(1)}, u32[]{:S(2)}, u32[]{:S(2)}) collective-permute-start(bf16[5,80,128]{2,1,0:T(8,128)(2,1)S(1)} %get-tuple-element.35), channel_id=1, source_target_pairs={{0,1},{1,2},{2,3},{3,4},{4,5},{5,6},{6,7},{7,8},{8,9},{9,10},{10,1... | collective-permute-start | bytes 307208 | tf_op jit(solution)/shard_map/ppermute | solution.py:567
  14.5 1.3 %collective-permute-start.3 = (bf16[5,80,128]{2,1,0:T(8,128)(2,1)S(1)}, bf16[5,80,128]{2,1,0:T(8,128)(2,1)S(1)}, u32[]{:S(2)}, u32[]{:S(2)}) collective-permute-start(bf16[5,80,128]{2,1,0:T(8,128)(2,1)S(1)} %get-tuple-element.36), channel_id=1, source_target_pairs={{1,0},{2,1},{3,2},{4,3},{5,4},{6,5},{7,6},{8,7},{9,8},{10,9},{11,1... | collective-permute-start | bytes 307208 | tf_op jit(solution)/shard_map/ppermute | solution.py:568
  15.8 0.1 broadcast_in_dim.2.reach_ref
  15.8 3.0 %inner_stencils.1 = (bf16[2,5,768,144]{3,2,1,0:T(8,128)(2,1)}, bf16[2,5,768,144]{3,2,1,0:T(8,128)(2,1)S(1)}, f32[144,144]{1,0:T(8,128)S(1)}) custom-call(s32[24,144]{1,0:T(8,128)S(1)} %broadcast_in_dim.2.reach_ref, f32[5,768,144]{2,1,0:T(8,128)S(1)} %get-tuple-element.32.y_ref), custom_call_target="tpu_custom_call" | custom-call | flops 1006632960 | bytes 7864320 | tf_op jit(solution)/shard_map/inner_stencils/pallas_call | solution.py:227
  18.8 0.0 collective-permute-done.2.before_r_in
  18.9 1.0 %collective-permute-done.3.after_r_in = bf16[5,80,128]{2,1,0:T(8,128)(2,1)S(1)} collective-permute-done((bf16[5,80,128]{2,1,0:T(8,128)(2,1)S(1)}, bf16[5,80,128]{2,1,0:T(8,128)(2,1)S(1)}, u32[]{:S(2)}, u32[]{:S(2)}) %collective-permute-start.3) | collective-permute-done | bytes 102432 | tf_op jit(solution)/shard_map/ppermute | solution.py:568
  19.9 0.0 collective-permute-done.before_t_in
  19.9 0.0 collective-permute-done.1.after_t_in
  19.9 3.8 %outer_stencils.1 = (bf16[5,96,144]{2,1,0:T(8,128)(2,1)}, bf16[5,768,144]{2,1,0:T(8,128)(2,1)}, bf16[5,768,144]{2,1,0:T(8,128)(2,1)S(1)}, f32[5,8,24,144]{3,2,1,...) custom-call(s32[24,144]{1,0:T(8,128)S(1)} %broadcast_in_dim.2.reach_ref, ...), custom_call_target="tpu_custom_call" | custom-call | tf_op jit(solution)/shard_map/outer_stencils/pallas_call | solution.py:309
  23.7 2.5 %collective-permute-start.6 = (f32[160,128]{1,0:T(8,128)S(1)}, f32[160,128]{1,0:T(8,128)S(1)}, u32[]{:S(2)}, u32[]{:S(2)}) collective-permute-start(f32[160,128]{1,0:T(8,128)S(1)} %get-tuple-element.43), channel_id=1, source_target_pairs={{0,64},{16,80},{32,96},{48,112},{64,0},{80,16},{96,32},{112,48},{1... | collective-permute-start | bytes 245768 | tf_op jit(solution)/shard_map/ppermute | solution.py:538
  26.3 1.1 %collective-permute-start.5 = (f32[160,128]{1,0:T(8,128)S(1)}, f32[160,128]{1,0:T(8,128)S(1)}, u32[]{:S(2)}, u32[]{:S(2)}) collective-permute-start(f32[160,128]{1,0:T(8,128)S(1)} %get-tuple-element.43), channel_id=1, source_target_pairs={{0,96},{16,112},{32,0},{48,16},{64,32},{80,48},{96,64},{112,80},{1... | collective-permute-start | bytes 245768 | tf_op jit(solution)/shard_map/ppermute | solution.py:538
  27.4 0.3 collective-permute-start.4
  27.7 2.1 %transposed_stencils.1.w_ref = bf16[5,768,144]{2,1,0:T(8,128)(2,1)S(1)} custom-call(s32[24,144]{1,0:T(8,128)S(1)} %broadcast_in_dim.2.reach_ref, bf16[2,5,768,144]{3,2,1,0:T(8,128)(2,1)S(1)} %get-tuple-element.44.z_ref, bf16[5,768,144]{2,1,0:T(8,128)(2,1)S(1)} %get-tuple-element.45.z2_ref, f32[5,8,24,144]{3,2,1,0:T(8,128)S(1)} %get-tuple-element.46.edge_t_ref, ...), custom_call_target="tpu_custom_call" | custom-call | tf_op jit(solution)/shard_map/transposed_stencils/pallas_call | solution.py:374
  29.9 0.0 collective-permute-done.5
  29.9 2.9 %collective-permute-done.4 = f32[160,128]{1,0:T(8,128)S(1)} collective-permute-done((f32[160,128]{1,0:T(8,128)S(1)}, f32[160,128]{1,0:T(8,128)S(1)}, u32[]{:S(2)}, u32[]{:S(2)}) %collective-permute-start.4) | collective-permute-done | bytes 81952 | tf_op jit(solution)/shard_map/ppermute | solution.py:538
  32.8 2.8 %collective-permute-start.9 = (f32[160,128]{1,0:T(8,128)S(1)}, f32[160,128]{1,0:T(8,128)S(1)}, u32[]{:S(2)}, u32[]{:S(2)}) collective-permute-start(f32[160,128]{1,0:T(8,128)S(1)} %add_add_fusion.2), channel_id=1, source_target_pairs={{0,2},{1,3},{2,0},{3,1},{4,6},{5,7},{6,4},{7,5},{8,10},{9,11},{10,... | collective-permute-start | bytes 245768 | tf_op jit(solution)/shard_map/ppermute | solution.py:538
  35.6 2.2 %collective-permute-start.8 = (f32[160,128]{1,0:T(8,128)S(1)}, f32[160,128]{1,0:T(8,128)S(1)}, u32[]{:S(2)}, u32[]{:S(2)}) collective-permute-start(f32[160,128]{1,0:T(8,128)S(1)} %add_add_fusion.2), channel_id=1, source_target_pairs={{0,3},{1,0},{2,1},{3,2},{4,7},{5,4},{6,5},{7,6},{8,11},{9,8},{10,9... | collective-permute-start | bytes 245768 | tf_op jit(solution)/shard_map/ppermute | solution.py:538
  37.8 0.5 collective-permute-start.7
  38.3 2.3 %project.1 = bf16[1024,144]{1,0:T(8,128)(2,1)} custom-call(bf16[5,768,1024]{2,1,0:T(8,128)(2,1)S(1)} %get-tuple-element.51.field_ref, bf16[5,768,144]{2,1,0:T(8,128)(2,1)S(1)} %transposed_stencils.1.w_ref), custom_call_target="tpu_custom_call" | custom-call | flops 2013265920 | bytes 7864320 | tf_op jit(solution)/shard_map/project/pallas_call | solution.py:394
  40.6 0.7 %collective-permute-done.8 = f32[160,128]{1,0:T(8,128)S(1)} collective-permute-done((f32[160,128]{1,0:T(8,128)S(1)}, f32[160,128]{1,0:T(8,128)S(1)}, u32[]{:S(2)}, u32[]{:S(2)}) %collective-permute-start.8) | collective-permute-done | bytes 81952 | tf_op jit(solution)/shard_map/ppermute | solution.py:538
  41.3 1.0 %collective-permute-done.7 = f32[160,128]{1,0:T(8,128)S(1)} collective-permute-done((f32[160,128]{1,0:T(8,128)S(1)}, f32[160,128]{1,0:T(8,128)S(1)}, u32[]{:S(2)}, u32[]{:S(2)}) %collective-permute-start.7) | collective-permute-done | bytes 81952 | tf_op jit(solution)/shard_map/ppermute | solution.py:538
  42.3 4.3 %collective-permute-start.12 = (f32[160,128]{1,0:T(8,128)S(1)}, f32[160,128]{1,0:T(8,128)S(1)}, u32[]{:S(2)}, u32[]{:S(2)}) collective-permute-start(f32[160,128]{1,0:T(8,128)S(1)} %add_add_fusion.1), channel_id=1, source_target_pairs={{0,8},{1,9},{2,10},{3,11},{4,12},{5,13},{6,14},{7,15},{8,0},{9,1},... | collective-permute-start | bytes 245768 | tf_op jit(solution)/shard_map/ppermute | solution.py:538
  46.6 0.6 collective-permute-start.11
  47.2 0.8 %collective-permute-start.10 = (f32[160,128]{1,0:T(8,128)S(1)}, f32[160,128]{1,0:T(8,128)S(1)}, u32[]{:S(2)}, u32[]{:S(2)}) collective-permute-start(f32[160,128]{1,0:T(8,128)S(1)} %add_add_fusion.1), channel_id=1, source_target_pairs={{0,4},{1,5},{2,6},{3,7},{4,8},{5,9},{6,10},{7,11},{8,12},{9,13},{1... | collective-permute-start | bytes 245768 | tf_op jit(solution)/shard_map/ppermute | solution.py:538
  48.1 8.5 %all-to-all-start = ((bf16[128,8,144]{2,1,0:T(8,128)(2,1)}), bf16[128,8,144]{2,1,0:T(8,128)(2,1)S(1)}, u32[]{:S(2)}, u32[]{:S(2)}) async-start(bf16[128,8,144]{2,1,0:T(8,128)(2,1)} %bitcast.3), calls=%async_computation | async-start | bytes 1048576 | tf_op jit(solution)/shard_map/all_to_all | solution.py:578
  56.6 1.1 %collective-permute-start.13 = (f32[160,128]{1,0:T(8,128)S(1)}, f32[160,128]{1,0:T(8,128)S(1)}, u32[]{:S(2)}, u32[]{:S(2)}) collective-permute-start(f32[160,128]{1,0:T(8,128)S(1)} %add_add_fusion), channel_id=1, source_target_pairs={{0,16},{16,0},{32,48},{48,32},{64,80},{80,64},{96,112},{112,96},{1... | collective-permute-start | bytes 245768 | tf_op jit(solution)/shard_map/ppermute | solution.py:538
  57.7 0.9 %collective-permute-done.13 = f32[160,128]{1,0:T(8,128)S(1)} collective-permute-done((f32[160,128]{1,0:T(8,128)S(1)}, f32[160,128]{1,0:T(8,128)S(1)}, u32[]{:S(2)}, u32[]{:S(2)}) %collective-permute-start.13) | collective-permute-done | bytes 81952 | tf_op jit(solution)/shard_map/ppermute | solution.py:538
  58.7 11.9 %basis.1 = (f32[11520,144]{1,0:T(8,128)}, f32[144,144]{1,0:T(8,128)S(1)}) custom-call(f32[160,128]{1,0:T(8,128)S(1)} %add.39.gram_ref, bf16[2,5,768,144]{3,2,1,0:T(8,128)(2,1)} %get-tuple-element.56.inner_hbm, bf16[5,96,144]{2,1,0:T(8,128)(2,1)} %get-tuple-element.57.rim_hbm, bf16[5,768,144]{2,1,0:T(8,128)(2,1)} %get-tuple-element.58.last_hbm), custom_call_target="tpu_custom_call" | custom-call | flops 1000 | bytes 1000 | tf_op jit(solution)/shard_map/basis/pallas_call | solution.py:501
  70.6 0.0 all-to-all-done.parts_ref
  70.6 1.0 %coefficients.1 = f32[8,144]{1,0:T(8,128)} custom-call(bf16[128,8,144]{2,1,0:T(8,128)(2,1)S(1)} %all-to-all-done.parts_ref, f32[144,144]{1,0:T(8,128)S(1)} %get-tuple-element.61.inv_ref), custom_call_target="tpu_custom_call" | custom-call | tf_op jit(solution)/shard_map/coefficients/pallas_call | solution.py:524
  (12 shorter events, 0.1 us)
Async XLA Ops:
  0.6 15.1 %copy-start = (s32[24]{0:T(128)S(1)}, s32[24]{0:T(128)}, u32[]{:S(2)}) copy-start(s32[24]{0:T(128)} %param.9) | copy-start | bytes 292
  8.6 11.2 %collective-permute-start = (bf16[5,112,128]{2,1,0:T(8,128)(2,1)S(1)}, bf16[5,112,128]{2,1,0:T(8,128)(2,1)S(1)}, u32[]{:S(2)}, u32[]{:S(2)}) collective-permute-start(bf16[5,112,128]{2,1,0:T(8,128)(2,1)S(1)} %get-tuple-element.33), channel_id=1, source_target_pairs={{0,16},{16,32},{32,48},{48,64},{64,80},{80,96},{96,112},{112,0},{1... | collective-permute-start | bytes 430088 | tf_op jit(solution)/shard_map/ppermute | solution.py:569
  11.3 8.6 %collective-permute-start.1 = (bf16[5,112,128]{2,1,0:T(8,128)(2,1)S(1)}, bf16[5,112,128]{2,1,0:T(8,128)(2,1)S(1)}, u32[]{:S(2)}, u32[]{:S(2)}) collective-permute-start(bf16[5,112,128]{2,1,0:T(8,128)(2,1)S(1)} %get-tuple-element.34), channel_id=1, source_target_pairs={{16,0},{32,16},{48,32},{64,48},{80,64},{96,80},{112,96},{0,112},{1... | collective-permute-start | bytes 430088 | tf_op jit(solution)/shard_map/ppermute | solution.py:570
  11.3 7.6 %collective-permute-start.2 = (bf16[5,80,128]{2,1,0:T(8,128)(2,1)S(1)}, bf16[5,80,128]{2,1,0:T(8,128)(2,1)S(1)}, u32[]{:S(2)}, u32[]{:S(2)}) collective-permute-start(bf16[5,80,128]{2,1,0:T(8,128)(2,1)S(1)} %get-tuple-element.35), channel_id=1, source_target_pairs={{0,1},{1,2},{2,3},{3,4},{4,5},{5,6},{6,7},{7,8},{8,9},{9,10},{10,1... | collective-permute-start | bytes 307208 | tf_op jit(solution)/shard_map/ppermute | solution.py:567
  14.5 5.4 %collective-permute-start.3 = (bf16[5,80,128]{2,1,0:T(8,128)(2,1)S(1)}, bf16[5,80,128]{2,1,0:T(8,128)(2,1)S(1)}, u32[]{:S(2)}, u32[]{:S(2)}) collective-permute-start(bf16[5,80,128]{2,1,0:T(8,128)(2,1)S(1)} %get-tuple-element.36), channel_id=1, source_target_pairs={{1,0},{2,1},{3,2},{4,3},{5,4},{6,5},{7,6},{8,7},{9,8},{10,9},{11,1... | collective-permute-start | bytes 307208 | tf_op jit(solution)/shard_map/ppermute | solution.py:568
  23.7 6.1 %collective-permute-start.6 = (f32[160,128]{1,0:T(8,128)S(1)}, f32[160,128]{1,0:T(8,128)S(1)}, u32[]{:S(2)}, u32[]{:S(2)}) collective-permute-start(f32[160,128]{1,0:T(8,128)S(1)} %get-tuple-element.43), channel_id=1, source_target_pairs={{0,64},{16,80},{32,96},{48,112},{64,0},{80,16},{96,32},{112,48},{1... | collective-permute-start | bytes 245768 | tf_op jit(solution)/shard_map/ppermute | solution.py:538
  26.3 3.6 %collective-permute-start.5 = (f32[160,128]{1,0:T(8,128)S(1)}, f32[160,128]{1,0:T(8,128)S(1)}, u32[]{:S(2)}, u32[]{:S(2)}) collective-permute-start(f32[160,128]{1,0:T(8,128)S(1)} %get-tuple-element.43), channel_id=1, source_target_pairs={{0,96},{16,112},{32,0},{48,16},{64,32},{80,48},{96,64},{112,80},{1... | collective-permute-start | bytes 245768 | tf_op jit(solution)/shard_map/ppermute | solution.py:538
  27.4 5.4 %collective-permute-start.4 = (f32[160,128]{1,0:T(8,128)S(1)}, f32[160,128]{1,0:T(8,128)S(1)}, u32[]{:S(2)}, u32[]{:S(2)}) collective-permute-start(f32[160,128]{1,0:T(8,128)S(1)} %get-tuple-element.43), channel_id=1, source_target_pairs={{0,32},{16,48},{32,64},{48,80},{64,96},{80,112},{96,0},{112,16},{1... | collective-permute-start | bytes 245768 | tf_op jit(solution)/shard_map/ppermute | solution.py:538
  32.8 7.8 %collective-permute-start.9 = (f32[160,128]{1,0:T(8,128)S(1)}, f32[160,128]{1,0:T(8,128)S(1)}, u32[]{:S(2)}, u32[]{:S(2)}) collective-permute-start(f32[160,128]{1,0:T(8,128)S(1)} %add_add_fusion.2), channel_id=1, source_target_pairs={{0,2},{1,3},{2,0},{3,1},{4,6},{5,7},{6,4},{7,5},{8,10},{9,11},{10,... | collective-permute-start | bytes 245768 | tf_op jit(solution)/shard_map/ppermute | solution.py:538
  35.6 5.7 %collective-permute-start.8 = (f32[160,128]{1,0:T(8,128)S(1)}, f32[160,128]{1,0:T(8,128)S(1)}, u32[]{:S(2)}, u32[]{:S(2)}) collective-permute-start(f32[160,128]{1,0:T(8,128)S(1)} %add_add_fusion.2), channel_id=1, source_target_pairs={{0,3},{1,0},{2,1},{3,2},{4,7},{5,4},{6,5},{7,6},{8,11},{9,8},{10,9... | collective-permute-start | bytes 245768 | tf_op jit(solution)/shard_map/ppermute | solution.py:538
  37.8 4.5 %collective-permute-start.7 = (f32[160,128]{1,0:T(8,128)S(1)}, f32[160,128]{1,0:T(8,128)S(1)}, u32[]{:S(2)}, u32[]{:S(2)}) collective-permute-start(f32[160,128]{1,0:T(8,128)S(1)} %add_add_fusion.2), channel_id=1, source_target_pairs={{0,1},{1,2},{2,3},{3,0},{4,5},{5,6},{6,7},{7,4},{8,9},{9,10},{10,1... | collective-permute-start | bytes 245768 | tf_op jit(solution)/shard_map/ppermute | solution.py:538
  42.3 14.2 %collective-permute-start.12 = (f32[160,128]{1,0:T(8,128)S(1)}, f32[160,128]{1,0:T(8,128)S(1)}, u32[]{:S(2)}, u32[]{:S(2)}) collective-permute-start(f32[160,128]{1,0:T(8,128)S(1)} %add_add_fusion.1), channel_id=1, source_target_pairs={{0,8},{1,9},{2,10},{3,11},{4,12},{5,13},{6,14},{7,15},{8,0},{9,1},... | collective-permute-start | bytes 245768 | tf_op jit(solution)/shard_map/ppermute | solution.py:538
  46.6 9.9 %collective-permute-start.11 = (f32[160,128]{1,0:T(8,128)S(1)}, f32[160,128]{1,0:T(8,128)S(1)}, u32[]{:S(2)}, u32[]{:S(2)}) collective-permute-start(f32[160,128]{1,0:T(8,128)S(1)} %add_add_fusion.1), channel_id=1, source_target_pairs={{0,12},{1,13},{2,14},{3,15},{4,0},{5,1},{6,2},{7,3},{8,4},{9,5},{1... | collective-permute-start | bytes 245768 | tf_op jit(solution)/shard_map/ppermute | solution.py:538
  47.2 9.3 %collective-permute-start.10 = (f32[160,128]{1,0:T(8,128)S(1)}, f32[160,128]{1,0:T(8,128)S(1)}, u32[]{:S(2)}, u32[]{:S(2)}) collective-permute-start(f32[160,128]{1,0:T(8,128)S(1)} %add_add_fusion.1), channel_id=1, source_target_pairs={{0,4},{1,5},{2,6},{3,7},{4,8},{5,9},{6,10},{7,11},{8,12},{9,13},{1... | collective-permute-start | bytes 245768 | tf_op jit(solution)/shard_map/ppermute | solution.py:538
  48.1 22.5 %all-to-all-start = ((bf16[128,8,144]{2,1,0:T(8,128)(2,1)}), bf16[128,8,144]{2,1,0:T(8,128)(2,1)S(1)}, u32[]{:S(2)}, u32[]{:S(2)}) async-start(bf16[128,8,144]{2,1,0:T(8,128)(2,1)} %bitcast.3), calls=%async_computation | async-start | bytes 1048576 | tf_op jit(solution)/shard_map/all_to_all | solution.py:578
  56.6 2.1 %collective-permute-start.13 = (f32[160,128]{1,0:T(8,128)S(1)}, f32[160,128]{1,0:T(8,128)S(1)}, u32[]{:S(2)}, u32[]{:S(2)}) collective-permute-start(f32[160,128]{1,0:T(8,128)S(1)} %add_add_fusion), channel_id=1, source_target_pairs={{0,16},{16,0},{32,48},{48,32},{64,80},{80,64},{96,112},{112,96},{1... | collective-permute-start | bytes 245768 | tf_op jit(solution)/shard_map/ppermute | solution.py:538
